TPU v7x, 32 devices: a whole 2x2x4 slice. The times are simulated.
32 devices in a mesh: layer: 2 (over y), feat: 16 (over z, x, core).
Axes of the slice: x: 2, y: 2, z: 4, core: 2. Of those that a mesh axis runs over, the one named last changes fastest.
Arguments:
- residual: bfloat16 [2, 256, 4096], P('layer', 'feat'), may hold values from -6 to 6
- targets: bfloat16 [2, 256, 4096], P('layer', 'feat'), may hold values from -6 to 6
- w_enc: bfloat16 [2, 4096, 8192], P('layer', None, 'feat'), may hold values from -0.09375 to 0.09375
- b_enc: float32 [2, 8192], P('layer', 'feat'), may hold values from -3 to 3
- w_dec: bfloat16 [2, 8192, 4096], P('layer', 'feat'), may hold values from -0.0625 to 0.0625
- block_mask: int32 [2, 2, 64], P('layer', None, 'feat'), may hold values from 0 to 1, as said below
Outputs:
- grad_encoder: bfloat16 [2, 4096, 8192], P('layer', None, 'feat')
- grad_bias: float32 [2, 8192], P('layer', 'feat')
- grad_decoder: bfloat16 [2, 8192, 4096], P('layer', 'feat')
- loss: float32 [], replicated
Inputs may be any that keep to these rules, and one draw needn't show every extreme that they name: `block_mask`: each feature block of a layer has its own activity level, so the number of active blocks differs from device to device; some feature blocks are never active and some always.
All inputs are finite; a program needn't handle non-finite values.
Results may differ from a plain program's by a relative error of at most 0.0056.
Values may be sent and summed in bfloat16 or wider, within the bound.
No kernel may reach another device: no remote copies, remote signals or barrier semaphores. Data moves between devices by JAX's collectives and lax.ppermute only.
A program may use at most 64 MiB of HBM per device.

v0:
```python
import jax
import jax.numpy as jnp
from jax import lax
from jax.sharding import PartitionSpec as P

TBLOCK = 128
FBLOCK = 128


penalty_weight = 0.5
norm_epsilon = 1e-06


def shifted(block, axis, distance):
    devices = range(lax.axis_size(axis))
    route = [((i - distance) % len(devices), i) for i in devices]
    return lax.ppermute(block, axis, route)


def contract_rows(left, right):
    return lax.dot_general(
        left, right, (((0,), (0,)), ((), ())), preferred_element_type=jnp.float32
    )


def body(residual, targets, w_enc, b_enc, w_dec, block_mask):
    own_rows = residual[0]
    encoder = w_enc[0]
    enc_bias = b_enc[0]
    decoder = w_dec[0]
    blocks = block_mask[0]
    row_count = own_rows.shape[0]
    width = own_rows.shape[1]
    layers = lax.axis_size("layer")
    tokens = row_count * lax.axis_size("feat")
    keep_mask = jnp.repeat(jnp.repeat(blocks, TBLOCK, axis=0), FBLOCK, axis=1).astype(jnp.float32)
    gathered = lax.all_gather(own_rows, "feat", axis=0, tiled=True)
    preact = jnp.dot(gathered, encoder, preferred_element_type=jnp.float32) + enc_bias
    positive = jnp.maximum(preact, 0.0)
    activation = (keep_mask * positive * positive).astype(jnp.bfloat16)
    act_float = activation.astype(jnp.float32)
    row_norms = jnp.sqrt(jnp.sum(jnp.square(decoder.astype(jnp.float32)), axis=1) + norm_epsilon)
    penalty_local = jnp.sum(act_float * row_norms[None, :])
    act_rows = activation
    recon_rows = lax.psum_scatter(
        jnp.dot(act_rows, decoder, preferred_element_type=jnp.float32),
        "feat",
        scatter_dimension=0,
        tiled=True,
    )
    owned = shifted(recon_rows, "layer", 1)
    misfit = owned - targets[0].astype(jnp.float32)
    error_back = shifted(misfit.astype(jnp.bfloat16), "layer", -1)
    square_local = jnp.sum(misfit * misfit)
    shard_rows = lax.all_gather(error_back, "feat", axis=0, tiled=True)
    act_rows = activation
    dec_total = contract_rows(act_rows, shard_rows)
    grad_rows = lax.dot_general(
        shard_rows, decoder, (((1,), (1,)), ((), ())), preferred_element_type=jnp.float32
    )
    dec_grad = dec_total
    act_grad = grad_rows
    act_sum = jnp.sum(act_float, axis=0)
    dec_grad = (
        dec_grad
        + penalty_weight * act_sum[:, None] * decoder.astype(jnp.float32) / row_norms[:, None]
    )
    act_grad = act_grad + penalty_weight * row_norms[None, :]
    pre_grad = (act_grad * keep_mask * 2.0 * positive).astype(jnp.bfloat16)
    bias_grad = jnp.sum(pre_grad.astype(jnp.float32), axis=0)
    enc_grad = contract_rows(gathered, pre_grad)
    square_sum, penalty_sum = lax.psum((square_local, penalty_local), ("layer", "feat"))
    loss = (0.5 * square_sum + penalty_weight * penalty_sum) / (layers * tokens * width)
    return (
        enc_grad.astype(jnp.bfloat16)[None],
        bias_grad[None],
        dec_grad.astype(jnp.bfloat16)[None],
        loss,
    )


def solution(mesh):
    return jax.shard_map(
        body,
        mesh=mesh,
        in_specs=(
            P("layer", "feat", None),
            P("layer", "feat", None),
            P("layer", None, "feat"),
            P("layer", "feat"),
            P("layer", "feat", None),
            P("layer", None, "feat"),
        ),
        out_specs=(P("layer", None, "feat"), P("layer", "feat"), P("layer", "feat", None), P()),
        check_vma=False,
    )
```

profile of v0, /device:TPU:0, one launch (start us, length us, event | category | flops | bytes accessed | tf_op | source)
XLA Modules:
  0.0 216.7 jit_solution(39205197943870104)
XLA Ops:
  7.2 0.0 all-gather.6.cloned.1.call-start
  7.2 0.7 all-gather.6.cloned.1.call-update
  7.9 0.0 reduce-scatter.2.cloned.1.call-start
  8.0 0.7 convert_bitcast_fusion
  8.6 3.1 %fusion = f32[512]{0:T(512)S(1)} fusion(bf16[1,512,4096]{2,1,0:T(8,128)(2,1)} %param.10), kind=kLoop, calls=%fused_computation.2 | loop fusion | flops 6290944 | bytes 4196352 | tf_op jit(solution)/shard_map/reduce_sum | solution.py:42
  11.7 42.6 %all-gather.6.cloned.1.call-done = bf16[1,256,4096]{2,1,0:T(8,128)(2,1)} async-done(((bf16[1,16,4096]{2,1,0:T(8,128)(2,1)}), bf16[1,256,4096]{2,1,0:T(8,128)(2,1)}) %all-gather.6.cloned.1.call-update) | async-done | bytes 2097168 | tf_op jit(solution)/shard_map/all_gather | solution.py:37
  54.3 0.3 broadcast_in_dim.20
  54.7 4.9 %fusion.39 = (f32[]{:T(128)}, f32[512]{0:T(512)S(1)}, bf16[256,512]{1,0:T(8,128)(2,1)S(1)}, f32[256,512]{1,0:T(8,128)S(1)}) fusion(f32[512]{0:T(512)S(1)} %get-tuple-element.14, f32[32,8,4,128]{3,2,1,0:T(4,128)S(1)} %bitcast.64, f32[512]{0:T(512)S(1)} %bitcast.67, bf16[1,4096,512]{2,1,0:T(8,128)(2,1)} %param.8, ...), kind=kOutput, calls=%fused_computation.27 | convolution fusion | flops 1074920960 | bytes 7608324 | tf_op jit(solution)/shard_map/dot_general | solution.py:38
  59.6 3.3 %fusion.8 = f32[256,4096]{1,0:T(8,128)} fusion(bf16[256,512]{1,0:T(8,128)(2,1)S(1)} %get-tuple-element.10, bf16[1,512,4096]{2,1,0:T(8,128)(2,1)S(1)} %copy-done), kind=kOutput, calls=%fused_computation.11 | convolution fusion | flops 1073741824 | bytes 8650752 | tf_op jit(solution)/shard_map/dot_general | solution.py:46
  62.9 0.0 reduce-scatter.2.cloned.1.call-update
  62.9 0.0 all-gather.4.cloned.1.call-start
  63.0 71.2 %reduce-scatter.2.cloned.1.call-done = f32[16,4096]{1,0:T(8,128)} async-done(((f32[256,4096]{1,0:T(8,128)}), f32[16,4096]{1,0:T(8,128)}) %reduce-scatter.2.cloned.1.call-update) | async-done | bytes 262160 | tf_op jit(solution)/shard_map/reduce_scatter | solution.py:45
  134.2 1.5 collective-permute-start
  135.7 5.1 %collective-permute-done = f32[16,4096]{1,0:T(8,128)S(1)} collective-permute-done((f32[16,4096]{1,0:T(8,128)}, f32[16,4096]{1,0:T(8,128)S(1)}, u32[]{:S(2)}, u32[]{:S(2)}) %collective-permute-start) | collective-permute-done | bytes 262176 | tf_op jit(solution)/shard_map/ppermute | solution.py:17
  140.8 0.7 multiply_reduce_fusion
  141.5 1.5 collective-permute-start.1
  142.9 3.5 %collective-permute-done.1 = bf16[16,4096]{1,0:T(8,128)(2,1)S(1)} collective-permute-done((bf16[16,4096]{1,0:T(8,128)(2,1)S(1)}, bf16[16,4096]{1,0:T(8,128)(2,1)S(1)}, u32[]{:S(2)}, u32[]{:S(2)}) %collective-permute-start.1) | collective-permute-done | bytes 131104 | tf_op jit(solution)/shard_map/ppermute | solution.py:17
  146.4 0.7 copy-done.3
  148.4 40.2 %psum.16 = f32[]{:T(128)} all-reduce(f32[]{:T(128)S(6)} %mul.75), channel_id=1, replica_groups=mesh['layer'=2,'feat'=16] {'layer','feat'}, use_global_device_ids=true, to_apply=%region_5.0 | all-reduce | flops 1 | bytes 8 | tf_op jit(solution)/shard_map/psum | solution.py:72
  189.2 0.0 all-gather.4.cloned.1.call-done
  189.3 4.7 %convert_reduce_fusion.1 = (f32[512]{0:T(512)}, bf16[256,512]{1,0:T(8,128)(2,1)S(1)}) fusion(f32[256,512]{1,0:T(8,128)S(1)} %get-tuple-element.15, f32[32,8,4,128]{3,2,1,0:T(4,128)S(1)} %bitcast.65, f32[512]{0:T(512)S(1)} %get-tuple-element.13, bf16[256,4096]{1,0:T(8,128)(2,1)} %all-gather.4.cloned.1.call-done, bf16[1,512,4096]{2,1,0:T(8,128)(2,1)} %param.10), kind=kOutput, calls=%fused_computation.29 | convolution fusion | flops 1074658816 | bytes 7606272 | tf_op jit(solution)/shard_map/dot_general | solution.py:58
  194.0 3.3 %fusion.4 = bf16[1,4096,512]{1,2,0:T(8,128)(2,1)} fusion(bf16[256,512]{1,0:T(8,128)(2,1)S(1)} %get-tuple-element.17, bf16[1,256,4096]{2,1,0:T(8,128)(2,1)S(1)} %copy-done.1), kind=kOutput, calls=%fused_computation.7 | convolution fusion | flops 1075838976 | bytes 6553600 | tf_op jit(solution)/shard_map/dot_general | solution.py:21
  197.3 6.5 %copy.10 = bf16[1,4096,512]{2,1,0:T(8,128)(2,1)} copy(bf16[1,4096,512]{1,2,0:T(8,128)(2,1)} %fusion.4) | data formatting | bytes 8388608
  203.9 5.2 %fusion.5 = bf16[1,512,4096]{2,1,0:T(8,128)(2,1)} fusion(bf16[256,512]{1,0:T(8,128)(2,1)S(1)} %get-tuple-element.10, bf16[256,4096]{1,0:T(8,128)(2,1)S(1)} %copy-done.4, bf16[1,512,4096]{2,1,0:T(8,128)(2,1)} %param.10, f32[512]{0:T(512)S(1)} %get-tuple-element.14, f32[512]{0:T(512)S(1)} %broadcast_multiply_fusion), kind=kOutput, calls=%fused_computation.8 | convolution fusion | flops 1084227584 | bytes 10752000 | tf_op jit(solution)/shard_map/dot_general | solution.py:21
  (15 shorter events, 0.1 us)
Async XLA Ops:
  7.2 47.5 %copy-start.5 = (f32[1,512]{1,0:T(1,128)S(1)}, f32[1,512]{1,0:T(1,128)}, u32[]{:S(2)}) copy-start(f32[1,512]{1,0:T(1,128)} %param.9) | copy-start | bytes 6148
  7.2 47.1 %all-gather.6.cloned.1.call-start = ((), (), s32[]{:S(2)}) async-start(), calls=%async_computation.3 | async-start | bytes 2228224 | tf_op jit(solution)/shard_map/all_gather | solution.py:37
  7.9 126.3 %reduce-scatter.2.cloned.1.call-start = ((), (), s32[]{:S(2)}) async-start(), calls=%async_computation.1 | async-start | bytes 4456448 | tf_op jit(solution)/shard_map/reduce_scatter | solution.py:45
  54.6 5.0 %copy-start = (bf16[1,512,4096]{2,1,0:T(8,128)(2,1)S(1)}, bf16[1,512,4096]{2,1,0:T(8,128)(2,1)}, u32[]{:S(2)}) copy-start(bf16[1,512,4096]{2,1,0:T(8,128)(2,1)} %param.10) | copy-start | bytes 12582916
  62.9 77.9 %copy-start.2 = (bf16[1,16,4096]{2,1,0:T(8,128)(2,1)S(1)}, bf16[1,16,4096]{2,1,0:T(8,128)(2,1)}, u32[]{:S(2)}) copy-start(bf16[1,16,4096]{2,1,0:T(8,128)(2,1)} %param.7) | copy-start | bytes 393220
  62.9 126.3 %all-gather.4.cloned.1.call-start = ((), (), s32[]{:S(2)}) async-start(), calls=%async_computation.2 | async-start | bytes 2228224 | tf_op jit(solution)/shard_map/all_gather | solution.py:55
  134.2 6.6 %collective-permute-start = (f32[16,4096]{1,0:T(8,128)}, f32[16,4096]{1,0:T(8,128)S(1)}, u32[]{:S(2)}, u32[]{:S(2)}) collective-permute-start(f32[16,4096]{1,0:T(8,128)} %reduce-scatter.2.cloned.1.call-done), channel_id=1, source_target_pairs={{16,0},{0,16},{17,1},{1,17},{18,2},{2,18},{19,3},{3,19},{20,4},{4,... | collective-permute-start | bytes 786440 | tf_op jit(solution)/shard_map/ppermute | solution.py:17
  141.5 52.5 %copy-start.1 = (bf16[1,256,4096]{2,1,0:T(8,128)(2,1)S(1)}, bf16[1,256,4096]{2,1,0:T(8,128)(2,1)}, u32[]{:S(2)}) copy-start(bf16[1,256,4096]{2,1,0:T(8,128)(2,1)} %all-gather.6.cloned.1.call-done) | copy-start | bytes 6291460
  141.5 5.0 %collective-permute-start.1 = (bf16[16,4096]{1,0:T(8,128)(2,1)S(1)}, bf16[16,4096]{1,0:T(8,128)(2,1)S(1)}, u32[]{:S(2)}, u32[]{:S(2)}) collective-permute-start(bf16[16,4096]{1,0:T(8,128)(2,1)S(1)} %get-tuple-element.12), channel_id=1, source_target_pairs={{16,0},{0,16},{17,1},{1,17},{18,2},{2,18},{19,3},{3,19},{20,4},{4,... | collective-permute-start | bytes 393224 | tf_op jit(solution)/shard_map/ppermute | solution.py:17
  146.4 0.7 copy-start.3
  197.3 6.6 %copy-start.4 = (bf16[256,4096]{1,0:T(8,128)(2,1)S(1)}, bf16[256,4096]{1,0:T(8,128)(2,1)}, u32[]{:S(2)}) copy-start(bf16[256,4096]{1,0:T(8,128)(2,1)} %all-gather.4.cloned.1.call-done) | copy-start | bytes 6291460
Sparse Core Ops, SparseCore 0:
  10.2 44.0 all-gather.5
  63.0 71.1 reduce-scatter.1
  147.2 40.8 all-gather.3
where the time goes:
time: 217 us
  waiting for transfers between devices  123 us (57%)
  blocking collectives  40.2 us (19%)
  matrix products  21.4 us (10%)
  between operations  16.9 us (8%)
  local copies, waits for them, and re-layouts  7.57 us (3%)
  other arithmetic  4.44 us (2%)
  starting transfers between devices  3.07 us (1%)
    reduce_scatter x1, waiting for transfers between devices, body(): lax.psum_scatter(jnp.dot(act_rows, decoder, preferred_element_type=jnp.fl...  71.2 us
    all_gather x1, waiting for transfers between devices, body(): gathered = lax.all_gather(own_rows, 'feat', axis=0, tiled=True)  42.6 us
    psum x1, blocking collectives, body(): lax.psum((square_local, penalty_local), ('layer', 'feat'))  40.2 us
    ppermute x2, waiting for transfers between devices, shifted(): return lax.ppermute(block, axis, route)  8.6 us
    dot_general x2, matrix products, contract_rows(): lax.dot_general(left, right, (((0,), (0,)), ((), ())), preferred_element_...  8.47 us
    unnamed x13, local copies, waits for them, and re-layouts  7.23 us
    dot_general x1, matrix products, body(): jnp.dot(gathered, encoder, preferred_element_type=jnp.float32) + enc_bias  4.94 us
    dot_general x1, matrix products, body(): lax.dot_general(shard_rows, decoder, (((1,), (1,)), ((), ())), preferred_...  4.73 us
  transfers between devices with their start and end apart: 5, of which 4 were waited for; matrix products, arithmetic and copies ran while one was open for 2% of the time, Pallas kernels for 0%

commit v1 on v0

v1 whole, which is shorter than its diff:
```python
import jax
import jax.numpy as jnp
import numpy as np
from jax import lax
from jax.sharding import PartitionSpec as P

TBLOCK = 128
FBLOCK = 128
PAD = 128

penalty_weight = 0.5
norm_epsilon = 1e-06
f32 = jnp.float32
bf16 = jnp.bfloat16


class Ring:
    def __init__(self, size):
        self.size = size
        chips = size // 2
        self.chips = chips
        self.hops = (chips - 1) // 2
        self.far = chips % 2 == 0
        order = list(range(0, chips, 2)) + list(range(1, chips, 2))[::-1]
        place = {chip: at for at, chip in enumerate(order)}
        self.step, self.far_step = [], []
        owners = []
        for device in range(size):
            chip, core = divmod(device, 2)
            at = place[chip]
            ahead = 1 if core == 0 else -1
            pair = (device, order[(at + ahead) % chips] * 2 + core)
            self.step.append(pair)
            if core == 1:
                self.far_step.append(pair)
            behind = [order[(at - ahead * k) % chips] for k in range(1, self.hops + 1)]
            front = [order[(at + ahead * k) % chips] for k in range(1, self.hops + 1)]
            last = [order[(at + self.hops + 1) % chips]] if self.far else []
            owners.append([2 * c + i for c in [chip] + behind + front + last for i in (0, 1)])
        self.owners = np.array(owners, np.int32)
        self.twin = [(device, device ^ 1) for device in range(size)]

    def along(self, block):
        return lax.ppermute(block, "feat", self.step)

    def along_far(self, block):
        return lax.ppermute(block, "feat", self.far_step)

    def across(self, block):
        return lax.ppermute(block, "feat", self.twin)


def chip_block(ring, core, own):
    other = ring.across(own)
    return jnp.concatenate(
        [jnp.where(core == 0, own, other), jnp.where(core == 0, other, own)], axis=0
    )


def gather(ring, core, block):
    behind = []
    moving = block
    for _ in range(ring.hops):
        moving = ring.along(moving)
        behind.append(moving)
    parts = [block] + behind
    if behind:
        parts.append(ring.across(jnp.concatenate(behind, axis=0)))
    if ring.far:
        came = ring.along_far(moving)
        parts.append(jnp.where(core == 1, came, ring.across(came)))
    return jnp.concatenate(parts, axis=0)


def scatter_sum(ring, rows, partial):
    sent = partial.astype(bf16)
    at = rows * (1 + ring.hops)
    end = rows * (1 + 2 * ring.hops)
    arrived = None
    if ring.far:
        total = partial[end:] + ring.across(sent[end:]).astype(f32)
        arrived = ring.along_far(total.astype(bf16))
    if ring.hops:
        from_twin = ring.across(sent[rows:at])
    for k in range(ring.hops, 0, -1):
        total = partial[at + rows * (k - 1) : at + rows * k]
        total = total + from_twin[rows * (k - 1) : rows * k].astype(f32)
        if arrived is not None:
            total = total + arrived.astype(f32)
        arrived = ring.along(total.astype(bf16))
    total = partial[:rows]
    if arrived is not None:
        total = total + arrived.astype(f32)
    mine = total.astype(bf16)
    return mine.astype(f32) + ring.across(mine).astype(f32)


def contract_rows(left, right):
    return lax.dot_general(
        left, right, (((0,), (0,)), ((), ())), preferred_element_type=f32
    )


def split_three(value):
    high = value.astype(bf16)
    rest = value - high.astype(f32)
    middle = rest.astype(bf16)
    low = (rest - middle.astype(f32)).astype(bf16)
    return [high, middle, low]


def body(residual, targets, w_enc, b_enc, w_dec, block_mask):
    encoder = w_enc[0]
    enc_bias = b_enc[0]
    decoder = w_dec[0]
    blocks = block_mask[0].astype(f32)
    row_count = residual.shape[1]
    width = residual.shape[2]
    layers = lax.axis_size("layer")
    feats = lax.axis_size("feat")
    tokens = row_count * feats
    ring = Ring(feats)
    device = lax.axis_index("feat")
    core = device % 2
    halves = 2 if row_count % 2 == 0 else 1
    rows = row_count // halves
    block_rows = 2 * rows

    goal = lax.ppermute(
        targets[0], "layer", [(i, (i - 1) % layers) for i in range(layers)]
    )
    owner = jnp.asarray(ring.owners)[device]
    mask_columns = jnp.repeat(blocks, FBLOCK, axis=1)

    row_norms = jnp.sqrt(jnp.sum(jnp.square(decoder.astype(f32)), axis=1) + norm_epsilon)

    own_block = chip_block(ring, core, residual[0])
    goal_block = chip_block(ring, core, goal)

    def half_of(block, h):
        return jnp.concatenate(
            [block[c * row_count + h * rows : c * row_count + (h + 1) * rows] for c in (0, 1)], axis=0
        )

    gathered = [gather(ring, core, half_of(own_block, h)) for h in range(halves)]
    keep, positive, activation, penalty = [], [], [], jnp.zeros((), f32)
    for h in range(halves):
        token = (owner[:, None] * row_count + h * rows + jnp.arange(rows)[None, :]).reshape(-1)
        token_block = token // TBLOCK
        mask = jnp.zeros((token.shape[0], mask_columns.shape[1]), f32)
        for b in range(blocks.shape[0]):
            mask = jnp.where((token_block == b)[:, None], mask_columns[b][None, :], mask)
        preact = jnp.dot(gathered[h], encoder, preferred_element_type=f32) + enc_bias
        positive.append(jnp.maximum(preact, 0.0))
        keep.append(mask)
        activation.append((mask * positive[h] * positive[h]).astype(bf16))
        penalty = penalty + jnp.sum(activation[h].astype(f32) * row_norms[None, :])
    penalty_chip = penalty + ring.across(penalty)
    errors, losses = [], []
    for h in range(halves):
        partial = jnp.dot(activation[h], decoder, preferred_element_type=f32)
        recon = scatter_sum(ring, block_rows, partial)
        misfit = recon - half_of(goal_block, h).astype(f32)
        loss_part = 0.5 * jnp.sum(misfit * misfit)
        if h == halves - 1:
            loss_part = loss_part + penalty_weight * penalty_chip
        three = jnp.stack(split_three(loss_part))
        tail = jnp.broadcast_to(jnp.pad(three, (0, PAD - 3))[None, :], (block_rows, PAD))
        payload = jnp.concatenate([misfit.astype(bf16), tail], axis=1)
        every = gather(ring, core, payload)
        errors.append(every[:, :width])
        losses.append(jnp.sum(every[::block_rows, width : width + 3].astype(f32)))
    loss_sum = sum(losses)
    whole = loss_sum
    for _ in range(layers - 1):
        loss_sum = lax.ppermute(
            loss_sum, "layer", [(i, (i + 1) % layers) for i in range(layers)]
        )
        whole = whole + loss_sum
    loss = whole / (layers * tokens * width)

    all_errors = jnp.concatenate(errors, axis=0)
    all_act = jnp.concatenate(activation, axis=0)
    all_rows = jnp.concatenate(gathered, axis=0)
    act_sum = jnp.sum(all_act.astype(f32), axis=0)
    dec_grad = (
        contract_rows(all_act, all_errors)
        + penalty_weight * act_sum[:, None] * decoder.astype(f32) / row_norms[:, None]
    )
    pre_grads = []
    for h in range(halves):
        act_grad = lax.dot_general(
            errors[h], decoder, (((1,), (1,)), ((), ())), preferred_element_type=f32
        )
        act_grad = act_grad + penalty_weight * row_norms[None, :]
        pre_grads.append((act_grad * keep[h] * 2.0 * positive[h]).astype(bf16))
    pre_grad = jnp.concatenate(pre_grads, axis=0)
    bias_grad = jnp.sum(pre_grad.astype(f32), axis=0)
    enc_grad = contract_rows(all_rows, pre_grad)
    return (
        enc_grad.astype(bf16)[None],
        bias_grad[None],
        dec_grad.astype(bf16)[None],
        loss,
    )


def solution(mesh):
    return jax.shard_map(
        body,
        mesh=mesh,
        in_specs=(
            P("layer", "feat", None),
            P("layer", "feat", None),
            P("layer", None, "feat"),
            P("layer", "feat"),
            P("layer", "feat", None),
            P("layer", None, "feat"),
        ),
        out_specs=(P("layer", None, "feat"), P("layer", "feat"), P("layer", "feat", None), P()),
        check_vma=False,
    )
```

time: 217 us -> 137 us (0.63)
  waiting for transfers between devices: 123 us -> 25.8 us
  starting transfers between devices: 3.07 us -> 50.1 us
  blocking collectives: 40.2 us -> 0 us
  other arithmetic: 4.44 us -> 18.6 us
  between operations: 16.9 us -> 7.49 us
  local copies, waits for them, and re-layouts: 7.57 us -> 14.7 us
    reduce_scatter x1 -> x0, waiting for transfers between devices: 71.2 us -> none  [body(): lax.psum_scatter(jnp.dot(act_rows, decoder, preferred_element_type=jnp.fl...]
    ppermute x2 -> x43, starting transfers between devices: 2.95 us -> 50.1 us  [the longest x18 20.6 us: along(): return lax.ppermute(block, 'feat', self.step)]
    all_gather x2 -> x0, waiting for transfers between devices: 42.6 us -> none  [the longest x1 42.6 us: body(): gathered = lax.all_gather(own_rows, 'feat', axis=0, tiled=True)]
    psum x1 -> x0, blocking collectives: 40.2 us -> none  [body(): lax.psum((square_local, penalty_local), ('layer', 'feat'))]
    ppermute x2 -> x43, waiting for transfers between devices: 8.6 us -> 25.8 us  [the longest x18 24.3 us: along(): return lax.ppermute(block, 'feat', self.step)]
    convert_element_type x1 -> x13, other arithmetic: 0.68 us -> 8.96 us  [the longest x6 3.13 us: scatter_sum(): arrived = ring.along(total.astype(bf16))]
    slice x0 -> x11, local copies, waits for them, and re-layouts: none -> 5.87 us  [the longest x2 2.23 us: body(): errors.append(every[:, :width])]
    dot_general x3 -> x6, matrix products: 12.9 us -> 11.2 us  [the longest x2 5.42 us: body(): lax.dot_general(errors[h], decoder, (((1,), (1,)), ((), ())), preferred_e...]
  transfers between devices with their start and end apart: 5 -> 43, of which waited for: 4 -> 16; matrix products, arithmetic and copies ran while one was open for 2% -> 25% of each run, Pallas kernels for 0% -> 0%
where the time goes in v1:
time: 137 us; the launch traced here: 136 us
  starting transfers between devices  50.1 us (37%)
  waiting for transfers between devices  25.8 us (19%)
  matrix products  19.4 us (14%)
  other arithmetic  18.6 us (14%)
  local copies, waits for them, and re-layouts  14.7 us (11%)
  between operations  7.49 us (5%)
    ppermute x18, waiting for transfers between devices, along(): return lax.ppermute(block, 'feat', self.step)  24.3 us
    ppermute x18, starting transfers between devices, along(): return lax.ppermute(block, 'feat', self.step)  20.6 us
    ppermute x17, starting transfers between devices, across(): return lax.ppermute(block, 'feat', self.twin)  20.4 us
    unnamed x60, local copies, waits for them, and re-layouts  8.58 us
    dot_general x2, matrix products, contract_rows(): lax.dot_general(left, right, (((0,), (0,)), ((), ())), preferred_element_...  8.24 us
    dot_general x2, matrix products, body(): lax.dot_general(errors[h], decoder, (((1,), (1,)), ((), ())), preferred_e...  5.42 us
    ppermute x6, starting transfers between devices, along_far(): return lax.ppermute(block, 'feat', self.far_step)  4.18 us
    convert_element_type x6, other arithmetic, scatter_sum(): arrived = ring.along(total.astype(bf16))  3.13 us
  transfers between devices with their start and end apart: 43, of which 16 were waited for; matrix products, arithmetic and copies ran while one was open for 25% of the time, Pallas kernels for 0%

profile of v1, /device:TPU:0, one launch (start us, length us, event | category | flops | bytes accessed | tf_op | source)
XLA Modules:
  0.0 136.2 jit_solution(6120475901856623419)
XLA Ops:
  0.6 3.0 %collective-permute-start.20 = (bf16[16,4096]{1,0:T(8,128)(2,1)}, bf16[16,4096]{1,0:T(8,128)(2,1)S(1)}, u32[]{:S(2)}, u32[]{:S(2)}) collective-permute-start(bf16[16,4096]{1,0:T(8,128)(2,1)} %bitcast.87), channel_id=1, source_target_pairs={{0,16},{16,0},{1,17},{17,1},{2,18},{18,2},{3,19},{19,3},{4,20},{20... | collective-permute-start | bytes 393224 | tf_op jit(solution)/shard_map/ppermute | solution.py:129
  5.7 3.1 %fusion = f32[512]{0:T(512)S(1)} fusion(bf16[1,512,4096]{2,1,0:T(8,128)(2,1)} %param.11), kind=kLoop, calls=%fused_computation.2 | loop fusion | flops 6290944 | bytes 4196352 | tf_op jit(solution)/shard_map/reduce_sum | solution.py:135
  12.9 1.6 %collective-permute-start.1 = (bf16[16,4096]{1,0:T(8,128)(2,1)S(1)}, bf16[16,4096]{1,0:T(8,128)(2,1)S(1)}, u32[]{:S(2)}, u32[]{:S(2)}) collective-permute-start(bf16[16,4096]{1,0:T(8,128)(2,1)S(1)} %pad_maximum_fusion.10), channel_id=1, source_target_pairs={{0,4},{1,3},{2,0},{3,7},{4,8},{5,1},{6,2},{7,11},{8,12},{9,5},{10,... | collective-permute-start | bytes 393224 | tf_op jit(solution)/shard_map/ppermute | solution.py:44
  14.5 1.6 %collective-permute-start.7 = (bf16[16,4096]{1,0:T(8,128)(2,1)S(1)}, bf16[16,4096]{1,0:T(8,128)(2,1)S(1)}, u32[]{:S(2)}, u32[]{:S(2)}) collective-permute-start(bf16[16,4096]{1,0:T(8,128)(2,1)S(1)} %pad_maximum_fusion.11), channel_id=1, source_target_pairs={{0,4},{1,3},{2,0},{3,7},{4,8},{5,1},{6,2},{7,11},{8,12},{9,5},{10,... | collective-permute-start | bytes 393224 | tf_op jit(solution)/shard_map/ppermute | solution.py:44
  26.7 2.7 %collective-permute-done.9 = bf16[16,4096]{1,0:T(8,128)(2,1)S(1)} collective-permute-done((bf16[16,4096]{1,0:T(8,128)(2,1)S(1)}, bf16[16,4096]{1,0:T(8,128)(2,1)S(1)}, u32[]{:S(2)}, u32[]{:S(2)}) %collective-permute-start.9) | collective-permute-done | bytes 131104 | tf_op jit(solution)/shard_map/ppermute | solution.py:44
  32.2 4.8 %collective-permute-start.6 = (bf16[16,4096]{1,0:T(8,128)(2,1)S(1)}, bf16[16,4096]{1,0:T(8,128)(2,1)S(1)}, u32[]{:S(2)}, u32[]{:S(2)}) collective-permute-start(bf16[16,4096]{1,0:T(8,128)(2,1)S(1)} %collective-permute-done.5), channel_id=1, source_target_pairs={{0,1},{1,0},{2,3},{3,2},{4,5},{5,4},{6,7},{7,6},{8,9},{9,8},{10,11... | collective-permute-start | bytes 393224 | tf_op jit(solution)/shard_map/ppermute | solution.py:50
  37.0 1.8 %collective-permute-start.12 = (bf16[16,4096]{1,0:T(8,128)(2,1)S(1)}, bf16[16,4096]{1,0:T(8,128)(2,1)S(1)}, u32[]{:S(2)}, u32[]{:S(2)}) collective-permute-start(bf16[16,4096]{1,0:T(8,128)(2,1)S(1)} %collective-permute-done.11), channel_id=1, source_target_pairs={{0,1},{1,0},{2,3},{3,2},{4,5},{5,4},{6,7},{7,6},{8,9},{9,8},{10,11... | collective-permute-start | bytes 393224 | tf_op jit(solution)/shard_map/ppermute | solution.py:50
  45.9 2.2 %multiply_reduce_fusion = (f32[]{:T(128)}, f32[]{:T(128)}, bf16[128,512]{1,0:T(8,128)(2,1)S(1)}, bf16[128,512]{1,0:T(8,128)(2,1)S(1)}, f32[128,512]{1,0:T(8,128)}) fusion(f32[512]{0:T(512)S(1)} %get-tuple-element.58, f32[512]{0:T(512)S(1)} %get-tuple-element.69, pred[128]{0:T(512)(128)(4,1)S(1)} %get-tuple-element.72, f32[512]{0:T(512)S(1)} %get-tuple-element.70, ...), kind=kOutput, calls=%fused_computation.76 | convolution fusion | flops 538050560 | bytes 6038024 | tf_op jit(solution)/shard_map/dot_general | solution.py:153
  48.1 2.1 %fusion.92 = (bf16[128,4096]{1,0:T(8,128)(2,1)S(1)}, f32[128,4096]{1,0:T(8,128)}) fusion(bf16[128,512]{1,0:T(8,128)(2,1)S(1)} %get-tuple-element.10, bf16[1,512,4096]{2,1,0:T(8,128)(2,1)S(1)} %copy-done), kind=kOutput, calls=%fused_computation.174 | convolution fusion | flops 537395200 | bytes 7471104 | tf_op jit(solution)/shard_map/dot_general | solution.py:161
  65.4 2.5 %collective-permute-done.16 = bf16[16,4096]{1,0:T(8,128)(2,1)S(1)} collective-permute-done((bf16[16,4096]{1,0:T(8,128)(2,1)S(1)}, bf16[16,4096]{1,0:T(8,128)(2,1)S(1)}, u32[]{:S(2)}, u32[]{:S(2)}) %collective-permute-start.16) | collective-permute-done | bytes 131104 | tf_op jit(solution)/shard_map/ppermute | solution.py:44
  69.8 1.6 %collective-permute-start.32 = (bf16[16,4096]{1,0:T(8,128)(2,1)S(1)}, bf16[16,4096]{1,0:T(8,128)(2,1)S(1)}, u32[]{:S(2)}, u32[]{:S(2)}) collective-permute-start(bf16[16,4096]{1,0:T(8,128)(2,1)S(1)} %fusion.69), channel_id=1, source_target_pairs={{0,4},{1,3},{2,0},{3,7},{4,8},{5,1},{6,2},{7,11},{8,12},{9,5},{10,... | collective-permute-start | bytes 393224 | tf_op jit(solution)/shard_map/ppermute | solution.py:44
  71.4 2.5 %collective-permute-done.17 = bf16[16,4096]{1,0:T(8,128)(2,1)S(1)} collective-permute-done((bf16[16,4096]{1,0:T(8,128)(2,1)S(1)}, bf16[16,4096]{1,0:T(8,128)(2,1)S(1)}, u32[]{:S(2)}, u32[]{:S(2)}) %collective-permute-start.17) | collective-permute-done | bytes 131104 | tf_op jit(solution)/shard_map/ppermute | solution.py:44
  75.8 1.6 %collective-permute-start.33 = (bf16[16,4096]{1,0:T(8,128)(2,1)S(1)}, bf16[16,4096]{1,0:T(8,128)(2,1)S(1)}, u32[]{:S(2)}, u32[]{:S(2)}) collective-permute-start(bf16[16,4096]{1,0:T(8,128)(2,1)S(1)} %fusion.71), channel_id=1, source_target_pairs={{0,4},{1,3},{2,0},{3,7},{4,8},{5,1},{6,2},{7,11},{8,12},{9,5},{10,... | collective-permute-start | bytes 393224 | tf_op jit(solution)/shard_map/ppermute | solution.py:44
  77.4 2.5 %collective-permute-done.18 = bf16[16,4096]{1,0:T(8,128)(2,1)S(1)} collective-permute-done((bf16[16,4096]{1,0:T(8,128)(2,1)S(1)}, bf16[16,4096]{1,0:T(8,128)(2,1)S(1)}, u32[]{:S(2)}, u32[]{:S(2)}) %collective-permute-start.18) | collective-permute-done | bytes 131104 | tf_op jit(solution)/shard_map/ppermute | solution.py:44
  80.9 2.2 %collective-permute-start.19 = (bf16[16,4096]{1,0:T(8,128)(2,1)S(1)}, bf16[16,4096]{1,0:T(8,128)(2,1)S(1)}, u32[]{:S(2)}, u32[]{:S(2)}) collective-permute-start(bf16[16,4096]{1,0:T(8,128)(2,1)S(1)} %fusion.80), channel_id=1, source_target_pairs={{0,1},{1,0},{2,3},{3,2},{4,5},{5,4},{6,7},{7,6},{8,9},{9,8},{10,11... | collective-permute-start | bytes 393224 | tf_op jit(solution)/shard_map/ppermute | solution.py:50
  91.1 2.4 %collective-permute-done.36 = bf16[16,4224]{1,0:T(8,128)(2,1)S(1)} collective-permute-done((bf16[16,4224]{1,0:T(8,128)(2,1)S(1)}, bf16[16,4224]{1,0:T(8,128)(2,1)S(1)}, u32[]{:S(2)}, u32[]{:S(2)}) %collective-permute-start.36) | collective-permute-done | bytes 135200 | tf_op jit(solution)/shard_map/ppermute | solution.py:44
  96.1 2.4 %collective-permute-done.37 = bf16[16,4224]{1,0:T(8,128)(2,1)S(1)} collective-permute-done((bf16[16,4224]{1,0:T(8,128)(2,1)S(1)}, bf16[16,4224]{1,0:T(8,128)(2,1)S(1)}, u32[]{:S(2)}, u32[]{:S(2)}) %collective-permute-start.37) | collective-permute-done | bytes 135200 | tf_op jit(solution)/shard_map/ppermute | solution.py:44
  100.8 2.7 %collective-permute-done.38 = bf16[16,4224]{1,0:T(8,128)(2,1)S(1)} collective-permute-done((bf16[16,4224]{1,0:T(8,128)(2,1)S(1)}, bf16[16,4224]{1,0:T(8,128)(2,1)S(1)}, u32[]{:S(2)}, u32[]{:S(2)}) %collective-permute-start.38) | collective-permute-done | bytes 135200 | tf_op jit(solution)/shard_map/ppermute | solution.py:44
  105.2 5.6 %collective-permute-start.27 = (bf16[16,4224]{1,0:T(8,128)(2,1)S(1)}, bf16[16,4224]{1,0:T(8,128)(2,1)S(1)}, u32[]{:S(2)}, u32[]{:S(2)}) collective-permute-start(bf16[16,4224]{1,0:T(8,128)(2,1)S(1)} %collective-permute-done.26), channel_id=1, source_target_pairs={{0,1},{1,0},{2,3},{3,2},{4,5},{5,4},{6,7},{7,6},{8,9},{9,8},{10,11... | collective-permute-start | bytes 405512 | tf_op jit(solution)/shard_map/ppermute | solution.py:50
  110.8 2.2 %collective-permute-start.41 = (bf16[16,4224]{1,0:T(8,128)(2,1)S(1)}, bf16[16,4224]{1,0:T(8,128)(2,1)S(1)}, u32[]{:S(2)}, u32[]{:S(2)}) collective-permute-start(bf16[16,4224]{1,0:T(8,128)(2,1)S(1)} %collective-permute-done.40), channel_id=1, source_target_pairs={{0,1},{1,0},{2,3},{3,2},{4,5},{5,4},{6,7},{7,6},{8,9},{9,8},{10,11... | collective-permute-start | bytes 405512 | tf_op jit(solution)/shard_map/ppermute | solution.py:50
  115.6 3.9 %fusion.57 = bf16[128,512]{1,0:T(8,128)(2,1)S(1)} fusion(f32[128,512]{1,0:T(8,128)S(1)} %fusion.30, bf16[1,512,4096]{2,1,0:T(8,128)(2,1)} %param.11, f32[512]{0:T(512)S(1)} %copy-done.14, f32[512]{0:T(512)S(1)} %get-tuple-element.69, f32[512]{0:T(512)S(1)} %get-tuple-element.70, pred[128]{0:T(512)(128)(4,1)S(1)} %copy-done.13, ...), kind=kOutput, calls=%fused_computation.36 | convolution fusion | flops 537329664 | bytes 5643264 | tf_op jit(solution)/shard_map/dot_general | solution.py:192
  123.6 1.9 %collective-permute-start.42 = (f32[]{:T(128)}, f32[]{:T(128)}, u32[]{:S(2)}, u32[]{:S(2)}) collective-permute-start(f32[]{:T(128)} %add.245), channel_id=1, source_target_pairs={{0,16},{16,0},{1,17},{17,1},{2,18},{18,2},{3,19},{19,3},{4,20},{20... | collective-permute-start | bytes 20 | tf_op jit(solution)/shard_map/ppermute | solution.py:176
  126.1 5.0 %fusion.4 = bf16[1,4096,512]{2,1,0:T(8,128)(2,1)} fusion(bf16[256,4096]{1,0:T(8,128)(2,1)} %get-tuple-element.29, bf16[128,512]{1,0:T(8,128)(2,1)S(1)} %fusion.57, bf16[128,512]{1,0:T(8,128)(2,1)S(1)} %fusion.60), kind=kOutput, calls=%fused_computation.7 | convolution fusion | flops 1076363264 | bytes 6553600 | tf_op jit(solution)/shard_map/dot_general | solution.py:99
  131.2 3.2 %fusion.5 = bf16[1,512,4096]{2,1,0:T(8,128)(2,1)} fusion(bf16[1,512,4096]{2,1,0:T(8,128)(2,1)S(1)} %copy-done.2, f32[512]{0:T(512)S(1)} %get-tuple-element.58, f32[512]{0:T(512)S(1)} %copy-done.15, bf16[128,4096]{1,0:T(8,128)(2,1)S(1)} %copy-done.5, bf16[128,4096]{1,0:T(8,128)(2,1)S(1)} %copy-done.4, bf16[128,512]{1,0:T(8,128)(2,1)S(1)} %get-tuple-element.11, ...), kind=kOutput, calls=%fused_computation.8 | convolution fusion | flops 1088946176 | bytes 10752000 | tf_op jit(solution)/shard_map/dot_general | solution.py:99
  (188 shorter events, 63.5 us)
Async XLA Ops:
  0.6 9.3 %collective-permute-start.20 = (bf16[16,4096]{1,0:T(8,128)(2,1)}, bf16[16,4096]{1,0:T(8,128)(2,1)S(1)}, u32[]{:S(2)}, u32[]{:S(2)}) collective-permute-start(bf16[16,4096]{1,0:T(8,128)(2,1)} %bitcast.87), channel_id=1, source_target_pairs={{0,16},{16,0},{1,17},{17,1},{2,18},{18,2},{3,19},{19,3},{4,20},{20... | collective-permute-start | bytes 393224 | tf_op jit(solution)/shard_map/ppermute | solution.py:129
  3.7 6.9 %collective-permute-start = (bf16[16,4096]{1,0:T(8,128)(2,1)}, bf16[16,4096]{1,0:T(8,128)(2,1)S(1)}, u32[]{:S(2)}, u32[]{:S(2)}) collective-permute-start(bf16[16,4096]{1,0:T(8,128)(2,1)} %bitcast.83), channel_id=1, source_target_pairs={{0,1},{1,0},{2,3},{3,2},{4,5},{5,4},{6,7},{7,6},{8,9},{9,8},{10,11... | collective-permute-start | bytes 393224 | tf_op jit(solution)/shard_map/ppermute | solution.py:50
  12.9 5.0 %collective-permute-start.1 = (bf16[16,4096]{1,0:T(8,128)(2,1)S(1)}, bf16[16,4096]{1,0:T(8,128)(2,1)S(1)}, u32[]{:S(2)}, u32[]{:S(2)}) collective-permute-start(bf16[16,4096]{1,0:T(8,128)(2,1)S(1)} %pad_maximum_fusion.10), channel_id=1, source_target_pairs={{0,4},{1,3},{2,0},{3,7},{4,8},{5,1},{6,2},{7,11},{8,12},{9,5},{10,... | collective-permute-start | bytes 393224 | tf_op jit(solution)/shard_map/ppermute | solution.py:44
  14.5 5.0 %collective-permute-start.7 = (bf16[16,4096]{1,0:T(8,128)(2,1)S(1)}, bf16[16,4096]{1,0:T(8,128)(2,1)S(1)}, u32[]{:S(2)}, u32[]{:S(2)}) collective-permute-start(bf16[16,4096]{1,0:T(8,128)(2,1)S(1)} %pad_maximum_fusion.11), channel_id=1, source_target_pairs={{0,4},{1,3},{2,0},{3,7},{4,8},{5,1},{6,2},{7,11},{8,12},{9,5},{10,... | collective-permute-start | bytes 393224 | tf_op jit(solution)/shard_map/ppermute | solution.py:44
  22.9 6.7 %collective-permute-start.3 = (bf16[16,4096]{1,0:T(8,128)(2,1)S(1)}, bf16[16,4096]{1,0:T(8,128)(2,1)S(1)}, u32[]{:S(2)}, u32[]{:S(2)}) collective-permute-start(bf16[16,4096]{1,0:T(8,128)(2,1)S(1)} %collective-permute-done.2), channel_id=1, source_target_pairs={{0,4},{1,3},{2,0},{3,7},{4,8},{5,1},{6,2},{7,11},{8,12},{9,5},{10,... | collective-permute-start | bytes 393224 | tf_op jit(solution)/shard_map/ppermute | solution.py:44
  29.5 14.1 %collective-permute-start.10 = (bf16[48,4096]{1,0:T(8,128)(2,1)S(1)}, bf16[48,4096]{1,0:T(8,128)(2,1)S(1)}, u32[]{:S(2)}, u32[]{:S(2)}) collective-permute-start(bf16[48,4096]{1,0:T(8,128)(2,1)S(1)} %pad_maximum_fusion.3), channel_id=1, source_target_pairs={{0,1},{1,0},{2,3},{3,2},{4,5},{5,4},{6,7},{7,6},{8,9},{9,8},{10,11... | collective-permute-start | bytes 1179656 | tf_op jit(solution)/shard_map/ppermute | solution.py:50
  29.6 9.2 %collective-permute-start.4 = (bf16[48,4096]{1,0:T(8,128)(2,1)S(1)}, bf16[48,4096]{1,0:T(8,128)(2,1)S(1)}, u32[]{:S(2)}, u32[]{:S(2)}) collective-permute-start(bf16[48,4096]{1,0:T(8,128)(2,1)S(1)} %pad_maximum_fusion.2), channel_id=1, source_target_pairs={{0,1},{1,0},{2,3},{3,2},{4,5},{5,4},{6,7},{7,6},{8,9},{9,8},{10,11... | collective-permute-start | bytes 1179656 | tf_op jit(solution)/shard_map/ppermute | solution.py:50
  30.8 6.1 %collective-permute-start.11 = (bf16[16,4096]{1,0:T(8,128)(2,1)S(1)}, bf16[16,4096]{1,0:T(8,128)(2,1)S(1)}, u32[]{:S(2)}, u32[]{:S(2)}) collective-permute-start(bf16[16,4096]{1,0:T(8,128)(2,1)S(1)} %collective-permute-done.9), channel_id=1, source_target_pairs={{1,3},{3,7},{5,1},{7,11},{9,5},{11,15},{13,9},{15,13},{17,19},{19,... | collective-permute-start | bytes 393224 | tf_op jit(solution)/shard_map/ppermute | solution.py:47
  32.2 7.4 %collective-permute-start.6 = (bf16[16,4096]{1,0:T(8,128)(2,1)S(1)}, bf16[16,4096]{1,0:T(8,128)(2,1)S(1)}, u32[]{:S(2)}, u32[]{:S(2)}) collective-permute-start(bf16[16,4096]{1,0:T(8,128)(2,1)S(1)} %collective-permute-done.5), channel_id=1, source_target_pairs={{0,1},{1,0},{2,3},{3,2},{4,5},{5,4},{6,7},{7,6},{8,9},{9,8},{10,11... | collective-permute-start | bytes 393224 | tf_op jit(solution)/shard_map/ppermute | solution.py:50
  37.0 7.4 %collective-permute-start.12 = (bf16[16,4096]{1,0:T(8,128)(2,1)S(1)}, bf16[16,4096]{1,0:T(8,128)(2,1)S(1)}, u32[]{:S(2)}, u32[]{:S(2)}) collective-permute-start(bf16[16,4096]{1,0:T(8,128)(2,1)S(1)} %collective-permute-done.11), channel_id=1, source_target_pairs={{0,1},{1,0},{2,3},{3,2},{4,5},{5,4},{6,7},{7,6},{8,9},{9,8},{10,11... | collective-permute-start | bytes 393224 | tf_op jit(solution)/shard_map/ppermute | solution.py:50
  56.8 5.1 %collective-permute-start.13 = (bf16[48,4096]{1,0:T(8,128)(2,1)}, bf16[48,4096]{1,0:T(8,128)(2,1)S(1)}, u32[]{:S(2)}, u32[]{:S(2)}) collective-permute-start(bf16[48,4096]{1,0:T(8,128)(2,1)} %slice.156), channel_id=1, source_target_pairs={{0,1},{1,0},{2,3},{3,2},{4,5},{5,4},{6,7},{7,6},{8,9},{9,8},{10,11... | collective-permute-start | bytes 1179656 | tf_op jit(solution)/shard_map/ppermute | solution.py:50
  57.3 6.4 %collective-permute-start.28 = (bf16[48,4096]{1,0:T(8,128)(2,1)}, bf16[48,4096]{1,0:T(8,128)(2,1)S(1)}, u32[]{:S(2)}, u32[]{:S(2)}) collective-permute-start(bf16[48,4096]{1,0:T(8,128)(2,1)} %slice.169), channel_id=1, source_target_pairs={{0,1},{1,0},{2,3},{3,2},{4,5},{5,4},{6,7},{7,6},{8,9},{9,8},{10,11... | collective-permute-start | bytes 1179656 | tf_op jit(solution)/shard_map/ppermute | solution.py:50
  62.9 5.0 %collective-permute-start.16 = (bf16[16,4096]{1,0:T(8,128)(2,1)S(1)}, bf16[16,4096]{1,0:T(8,128)(2,1)S(1)}, u32[]{:S(2)}, u32[]{:S(2)}) collective-permute-start(bf16[16,4096]{1,0:T(8,128)(2,1)S(1)} %fusion.75), channel_id=1, source_target_pairs={{0,4},{1,3},{2,0},{3,7},{4,8},{5,1},{6,2},{7,11},{8,12},{9,5},{10,... | collective-permute-start | bytes 393224 | tf_op jit(solution)/shard_map/ppermute | solution.py:44
  63.8 6.0 %collective-permute-start.31 = (bf16[16,4096]{1,0:T(8,128)(2,1)S(1)}, bf16[16,4096]{1,0:T(8,128)(2,1)S(1)}, u32[]{:S(2)}, u32[]{:S(2)}) collective-permute-start(bf16[16,4096]{1,0:T(8,128)(2,1)S(1)} %fusion.67), channel_id=1, source_target_pairs={{0,4},{1,3},{2,0},{3,7},{4,8},{5,1},{6,2},{7,11},{8,12},{9,5},{10,... | collective-permute-start | bytes 393224 | tf_op jit(solution)/shard_map/ppermute | solution.py:44
  68.9 5.0 %collective-permute-start.17 = (bf16[16,4096]{1,0:T(8,128)(2,1)S(1)}, bf16[16,4096]{1,0:T(8,128)(2,1)S(1)}, u32[]{:S(2)}, u32[]{:S(2)}) collective-permute-start(bf16[16,4096]{1,0:T(8,128)(2,1)S(1)} %fusion.77), channel_id=1, source_target_pairs={{0,4},{1,3},{2,0},{3,7},{4,8},{5,1},{6,2},{7,11},{8,12},{9,5},{10,... | collective-permute-start | bytes 393224 | tf_op jit(solution)/shard_map/ppermute | solution.py:44
  69.8 6.0 %collective-permute-start.32 = (bf16[16,4096]{1,0:T(8,128)(2,1)S(1)}, bf16[16,4096]{1,0:T(8,128)(2,1)S(1)}, u32[]{:S(2)}, u32[]{:S(2)}) collective-permute-start(bf16[16,4096]{1,0:T(8,128)(2,1)S(1)} %fusion.69), channel_id=1, source_target_pairs={{0,4},{1,3},{2,0},{3,7},{4,8},{5,1},{6,2},{7,11},{8,12},{9,5},{10,... | collective-permute-start | bytes 393224 | tf_op jit(solution)/shard_map/ppermute | solution.py:44
  75.8 7.3 %collective-permute-start.33 = (bf16[16,4096]{1,0:T(8,128)(2,1)S(1)}, bf16[16,4096]{1,0:T(8,128)(2,1)S(1)}, u32[]{:S(2)}, u32[]{:S(2)}) collective-permute-start(bf16[16,4096]{1,0:T(8,128)(2,1)S(1)} %fusion.71), channel_id=1, source_target_pairs={{0,4},{1,3},{2,0},{3,7},{4,8},{5,1},{6,2},{7,11},{8,12},{9,5},{10,... | collective-permute-start | bytes 393224 | tf_op jit(solution)/shard_map/ppermute | solution.py:44
  85.6 5.1 %collective-permute-start.22 = (bf16[16,4224]{1,0:T(8,128)(2,1)S(1)}, bf16[16,4224]{1,0:T(8,128)(2,1)S(1)}, u32[]{:S(2)}, u32[]{:S(2)}) collective-permute-start(bf16[16,4224]{1,0:T(8,128)(2,1)S(1)} %get-tuple-element.7), channel_id=1, source_target_pairs={{0,4},{1,3},{2,0},{3,7},{4,8},{5,1},{6,2},{7,11},{8,12},{9,5},{10,... | collective-permute-start | bytes 405512 | tf_op jit(solution)/shard_map/ppermute | solution.py:44
  88.4 5.1 %collective-permute-start.36 = (bf16[16,4224]{1,0:T(8,128)(2,1)S(1)}, bf16[16,4224]{1,0:T(8,128)(2,1)S(1)}, u32[]{:S(2)}, u32[]{:S(2)}) collective-permute-start(bf16[16,4224]{1,0:T(8,128)(2,1)S(1)} %get-tuple-element.9), channel_id=1, source_target_pairs={{0,4},{1,3},{2,0},{3,7},{4,8},{5,1},{6,2},{7,11},{8,12},{9,5},{10,... | collective-permute-start | bytes 405512 | tf_op jit(solution)/shard_map/ppermute | solution.py:44
  100.7 12.4 %collective-permute-start.25 = (bf16[48,4224]{1,0:T(8,128)(2,1)S(1)}, bf16[48,4224]{1,0:T(8,128)(2,1)S(1)}, u32[]{:S(2)}, u32[]{:S(2)}) collective-permute-start(bf16[48,4224]{1,0:T(8,128)(2,1)S(1)} %pad_maximum_fusion), channel_id=1, source_target_pairs={{0,1},{1,0},{2,3},{3,2},{4,5},{5,4},{6,7},{7,6},{8,9},{9,8},{10,11... | collective-permute-start | bytes 1216520 | tf_op jit(solution)/shard_map/ppermute | solution.py:50
  103.6 9.6 %collective-permute-start.39 = (bf16[48,4224]{1,0:T(8,128)(2,1)S(1)}, bf16[48,4224]{1,0:T(8,128)(2,1)S(1)}, u32[]{:S(2)}, u32[]{:S(2)}) collective-permute-start(bf16[48,4224]{1,0:T(8,128)(2,1)S(1)} %pad_maximum_fusion.1), channel_id=1, source_target_pairs={{0,1},{1,0},{2,3},{3,2},{4,5},{5,4},{6,7},{7,6},{8,9},{9,8},{10,11... | collective-permute-start | bytes 1216520 | tf_op jit(solution)/shard_map/ppermute | solution.py:50
  104.3 6.5 %collective-permute-start.40 = (bf16[16,4224]{1,0:T(8,128)(2,1)S(1)}, bf16[16,4224]{1,0:T(8,128)(2,1)S(1)}, u32[]{:S(2)}, u32[]{:S(2)}) collective-permute-start(bf16[16,4224]{1,0:T(8,128)(2,1)S(1)} %collective-permute-done.38), channel_id=1, source_target_pairs={{1,3},{3,7},{5,1},{7,11},{9,5},{11,15},{13,9},{15,13},{17,19},{19,... | collective-permute-start | bytes 405512 | tf_op jit(solution)/shard_map/ppermute | solution.py:47
  105.2 7.9 %collective-permute-start.27 = (bf16[16,4224]{1,0:T(8,128)(2,1)S(1)}, bf16[16,4224]{1,0:T(8,128)(2,1)S(1)}, u32[]{:S(2)}, u32[]{:S(2)}) collective-permute-start(bf16[16,4224]{1,0:T(8,128)(2,1)S(1)} %collective-permute-done.26), channel_id=1, source_target_pairs={{0,1},{1,0},{2,3},{3,2},{4,5},{5,4},{6,7},{7,6},{8,9},{9,8},{10,11... | collective-permute-start | bytes 405512 | tf_op jit(solution)/shard_map/ppermute | solution.py:50
  123.6 10.8 %collective-permute-start.42 = (f32[]{:T(128)}, f32[]{:T(128)}, u32[]{:S(2)}, u32[]{:S(2)}) collective-permute-start(f32[]{:T(128)} %add.245), channel_id=1, source_target_pairs={{0,16},{16,0},{1,17},{17,1},{2,18},{18,2},{3,19},{19,3},{4,20},{20... | collective-permute-start | bytes 20 | tf_op jit(solution)/shard_map/ppermute | solution.py:176
  (39 other events, 294.7 us)

commit v2 on v1

v2 whole, which is shorter than its diff:
```python
import functools

import jax
import jax.numpy as jnp
import numpy as np
from jax import lax
from jax.experimental import pallas as pl
from jax.experimental.pallas import tpu as pltpu
from jax.sharding import PartitionSpec as P

TBLOCK = 128
FBLOCK = 128
PAD = 128

penalty_weight = 0.5
norm_epsilon = 1e-06
f32 = jnp.float32
bf16 = jnp.bfloat16


class Ring:
    def __init__(self, size):
        self.size = size
        chips = size // 2
        self.chips = chips
        self.hops = (chips - 1) // 2
        self.far = chips % 2 == 0
        order = list(range(0, chips, 2)) + list(range(1, chips, 2))[::-1]
        place = {chip: at for at, chip in enumerate(order)}
        self.step, self.far_step = [], []
        owners = []
        for device in range(size):
            chip, core = divmod(device, 2)
            at = place[chip]
            ahead = 1 if core == 0 else -1
            pair = (device, order[(at + ahead) % chips] * 2 + core)
            self.step.append(pair)
            if core == 1:
                self.far_step.append(pair)
            behind = [order[(at - ahead * k) % chips] for k in range(1, self.hops + 1)]
            front = [order[(at + ahead * k) % chips] for k in range(1, self.hops + 1)]
            last = [order[(at + self.hops + 1) % chips]] if self.far else []
            owners.append([2 * c + i for c in [chip] + behind + front + last for i in (0, 1)])
        self.owners = np.array(owners, np.int32)
        self.twin = [(device, device ^ 1) for device in range(size)]

    def along(self, block):
        return lax.ppermute(block, "feat", self.step)

    def along_far(self, block):
        return lax.ppermute(block, "feat", self.far_step)

    def across(self, block):
        return lax.ppermute(block, "feat", self.twin)


def chip_block(ring, core, own):
    other = ring.across(own)
    return jnp.concatenate(
        [jnp.where(core == 0, own, other), jnp.where(core == 0, other, own)], axis=0
    )


def after(values, signal):
    return lax.optimization_barrier((values, signal))[0]


def gather(ring, core, block):
    behind = []
    moving = block
    for _ in range(ring.hops):
        moving = ring.along(moving)
        behind.append(moving)
    parts = [block]
    came = None
    if ring.far:
        came = ring.along_far(moving)
    if behind:
        stack = jnp.concatenate(behind, axis=0)
        parts += [stack, ring.across(stack)]
    if ring.far:
        parts.append(jnp.where(core == 1, came, ring.across(came)))
    return parts, behind


def scatter_sum(ring, rows, own, sent, front, last):
    from_twin = ring.across(sent)
    arrived = None
    states = []
    if ring.far:
        total = last + from_twin[rows * ring.hops :].astype(f32)
        arrived = ring.along_far(total.astype(bf16))
    for k in range(ring.hops, 0, -1):
        total = front[rows * (k - 1) : rows * k]
        total = total + from_twin[rows * (k - 1) : rows * k].astype(f32)
        if arrived is not None:
            total = total + arrived.astype(f32)
        arrived = ring.along(total.astype(bf16))
        states.append(arrived)
    total = own
    if arrived is not None:
        total = total + arrived.astype(f32)
    mine = total.astype(bf16)
    return mine.astype(f32) + ring.across(mine).astype(f32), states


def in_vmem(x):
    return pltpu.with_memory_space_constraint(x, pltpu.VMEM)


VMEM_SPEC = pl.BlockSpec(memory_space=pltpu.VMEM)
ANY_SPEC = pl.BlockSpec(memory_space=pl.ANY)


def stacked(refs, columns):
    return jnp.concatenate([ref[:, columns] for ref in refs], axis=0)


def whole_pieces(parts):
    if all(p.shape[0] % 16 == 0 for p in parts):
        return parts
    return [jnp.concatenate(parts, axis=0)]


def forward_kernel(count, step, *refs):
    pieces = refs[:count]
    enc_ref, bias_ref, keep_ref, dec_ref = refs[count : count + 4]
    act_ref, gate_ref, sum_ref = refs[count + 4 : count + 7]
    outs = refs[count + 7 :]
    width = dec_ref.shape[1]
    preact = jnp.zeros(gate_ref.shape, f32)
    for at in range(0, width, step):
        preact = preact + jnp.dot(
            stacked(pieces, slice(at, at + step)), enc_ref[at : at + step, :], preferred_element_type=f32
        )
    positive = jnp.maximum(preact + bias_ref[...], 0.0)
    keep = keep_ref[...]
    act = (keep * positive * positive).astype(bf16)
    act_ref[...] = act
    gate_ref[...] = keep * 2.0 * positive
    sum_ref[...] = jnp.sum(act.astype(f32), axis=0, keepdims=True)
    for at in range(0, width, step):
        part = jnp.dot(act, dec_ref[:, at : at + step], preferred_element_type=f32)
        if len(outs) == 1:
            outs[0][:, at : at + step] = part
            continue
        own_ref, sent_ref, front_ref, last_ref = outs
        rows, hop = own_ref.shape[0], front_ref.shape[0]
        own_ref[:, at : at + step] = part[:rows]
        sent_ref[:hop, at : at + step] = part[rows : rows + hop].astype(bf16)
        sent_ref[hop:, at : at + step] = part[rows + 2 * hop :].astype(bf16)
        front_ref[:, at : at + step] = part[rows + hop : rows + 2 * hop]
        last_ref[:, at : at + step] = part[rows + 2 * hop :]


def forward(parts, encoder, bias, keep, decoder):
    pieces = whole_pieces(parts)
    total, features = keep.shape
    width = decoder.shape[1]
    shapes = [((total, features), bf16), ((total, features), f32), ((1, features), f32)]
    if len(pieces) == 4:
        rows, hop = parts[0].shape[0], parts[1].shape[0]
        shapes += [((rows, width), f32), ((hop + rows, width), bf16), ((hop, width), f32), ((rows, width), f32)]
    else:
        shapes += [((total, width), f32)]
    flops = 4 * total * features * width
    outs = pl.pallas_call(
        functools.partial(forward_kernel, len(pieces), min(512, width)),
        out_shape=[pltpu.VMEM(shape, dtype) for shape, dtype in shapes],
        in_specs=[VMEM_SPEC] * (len(pieces) + 4),
        out_specs=[VMEM_SPEC] * len(shapes),
        compiler_params=pltpu.CompilerParams(vmem_limit_bytes=12 << 20),
        cost_estimate=pl.CostEstimate(flops=flops, bytes_accessed=1 << 20, transcendentals=0),
    )(*[in_vmem(x) for x in (*pieces, encoder, bias, keep, decoder)])
    act, gate, act_sum = outs[:3]
    if len(outs) > 4:
        return act, gate, act_sum, outs[3:]
    full = outs[3]
    sizes = [p.shape[0] for p in parts]
    ends = np.cumsum([0] + sizes)
    cut = [full[ends[i] : ends[i + 1]] for i in range(len(sizes))]
    own = cut[0]
    hop = sizes[1] if len(sizes) > 2 else 0
    front = full[ends[2] : ends[3]] if hop else None
    last = cut[-1] if len(sizes) % 2 == 0 else full[:0]
    behind = full[ends[1] : ends[2]] if hop else full[:0]
    sent = jnp.concatenate([behind, last], axis=0).astype(bf16)
    return act, gate, act_sum, (own, sent, front, last)


def turn_kernel(*refs):
    pieces, out_ref = refs[:-1], refs[-1]
    step = 128 if out_ref.shape[0] % 128 == 0 else out_ref.shape[0]
    for at in range(0, out_ref.shape[0], step):
        out_ref[at : at + step, :] = stacked(pieces, slice(at, at + step)).T


def turned(parts):
    pieces = whole_pieces(parts)
    total = sum(p.shape[0] for p in pieces)
    width = pieces[0].shape[1]
    return pl.pallas_call(
        turn_kernel,
        out_shape=pltpu.VMEM((width, total), bf16),
        in_specs=[VMEM_SPEC] * len(pieces),
        out_specs=VMEM_SPEC,
        compiler_params=pltpu.CompilerParams(vmem_limit_bytes=12 << 20),
        cost_estimate=pl.CostEstimate(flops=0, bytes_accessed=4 << 20, transcendentals=0),
    )(*[in_vmem(x) for x in pieces])


def backward_kernel(counts, step, *refs):
    halves = len(counts)
    at = sum(counts)
    errors = refs[:at]
    acts, gates, rows = (refs[at + halves * i : at + halves * (i + 1)] for i in range(3))
    dec_ref, norm_ref, coef_ref = refs[at + 3 * halves : at + 3 * halves + 3]
    enc_out, bias_out, dec_out = refs[at + 3 * halves + 3 : at + 3 * halves + 6]
    enc_stage, dec_stage, enc_sems, dec_sems = refs[at + 3 * halves + 6 :]
    features, width = dec_ref.shape
    turned_act = jnp.concatenate([a[...] for a in acts], axis=0).T
    coef = coef_ref[...]
    copies = []
    for i, at in enumerate(range(0, width, step)):
        columns = slice(at, at + step)
        grad = jnp.dot(turned_act, stacked(errors, columns), preferred_element_type=f32)
        grad = grad + coef * dec_ref[:, columns].astype(f32)
        dec_stage[:, columns] = grad.astype(bf16)
        copy = pltpu.make_async_copy(dec_stage.at[:, columns], dec_out.at[:, columns], dec_sems.at[i])
        copy.start()
        copies.append(copy)
    total = turned_act.shape[1]
    act_grad = jnp.zeros((total, features), f32)
    for at in range(0, width, step):
        columns = slice(at, at + step)
        act_grad = act_grad + lax.dot_general(
            stacked(errors, columns), dec_ref[:, columns], (((1,), (1,)), ((), ())), preferred_element_type=f32
        )
    gate = jnp.concatenate([g[...] for g in gates], axis=0)
    pre_grad = ((act_grad + penalty_weight * norm_ref[...]) * gate).astype(bf16)
    bias_out[...] = jnp.sum(pre_grad.astype(f32), axis=0, keepdims=True)
    for i, at in enumerate(range(0, width, step)):
        here = slice(at, at + step)
        left = jnp.concatenate([r[here, :] for r in rows], axis=1)
        enc_stage[here, :] = jnp.dot(left, pre_grad, preferred_element_type=f32).astype(bf16)
        copy = pltpu.make_async_copy(enc_stage.at[here, :], enc_out.at[here, :], enc_sems.at[i])
        copy.start()
        copies.append(copy)
    for copy in copies:
        copy.wait()


def backward(errors, acts, gates, rows, decoder, norms, coef):
    errors = [whole_pieces(e) for e in errors]
    features, width = decoder.shape
    step = min(512, width)
    operands = [x for e in errors for x in e] + acts + gates + rows + [decoder, norms, coef]
    total = sum(a.shape[0] for a in acts)
    return pl.pallas_call(
        functools.partial(backward_kernel, tuple(len(e) for e in errors), step),
        out_shape=[
            jax.ShapeDtypeStruct((width, features), bf16),
            jax.ShapeDtypeStruct((1, features), f32),
            jax.ShapeDtypeStruct((features, width), bf16),
        ],
        in_specs=[VMEM_SPEC] * len(operands),
        out_specs=[ANY_SPEC, VMEM_SPEC, ANY_SPEC],
        scratch_shapes=[
            pltpu.VMEM((width, features), bf16),
            pltpu.VMEM((features, width), bf16),
            pltpu.SemaphoreType.DMA((width // step,)),
            pltpu.SemaphoreType.DMA((width // step,)),
        ],
        compiler_params=pltpu.CompilerParams(vmem_limit_bytes=24 << 20),
        cost_estimate=pl.CostEstimate(flops=6 * total * features * width, bytes_accessed=8 << 20, transcendentals=0),
    )(*[in_vmem(x) for x in operands])


def split_three(value):
    high = value.astype(bf16)
    rest = value - high.astype(f32)
    middle = rest.astype(bf16)
    low = (rest - middle.astype(f32)).astype(bf16)
    return [high, middle, low]


def body(residual, targets, w_enc, b_enc, w_dec, block_mask):
    row_count = residual.shape[1]
    width = residual.shape[2]
    layers = lax.axis_size("layer")
    feats = lax.axis_size("feat")
    tokens = row_count * feats
    ring = Ring(feats)
    device = lax.axis_index("feat")
    core = device % 2
    halves = 2 if row_count % 16 == 0 else 1
    rows = row_count // halves
    block_rows = 2 * rows

    def half_of(block, h):
        return jnp.concatenate(
            [block[c * row_count + h * rows : c * row_count + (h + 1) * rows] for c in (0, 1)], axis=0
        )

    own_block = chip_block(ring, core, residual[0])
    gathered, steps = [], []
    for h in range(halves):
        parts, behind = gather(ring, core, half_of(own_block, h))
        gathered.append(parts)
        steps.append(behind)
    first = steps[0][0]
    targets, b_enc, w_dec_later, block_mask = after((targets, b_enc, w_dec, block_mask), first)

    goal = lax.ppermute(targets[0], "layer", [(i, (i - 1) % layers) for i in range(layers)])
    goal_block = chip_block(ring, core, goal)
    row_norms = jnp.sqrt(jnp.sum(jnp.square(w_dec_later[0].astype(f32)), axis=1) + norm_epsilon)
    owner = jnp.asarray(ring.owners)[device]
    mask_columns = jnp.repeat(block_mask[0].astype(f32), FBLOCK, axis=1)
    encoder = w_enc[0]
    decoder = w_dec[0]
    bias = b_enc[0][None, :]

    acts, gates, shares, act_sum = [], [], [], None
    for h in range(halves):
        token = (owner[:, None] * row_count + h * rows + jnp.arange(rows)[None, :]).reshape(-1)
        token_block = token // TBLOCK
        keep = jnp.zeros((token.shape[0], mask_columns.shape[1]), f32)
        for b in range(mask_columns.shape[0]):
            keep = jnp.where((token_block == b)[:, None], mask_columns[b][None, :], keep)
        act, gate, half_sum, share = forward(gathered[h], encoder, bias, keep, decoder)
        acts.append(act)
        gates.append(gate)
        shares.append(share)
        act_sum = half_sum if act_sum is None else act_sum + half_sum
    act_sum = act_sum[0]
    penalty = jnp.sum(act_sum * row_norms)
    penalty_chip = penalty + ring.across(penalty)
    errors, turned_rows = [], []
    loss_part = penalty_weight * penalty_chip
    for h in range(halves):
        recon, states = scatter_sum(ring, block_rows, *shares[h])
        turned_rows.append(turned(after(gathered[h], states[-1])))
        misfit = recon - half_of(goal_block, h).astype(f32)
        loss_part = loss_part + 0.5 * jnp.sum(misfit * misfit)
        payload = misfit.astype(bf16)
        if h == halves - 1:
            three = jnp.stack(split_three(loss_part))
            tail = jnp.broadcast_to(jnp.pad(three, (0, PAD - 3))[None, :], (block_rows, PAD))
            payload = jnp.concatenate([payload, tail], axis=1)
        errors.append(gather(ring, core, payload)[0])
    loss_sum = sum(
        jnp.sum(piece[::block_rows, width : width + 3].astype(f32)) for piece in errors[-1]
    )
    whole = loss_sum
    for _ in range(layers - 1):
        loss_sum = lax.ppermute(
            loss_sum, "layer", [(i, (i + 1) % layers) for i in range(layers)]
        )
        whole = whole + loss_sum
    loss = whole / (layers * tokens * width)

    coef = (penalty_weight * act_sum / row_norms)[:, None]
    enc_grad, bias_grad, dec_grad = backward(
        errors, acts, gates, turned_rows, decoder, row_norms[None, :], coef
    )
    return enc_grad[None], bias_grad, dec_grad[None], loss


def solution(mesh):
    return jax.shard_map(
        body,
        mesh=mesh,
        in_specs=(
            P("layer", "feat", None),
            P("layer", "feat", None),
            P("layer", None, "feat"),
            P("layer", "feat"),
            P("layer", "feat", None),
            P("layer", None, "feat"),
        ),
        out_specs=(P("layer", None, "feat"), P("layer", "feat"), P("layer", "feat", None), P()),
        check_vma=False,
    )
```

time: 137 us -> 123 us (0.90)
  matrix products: 19.4 us -> 0 us
  Pallas kernels: 0 us -> 11.7 us
  waiting for transfers between devices: 25.8 us -> 19.6 us
  other arithmetic: 18.6 us -> 21.7 us
  starting transfers between devices: 50.1 us -> 48 us
  local copies, waits for them, and re-layouts: 14.7 us -> 13.2 us
    dot_general x8 -> x0, matrix products: 19.4 us -> none  [the longest x2 8.24 us: contract_rows(): lax.dot_general(left, right, (((0,), (0,)), ((), ())), preferred_element_...]
    pallas_call x0 -> x5, Pallas kernels: none -> 11.7 us  [the longest x1 6.6 us: backward(): pl.pallas_call(functools.partial(backward_kernel, tuple((len(e) for e in...]
    ppermute x18, waiting for transfers between devices: 24.3 us -> 17.6 us  [along(): return lax.ppermute(block, 'feat', self.step)]
    ppermute x17 -> x15, starting transfers between devices: 20.4 us -> 14.6 us  [across(): return lax.ppermute(block, 'feat', self.twin)]
    slice x8 -> x2, local copies, waits for them, and re-layouts: 5.19 us -> 0.06 us  [body(): piece[::block_rows, width:width + 3].astype(f32)]
    ppermute x18, starting transfers between devices: 20.6 us -> 24.2 us  [along(): return lax.ppermute(block, 'feat', self.step)]
    reduce_sum x5 -> x7, other arithmetic: 5.01 us -> 7.92 us  [the longest x1 3.08 us: body(): jnp.sum(jnp.square(w_dec_later[0].astype(f32)), axis=1) + norm_epsilon]
    convert_element_type x6, other arithmetic: 3.13 us -> 5.98 us  [scatter_sum(): arrived = ring.along(total.astype(bf16))]
  transfers between devices with their start and end apart: 43 -> 41, of which waited for: 16 -> 20; matrix products, arithmetic and copies ran while one was open for 25% -> 17% of each run, Pallas kernels for 0% -> 10%
where the time goes in v2:
time: 123 us; the launch traced here: 122 us
  starting transfers between devices  48 us (39%)
  other arithmetic  21.7 us (18%)
  waiting for transfers between devices  19.6 us (16%)
  local copies, waits for them, and re-layouts  13.2 us (11%)
  Pallas kernels  11.7 us (10%)
  between operations  8.01 us (7%)
    ppermute x18, starting transfers between devices, along(): return lax.ppermute(block, 'feat', self.step)  24.2 us
    ppermute x18, waiting for transfers between devices, along(): return lax.ppermute(block, 'feat', self.step)  17.6 us
    ppermute x15, starting transfers between devices, across(): return lax.ppermute(block, 'feat', self.twin)  14.6 us
    unnamed x50, local copies, waits for them, and re-layouts  11.3 us
    pallas_call x1, Pallas kernels, backward(): pl.pallas_call(functools.partial(backward_kernel, tuple((len(e) for e in...  6.6 us
    convert_element_type x6, other arithmetic, scatter_sum(): arrived = ring.along(total.astype(bf16))  5.98 us
    pallas_call x2, Pallas kernels, forward(): pl.pallas_call(functools.partial(forward_kernel, len(pieces), min(512, wi...  4.43 us
    ppermute x6, starting transfers between devices, along_far(): return lax.ppermute(block, 'feat', self.far_step)  4.15 us
  transfers between devices with their start and end apart: 41, of which 20 were waited for; matrix products, arithmetic and copies ran while one was open for 17% of the time, Pallas kernels for 10%

profile of v2, /device:TPU:0, one launch (start us, length us, event | category | flops | bytes accessed | tf_op | source)
XLA Modules:
  0.0 122.2 jit_solution(17109953043091720893)
XLA Ops:
  3.9 2.7 %collective-permute-start.1 = (bf16[16,4096]{1,0:T(8,128)(2,1)S(1)}, bf16[16,4096]{1,0:T(8,128)(2,1)S(1)}, u32[]{:S(2)}, u32[]{:S(2)}) collective-permute-start(bf16[16,4096]{1,0:T(8,128)(2,1)S(1)} %pad_maximum_fusion.1.refs_0_), channel_id=1, source_target_pairs={{0,4},{1,3},{2,0},{3,7},{4,8},{5,1},{6,2},{7,11},{8,12},{9,5},{10,... | collective-permute-start | bytes 393224 | tf_op jit(solution)/shard_map/ppermute | solution.py:48
  6.6 1.6 %collective-permute-start.21 = (bf16[16,4096]{1,0:T(8,128)(2,1)S(1)}, bf16[16,4096]{1,0:T(8,128)(2,1)S(1)}, u32[]{:S(2)}, u32[]{:S(2)}) collective-permute-start(bf16[16,4096]{1,0:T(8,128)(2,1)S(1)} %pad_maximum_fusion.3.refs_0_), channel_id=1, source_target_pairs={{0,4},{1,3},{2,0},{3,7},{4,8},{5,1},{6,2},{7,11},{8,12},{9,5},{10,... | collective-permute-start | bytes 393224 | tf_op jit(solution)/shard_map/ppermute | solution.py:48
  10.2 3.1 %multiply_reduce_fusion = f32[512]{0:T(512)S(1)} fusion(bf16[1,512,4096]{2,1,0:T(8,128)(2,1)} %param.11), kind=kLoop, calls=%fused_computation | loop fusion | flops 6290944 | bytes 4196352 | tf_op jit(solution)/shard_map/reduce_sum | solution.py:316
  13.4 2.1 %collective-permute-start.13 = (bf16[16,4096]{1,0:T(8,128)(2,1)S(1)}, bf16[16,4096]{1,0:T(8,128)(2,1)S(1)}, u32[]{:S(2)}, u32[]{:S(2)}) collective-permute-start(bf16[16,4096]{1,0:T(8,128)(2,1)S(1)} %bitcast.37), channel_id=1, source_target_pairs={{0,16},{16,0},{1,17},{17,1},{2,18},{18,2},{3,19},{19,3},{4,20},{20... | collective-permute-start | bytes 393224 | tf_op jit(solution)/shard_map/ppermute | solution.py:314
  17.1 1.6 %collective-permute-start.22 = (bf16[16,4096]{1,0:T(8,128)(2,1)S(1)}, bf16[16,4096]{1,0:T(8,128)(2,1)S(1)}, u32[]{:S(2)}, u32[]{:S(2)}) collective-permute-start(bf16[16,4096]{1,0:T(8,128)(2,1)S(1)} %collective-permute-done.21), channel_id=1, source_target_pairs={{0,4},{1,3},{2,0},{3,7},{4,8},{5,1},{6,2},{7,11},{8,12},{9,5},{10,... | collective-permute-start | bytes 393224 | tf_op jit(solution)/shard_map/ppermute | solution.py:48
  22.2 1.6 %collective-permute-start.23 = (bf16[16,4096]{1,0:T(8,128)(2,1)S(1)}, bf16[16,4096]{1,0:T(8,128)(2,1)S(1)}, u32[]{:S(2)}, u32[]{:S(2)}) collective-permute-start(bf16[16,4096]{1,0:T(8,128)(2,1)S(1)} %collective-permute-done.22), channel_id=1, source_target_pairs={{0,4},{1,3},{2,0},{3,7},{4,8},{5,1},{6,2},{7,11},{8,12},{9,5},{10,... | collective-permute-start | bytes 393224 | tf_op jit(solution)/shard_map/ppermute | solution.py:48
  27.8 2.2 %collective-permute-start.6 = (bf16[16,4096]{1,0:T(8,128)(2,1)S(1)}, bf16[16,4096]{1,0:T(8,128)(2,1)S(1)}, u32[]{:S(2)}, u32[]{:S(2)}) collective-permute-start(bf16[16,4096]{1,0:T(8,128)(2,1)S(1)} %collective-permute-done.5), channel_id=1, source_target_pairs={{0,1},{1,0},{2,3},{3,2},{4,5},{5,4},{6,7},{7,6},{8,9},{9,8},{10,11... | collective-permute-start | bytes 393224 | tf_op jit(solution)/shard_map/ppermute | solution.py:54
  30.1 2.3 %collective-permute-start.26 = (bf16[16,4096]{1,0:T(8,128)(2,1)S(1)}, bf16[16,4096]{1,0:T(8,128)(2,1)S(1)}, u32[]{:S(2)}, u32[]{:S(2)}) collective-permute-start(bf16[16,4096]{1,0:T(8,128)(2,1)S(1)} %collective-permute-done.25), channel_id=1, source_target_pairs={{0,1},{1,0},{2,3},{3,2},{4,5},{5,4},{6,7},{7,6},{8,9},{9,8},{10,11... | collective-permute-start | bytes 393224 | tf_op jit(solution)/shard_map/ppermute | solution.py:54
  33.4 2.2 %shard_map.102 = (bf16[128,512]{1,0:T(8,128)(2,1)S(1)}, f32[128,512]{1,0:T(8,128)S(1)}, f32[1,512]{1,0:T(1,128)S(1)}, f32[16,4096]{1,0:T(8,128)S(1)}, bf16[64,40...) custom-call(bf16[16,4096]{1,0:T(8,128)(2,1)S(1)} %pad_maximum_fusion.1.refs_0_, ...), custom_call_target="tpu_custom_call" | custom-call | flops 1073741824 | bytes 1048576 | tf_op jit(solution)/shard_map/pallas_call | solution.py:167
  37.1 2.2 %shard_map.103 = (bf16[128,512]{1,0:T(8,128)(2,1)S(1)}, f32[128,512]{1,0:T(8,128)S(1)}, f32[1,512]{1,0:T(1,128)S(1)}, f32[16,4096]{1,0:T(8,128)S(1)}, bf16[64,40...) custom-call(bf16[16,4096]{1,0:T(8,128)(2,1)S(1)} %pad_maximum_fusion.3.refs_0_, ...), custom_call_target="tpu_custom_call" | custom-call | flops 1073741824 | bytes 1048576 | tf_op jit(solution)/shard_map/pallas_call | solution.py:167
  52.8 1.6 %collective-permute-start.29 = (bf16[16,4096]{1,0:T(8,128)(2,1)S(1)}, bf16[16,4096]{1,0:T(8,128)(2,1)S(1)}, u32[]{:S(2)}, u32[]{:S(2)}) collective-permute-start(bf16[16,4096]{1,0:T(8,128)(2,1)S(1)} %add_convert_fusion.3), channel_id=1, source_target_pairs={{0,4},{1,3},{2,0},{3,7},{4,8},{5,1},{6,2},{7,11},{8,12},{9,5},{10,... | collective-permute-start | bytes 393224 | tf_op jit(solution)/shard_map/ppermute | solution.py:48
  58.8 1.6 %collective-permute-start.30 = (bf16[16,4096]{1,0:T(8,128)(2,1)S(1)}, bf16[16,4096]{1,0:T(8,128)(2,1)S(1)}, u32[]{:S(2)}, u32[]{:S(2)}) collective-permute-start(bf16[16,4096]{1,0:T(8,128)(2,1)S(1)} %add_convert_fusion.2), channel_id=1, source_target_pairs={{0,4},{1,3},{2,0},{3,7},{4,8},{5,1},{6,2},{7,11},{8,12},{9,5},{10,... | collective-permute-start | bytes 393224 | tf_op jit(solution)/shard_map/ppermute | solution.py:48
  64.9 1.6 %collective-permute-start.31 = (bf16[16,4096]{1,0:T(8,128)(2,1)S(1)}, bf16[16,4096]{1,0:T(8,128)(2,1)S(1)}, u32[]{:S(2)}, u32[]{:S(2)}) collective-permute-start(bf16[16,4096]{1,0:T(8,128)(2,1)S(1)} %add_convert_fusion.1), channel_id=1, source_target_pairs={{0,4},{1,3},{2,0},{3,7},{4,8},{5,1},{6,2},{7,11},{8,12},{9,5},{10,... | collective-permute-start | bytes 393224 | tf_op jit(solution)/shard_map/ppermute | solution.py:48
  67.1 2.7 %collective-permute-start.12 = (bf16[16,4096]{1,0:T(8,128)(2,1)S(1)}, bf16[16,4096]{1,0:T(8,128)(2,1)S(1)}, u32[]{:S(2)}, u32[]{:S(2)}) collective-permute-start(bf16[16,4096]{1,0:T(8,128)(2,1)S(1)} %add_convert_fusion.5), channel_id=1, source_target_pairs={{0,1},{1,0},{2,3},{3,2},{4,5},{5,4},{6,7},{7,6},{8,9},{9,8},{10,11... | collective-permute-start | bytes 393224 | tf_op jit(solution)/shard_map/ppermute | solution.py:54
  70.6 2.6 %collective-permute-start.32 = (bf16[16,4096]{1,0:T(8,128)(2,1)}, bf16[16,4096]{1,0:T(8,128)(2,1)}, u32[]{:S(2)}, u32[]{:S(2)}) collective-permute-start(bf16[16,4096]{1,0:T(8,128)(2,1)} %add_convert_fusion), channel_id=1, source_target_pairs={{0,1},{1,0},{2,3},{3,2},{4,5},{5,4},{6,7},{7,6},{8,9},{9,8},{10,11... | collective-permute-start | bytes 393224 | tf_op jit(solution)/shard_map/ppermute | solution.py:54
  76.1 1.7 %multiply_reduce_fusion.1 = (f32[]{:T(128)}, bf16[16,4096]{1,0:T(8,128)(2,1)S(1)}) fusion(bf16[16,4096]{1,0:T(8,128)(2,1)} %collective-permute-done.32, bf16[16,4096]{1,0:T(8,128)(2,1)} %add_convert_fusion, bf16[8,4096]{1,0:T(8,128)(2,1)} %get-tuple-element.80, bf16[8,4096]{1,0:T(8,128)(2,1)} %get-tuple-element.78), kind=kLoop, calls=%fused_computation.1 | loop fusion | flops 720895 | bytes 524292 | tf_op jit(solution)/shard_map/reduce_sum | solution.py:344
  79.6 1.6 %collective-permute-start.34 = (bf16[16,4224]{1,0:T(8,128)(2,1)S(1)}, bf16[16,4224]{1,0:T(8,128)(2,1)S(1)}, u32[]{:S(2)}, u32[]{:S(2)}) collective-permute-start(bf16[16,4224]{1,0:T(8,128)(2,1)S(1)} %pad_maximum_fusion.refs_4_), channel_id=1, source_target_pairs={{0,4},{1,3},{2,0},{3,7},{4,8},{5,1},{6,2},{7,11},{8,12},{9,5},{10,... | collective-permute-start | bytes 405512 | tf_op jit(solution)/shard_map/ppermute | solution.py:48
  81.2 2.9 %collective-permute-done.15 = bf16[16,4096]{1,0:T(8,128)(2,1)S(1)} collective-permute-done((bf16[16,4096]{1,0:T(8,128)(2,1)S(1)}, bf16[16,4096]{1,0:T(8,128)(2,1)S(1)}, u32[]{:S(2)}, u32[]{:S(2)}) %collective-permute-start.15) | collective-permute-done | bytes 131104 | tf_op jit(solution)/shard_map/ppermute | solution.py:48
  86.2 2.9 %collective-permute-done.16 = bf16[16,4096]{1,0:T(8,128)(2,1)S(1)} collective-permute-done((bf16[16,4096]{1,0:T(8,128)(2,1)S(1)}, bf16[16,4096]{1,0:T(8,128)(2,1)S(1)}, u32[]{:S(2)}, u32[]{:S(2)}) %collective-permute-start.16) | collective-permute-done | bytes 131104 | tf_op jit(solution)/shard_map/ppermute | solution.py:48
  91.2 2.8 %collective-permute-done.17 = bf16[16,4096]{1,0:T(8,128)(2,1)S(1)} collective-permute-done((bf16[16,4096]{1,0:T(8,128)(2,1)S(1)}, bf16[16,4096]{1,0:T(8,128)(2,1)S(1)}, u32[]{:S(2)}, u32[]{:S(2)}) %collective-permute-start.17) | collective-permute-done | bytes 131104 | tf_op jit(solution)/shard_map/ppermute | solution.py:48
  96.5 2.0 %collective-permute-start.20 = (bf16[16,4096]{1,0:T(8,128)(2,1)S(1)}, bf16[16,4096]{1,0:T(8,128)(2,1)}, u32[]{:S(2)}, u32[]{:S(2)}) collective-permute-start(bf16[16,4096]{1,0:T(8,128)(2,1)S(1)} %collective-permute-done.19), channel_id=1, source_target_pairs={{0,1},{1,0},{2,3},{3,2},{4,5},{5,4},{6,7},{7,6},{8,9},{9,8},{10,11... | collective-permute-start | bytes 393224 | tf_op jit(solution)/shard_map/ppermute | solution.py:54
  104.6 3.0 %collective-permute-start.40 = (f32[]{:T(128)}, f32[]{:T(128)}, u32[]{:S(2)}, u32[]{:S(2)}) collective-permute-start(f32[]{:T(128)} %add.220), channel_id=1, source_target_pairs={{0,16},{16,0},{1,17},{17,1},{2,18},{18,2},{3,19},{19,3},{4,20},{20... | collective-permute-start | bytes 20 | tf_op jit(solution)/shard_map/ppermute | solution.py:356
  107.6 2.2 %copy-done.1 = bf16[1,512,4096]{2,1,0:T(8,128)(2,1)S(1)} copy-done((bf16[1,512,4096]{2,1,0:T(8,128)(2,1)S(1)}, bf16[1,512,4096]{2,1,0:T(8,128)(2,1)}, u32[]{:S(2)}) %copy-start.1) | copy-done | bytes 4194328
  113.8 6.6 %shard_map.106 = (bf16[4096,512]{1,0:T(8,128)(2,1)}, f32[1,512]{1,0:T(1,128)}, bf16[512,4096]{1,0:T(8,128)(2,1)}) custom-call(bf16[16,4096]{1,0:T(8,128)(2,1)S(1)} %get-tuple-element.73.refs_0_, bf16[48,4096]{1,0:T(8,128)(2,1)S(1)} %constant_dynamic-update-slice_fusion.3.refs_1_, bf16[48,4096]{1,0:T(8,128)(2,1)} %collective-permute-done.18.refs_2_, ...), custom_call_target="tpu_custom_call" | custom-call | flops 3221225472 | bytes 8388608 | tf_op jit(solution)/shard_map/pallas_call | solution.py:259
  (167 shorter events, 56.9 us)
Async XLA Ops:
  3.9 5.5 %collective-permute-start.1 = (bf16[16,4096]{1,0:T(8,128)(2,1)S(1)}, bf16[16,4096]{1,0:T(8,128)(2,1)S(1)}, u32[]{:S(2)}, u32[]{:S(2)}) collective-permute-start(bf16[16,4096]{1,0:T(8,128)(2,1)S(1)} %pad_maximum_fusion.1.refs_0_), channel_id=1, source_target_pairs={{0,4},{1,3},{2,0},{3,7},{4,8},{5,1},{6,2},{7,11},{8,12},{9,5},{10,... | collective-permute-start | bytes 393224 | tf_op jit(solution)/shard_map/ppermute | solution.py:48
  6.6 10.5 %collective-permute-start.21 = (bf16[16,4096]{1,0:T(8,128)(2,1)S(1)}, bf16[16,4096]{1,0:T(8,128)(2,1)S(1)}, u32[]{:S(2)}, u32[]{:S(2)}) collective-permute-start(bf16[16,4096]{1,0:T(8,128)(2,1)S(1)} %pad_maximum_fusion.3.refs_0_), channel_id=1, source_target_pairs={{0,4},{1,3},{2,0},{3,7},{4,8},{5,1},{6,2},{7,11},{8,12},{9,5},{10,... | collective-permute-start | bytes 393224 | tf_op jit(solution)/shard_map/ppermute | solution.py:48
  13.4 5.5 %collective-permute-start.13 = (bf16[16,4096]{1,0:T(8,128)(2,1)S(1)}, bf16[16,4096]{1,0:T(8,128)(2,1)S(1)}, u32[]{:S(2)}, u32[]{:S(2)}) collective-permute-start(bf16[16,4096]{1,0:T(8,128)(2,1)S(1)} %bitcast.37), channel_id=1, source_target_pairs={{0,16},{16,0},{1,17},{17,1},{2,18},{18,2},{3,19},{19,3},{4,20},{20... | collective-permute-start | bytes 393224 | tf_op jit(solution)/shard_map/ppermute | solution.py:314
  17.1 5.0 %collective-permute-start.22 = (bf16[16,4096]{1,0:T(8,128)(2,1)S(1)}, bf16[16,4096]{1,0:T(8,128)(2,1)S(1)}, u32[]{:S(2)}, u32[]{:S(2)}) collective-permute-start(bf16[16,4096]{1,0:T(8,128)(2,1)S(1)} %collective-permute-done.21), channel_id=1, source_target_pairs={{0,4},{1,3},{2,0},{3,7},{4,8},{5,1},{6,2},{7,11},{8,12},{9,5},{10,... | collective-permute-start | bytes 393224 | tf_op jit(solution)/shard_map/ppermute | solution.py:48
  22.2 5.0 %collective-permute-start.23 = (bf16[16,4096]{1,0:T(8,128)(2,1)S(1)}, bf16[16,4096]{1,0:T(8,128)(2,1)S(1)}, u32[]{:S(2)}, u32[]{:S(2)}) collective-permute-start(bf16[16,4096]{1,0:T(8,128)(2,1)S(1)} %collective-permute-done.22), channel_id=1, source_target_pairs={{0,4},{1,3},{2,0},{3,7},{4,8},{5,1},{6,2},{7,11},{8,12},{9,5},{10,... | collective-permute-start | bytes 393224 | tf_op jit(solution)/shard_map/ppermute | solution.py:48
  26.0 7.4 %collective-permute-start.4 = (bf16[48,4096]{1,0:T(8,128)(2,1)S(1)}, bf16[48,4096]{1,0:T(8,128)(2,1)S(1)}, u32[]{:S(2)}, u32[]{:S(2)}) collective-permute-start(bf16[48,4096]{1,0:T(8,128)(2,1)S(1)} %constant_dynamic-update-slice_fusion.refs_1_), channel_id=1, source_target_pairs={{0,1},{1,0},{2,3},{3,2},{4,5},{5,4},{6,7},{7,6},{8,9},{9,8},{10,11... | collective-permute-start | bytes 1179656 | tf_op jit(solution)/shard_map/ppermute | solution.py:54
  30.0 6.7 %collective-permute-start.24 = (bf16[48,4096]{1,0:T(8,128)(2,1)S(1)}, bf16[48,4096]{1,0:T(8,128)(2,1)S(1)}, u32[]{:S(2)}, u32[]{:S(2)}) collective-permute-start(bf16[48,4096]{1,0:T(8,128)(2,1)S(1)} %constant_dynamic-update-slice_fusion.6.refs_1_), channel_id=1, source_target_pairs={{0,1},{1,0},{2,3},{3,2},{4,5},{5,4},{6,7},{7,6},{8,9},{9,8},{10,11... | collective-permute-start | bytes 1179656 | tf_op jit(solution)/shard_map/ppermute | solution.py:54
  36.4 9.4 %collective-permute-start.7 = (bf16[64,4096]{1,0:T(8,128)(2,1)}, bf16[64,4096]{1,0:T(8,128)(2,1)}, u32[]{:S(2)}, u32[]{:S(2)}) collective-permute-start(bf16[64,4096]{1,0:T(8,128)(2,1)} %get-tuple-element.37), channel_id=1, source_target_pairs={{0,1},{1,0},{2,3},{3,2},{4,5},{5,4},{6,7},{7,6},{8,9},{9,8},{10,11... | collective-permute-start | bytes 1572872 | tf_op jit(solution)/shard_map/ppermute | solution.py:54
  42.2 5.3 %collective-permute-start.27 = (bf16[64,4096]{1,0:T(8,128)(2,1)}, bf16[64,4096]{1,0:T(8,128)(2,1)}, u32[]{:S(2)}, u32[]{:S(2)}) collective-permute-start(bf16[64,4096]{1,0:T(8,128)(2,1)} %get-tuple-element.42), channel_id=1, source_target_pairs={{0,1},{1,0},{2,3},{3,2},{4,5},{5,4},{6,7},{7,6},{8,9},{9,8},{10,11... | collective-permute-start | bytes 1572872 | tf_op jit(solution)/shard_map/ppermute | solution.py:54
  50.1 5.0 %collective-permute-start.9 = (bf16[16,4096]{1,0:T(8,128)(2,1)S(1)}, bf16[16,4096]{1,0:T(8,128)(2,1)S(1)}, u32[]{:S(2)}, u32[]{:S(2)}) collective-permute-start(bf16[16,4096]{1,0:T(8,128)(2,1)S(1)} %add_convert_fusion.8), channel_id=1, source_target_pairs={{0,4},{1,3},{2,0},{3,7},{4,8},{5,1},{6,2},{7,11},{8,12},{9,5},{10,... | collective-permute-start | bytes 393224 | tf_op jit(solution)/shard_map/ppermute | solution.py:48
  52.8 5.0 %collective-permute-start.29 = (bf16[16,4096]{1,0:T(8,128)(2,1)S(1)}, bf16[16,4096]{1,0:T(8,128)(2,1)S(1)}, u32[]{:S(2)}, u32[]{:S(2)}) collective-permute-start(bf16[16,4096]{1,0:T(8,128)(2,1)S(1)} %add_convert_fusion.3), channel_id=1, source_target_pairs={{0,4},{1,3},{2,0},{3,7},{4,8},{5,1},{6,2},{7,11},{8,12},{9,5},{10,... | collective-permute-start | bytes 393224 | tf_op jit(solution)/shard_map/ppermute | solution.py:48
  56.1 5.0 %collective-permute-start.10 = (bf16[16,4096]{1,0:T(8,128)(2,1)S(1)}, bf16[16,4096]{1,0:T(8,128)(2,1)S(1)}, u32[]{:S(2)}, u32[]{:S(2)}) collective-permute-start(bf16[16,4096]{1,0:T(8,128)(2,1)S(1)} %add_convert_fusion.7), channel_id=1, source_target_pairs={{0,4},{1,3},{2,0},{3,7},{4,8},{5,1},{6,2},{7,11},{8,12},{9,5},{10,... | collective-permute-start | bytes 393224 | tf_op jit(solution)/shard_map/ppermute | solution.py:48
  58.8 5.0 %collective-permute-start.30 = (bf16[16,4096]{1,0:T(8,128)(2,1)S(1)}, bf16[16,4096]{1,0:T(8,128)(2,1)S(1)}, u32[]{:S(2)}, u32[]{:S(2)}) collective-permute-start(bf16[16,4096]{1,0:T(8,128)(2,1)S(1)} %add_convert_fusion.2), channel_id=1, source_target_pairs={{0,4},{1,3},{2,0},{3,7},{4,8},{5,1},{6,2},{7,11},{8,12},{9,5},{10,... | collective-permute-start | bytes 393224 | tf_op jit(solution)/shard_map/ppermute | solution.py:48
  62.1 5.0 %collective-permute-start.11 = (bf16[16,4096]{1,0:T(8,128)(2,1)S(1)}, bf16[16,4096]{1,0:T(8,128)(2,1)S(1)}, u32[]{:S(2)}, u32[]{:S(2)}) collective-permute-start(bf16[16,4096]{1,0:T(8,128)(2,1)S(1)} %add_convert_fusion.6), channel_id=1, source_target_pairs={{0,4},{1,3},{2,0},{3,7},{4,8},{5,1},{6,2},{7,11},{8,12},{9,5},{10,... | collective-permute-start | bytes 393224 | tf_op jit(solution)/shard_map/ppermute | solution.py:48
  64.9 5.0 %collective-permute-start.31 = (bf16[16,4096]{1,0:T(8,128)(2,1)S(1)}, bf16[16,4096]{1,0:T(8,128)(2,1)S(1)}, u32[]{:S(2)}, u32[]{:S(2)}) collective-permute-start(bf16[16,4096]{1,0:T(8,128)(2,1)S(1)} %add_convert_fusion.1), channel_id=1, source_target_pairs={{0,4},{1,3},{2,0},{3,7},{4,8},{5,1},{6,2},{7,11},{8,12},{9,5},{10,... | collective-permute-start | bytes 393224 | tf_op jit(solution)/shard_map/ppermute | solution.py:48
  67.1 7.6 %collective-permute-start.12 = (bf16[16,4096]{1,0:T(8,128)(2,1)S(1)}, bf16[16,4096]{1,0:T(8,128)(2,1)S(1)}, u32[]{:S(2)}, u32[]{:S(2)}) collective-permute-start(bf16[16,4096]{1,0:T(8,128)(2,1)S(1)} %add_convert_fusion.5), channel_id=1, source_target_pairs={{0,1},{1,0},{2,3},{3,2},{4,5},{5,4},{6,7},{7,6},{8,9},{9,8},{10,11... | collective-permute-start | bytes 393224 | tf_op jit(solution)/shard_map/ppermute | solution.py:54
  70.6 5.5 %collective-permute-start.32 = (bf16[16,4096]{1,0:T(8,128)(2,1)}, bf16[16,4096]{1,0:T(8,128)(2,1)}, u32[]{:S(2)}, u32[]{:S(2)}) collective-permute-start(bf16[16,4096]{1,0:T(8,128)(2,1)} %add_convert_fusion), channel_id=1, source_target_pairs={{0,1},{1,0},{2,3},{3,2},{4,5},{5,4},{6,7},{7,6},{8,9},{9,8},{10,11... | collective-permute-start | bytes 393224 | tf_op jit(solution)/shard_map/ppermute | solution.py:54
  79.2 5.0 %collective-permute-start.15 = (bf16[16,4096]{1,0:T(8,128)(2,1)S(1)}, bf16[16,4096]{1,0:T(8,128)(2,1)S(1)}, u32[]{:S(2)}, u32[]{:S(2)}) collective-permute-start(bf16[16,4096]{1,0:T(8,128)(2,1)S(1)} %get-tuple-element.73.refs_0_), channel_id=1, source_target_pairs={{0,4},{1,3},{2,0},{3,7},{4,8},{5,1},{6,2},{7,11},{8,12},{9,5},{10,... | collective-permute-start | bytes 393224 | tf_op jit(solution)/shard_map/ppermute | solution.py:48
  79.6 6.0 %collective-permute-start.34 = (bf16[16,4224]{1,0:T(8,128)(2,1)S(1)}, bf16[16,4224]{1,0:T(8,128)(2,1)S(1)}, u32[]{:S(2)}, u32[]{:S(2)}) collective-permute-start(bf16[16,4224]{1,0:T(8,128)(2,1)S(1)} %pad_maximum_fusion.refs_4_), channel_id=1, source_target_pairs={{0,4},{1,3},{2,0},{3,7},{4,8},{5,1},{6,2},{7,11},{8,12},{9,5},{10,... | collective-permute-start | bytes 405512 | tf_op jit(solution)/shard_map/ppermute | solution.py:48
  84.1 5.0 %collective-permute-start.16 = (bf16[16,4096]{1,0:T(8,128)(2,1)S(1)}, bf16[16,4096]{1,0:T(8,128)(2,1)S(1)}, u32[]{:S(2)}, u32[]{:S(2)}) collective-permute-start(bf16[16,4096]{1,0:T(8,128)(2,1)S(1)} %collective-permute-done.15), channel_id=1, source_target_pairs={{0,4},{1,3},{2,0},{3,7},{4,8},{5,1},{6,2},{7,11},{8,12},{9,5},{10,... | collective-permute-start | bytes 393224 | tf_op jit(solution)/shard_map/ppermute | solution.py:48
  85.6 5.0 %collective-permute-start.35 = (bf16[16,4224]{1,0:T(8,128)(2,1)S(1)}, bf16[16,4224]{1,0:T(8,128)(2,1)S(1)}, u32[]{:S(2)}, u32[]{:S(2)}) collective-permute-start(bf16[16,4224]{1,0:T(8,128)(2,1)S(1)} %collective-permute-done.34), channel_id=1, source_target_pairs={{0,4},{1,3},{2,0},{3,7},{4,8},{5,1},{6,2},{7,11},{8,12},{9,5},{10,... | collective-permute-start | bytes 405512 | tf_op jit(solution)/shard_map/ppermute | solution.py:48
  90.6 5.0 %collective-permute-start.36 = (bf16[16,4224]{1,0:T(8,128)(2,1)S(1)}, bf16[16,4224]{1,0:T(8,128)(2,1)S(1)}, u32[]{:S(2)}, u32[]{:S(2)}) collective-permute-start(bf16[16,4224]{1,0:T(8,128)(2,1)S(1)} %collective-permute-done.35), channel_id=1, source_target_pairs={{0,4},{1,3},{2,0},{3,7},{4,8},{5,1},{6,2},{7,11},{8,12},{9,5},{10,... | collective-permute-start | bytes 405512 | tf_op jit(solution)/shard_map/ppermute | solution.py:48
  94.7 12.9 %collective-permute-start.18 = (bf16[48,4096]{1,0:T(8,128)(2,1)S(1)}, bf16[48,4096]{1,0:T(8,128)(2,1)}, u32[]{:S(2)}, u32[]{:S(2)}) collective-permute-start(bf16[48,4096]{1,0:T(8,128)(2,1)S(1)} %constant_dynamic-update-slice_fusion.3.refs_1_), channel_id=1, source_target_pairs={{0,1},{1,0},{2,3},{3,2},{4,5},{5,4},{6,7},{7,6},{8,9},{9,8},{10,11... | collective-permute-start | bytes 1179656 | tf_op jit(solution)/shard_map/ppermute | solution.py:54
  104.6 15.8 %collective-permute-start.40 = (f32[]{:T(128)}, f32[]{:T(128)}, u32[]{:S(2)}, u32[]{:S(2)}) collective-permute-start(f32[]{:T(128)} %add.220), channel_id=1, source_target_pairs={{0,16},{16,0},{1,17},{17,1},{2,18},{18,2},{3,19},{19,3},{4,20},{20... | collective-permute-start | bytes 20 | tf_op jit(solution)/shard_map/ppermute | solution.py:356
  (38 other events, 240.7 us)

commit v3 on v2

--- a/solution.py
+++ b/solution.py
@@ -20,23 +20,18 @@
 
 class Ring:
     def __init__(self, size):
-        self.size = size
         chips = size // 2
-        self.chips = chips
         self.hops = (chips - 1) // 2
         self.far = chips % 2 == 0
         order = list(range(0, chips, 2)) + list(range(1, chips, 2))[::-1]
         place = {chip: at for at, chip in enumerate(order)}
-        self.step, self.far_step = [], []
+        self.step = []
         owners = []
         for device in range(size):
             chip, core = divmod(device, 2)
             at = place[chip]
             ahead = 1 if core == 0 else -1
-            pair = (device, order[(at + ahead) % chips] * 2 + core)
-            self.step.append(pair)
-            if core == 1:
-                self.far_step.append(pair)
+            self.step.append((device, order[(at + ahead) % chips] * 2 + core))
             behind = [order[(at - ahead * k) % chips] for k in range(1, self.hops + 1)]
             front = [order[(at + ahead * k) % chips] for k in range(1, self.hops + 1)]
             last = [order[(at + self.hops + 1) % chips]] if self.far else []
@@ -47,49 +42,43 @@
     def along(self, block):
         return lax.ppermute(block, "feat", self.step)
 
-    def along_far(self, block):
-        return lax.ppermute(block, "feat", self.far_step)
-
     def across(self, block):
         return lax.ppermute(block, "feat", self.twin)
 
 
-def chip_block(ring, core, own):
-    other = ring.across(own)
-    return jnp.concatenate(
-        [jnp.where(core == 0, own, other), jnp.where(core == 0, other, own)], axis=0
-    )
-
-
 def after(values, signal):
     return lax.optimization_barrier((values, signal))[0]
 
 
-def gather(ring, core, block):
+def gather(ring, block):
     behind = []
     moving = block
     for _ in range(ring.hops):
         moving = ring.along(moving)
         behind.append(moving)
     parts = [block]
-    came = None
-    if ring.far:
-        came = ring.along_far(moving)
     if behind:
         stack = jnp.concatenate(behind, axis=0)
         parts += [stack, ring.across(stack)]
     if ring.far:
-        parts.append(jnp.where(core == 1, came, ring.across(came)))
+        parts.append(ring.along(moving))
     return parts, behind
 
 
-def scatter_sum(ring, rows, own, sent, front, last):
+def scatter_sum(ring, first_core, rows, own, sent, front, last):
     from_twin = ring.across(sent)
     arrived = None
     states = []
     if ring.far:
         total = last + from_twin[rows * ring.hops :].astype(f32)
-        arrived = ring.along_far(total.astype(bf16))
+        half = rows // 2
+        total = jnp.where(first_core, total[:half], total[half:])
+        half_sum = ring.along(total.astype(bf16))
+        states.append(half_sum)
+        nothing = jnp.zeros_like(half_sum)
+        arrived = jnp.concatenate(
+            [jnp.where(first_core, half_sum, nothing), jnp.where(first_core, nothing, half_sum)], axis=0
+        )
     for k in range(ring.hops, 0, -1):
         total = front[rows * (k - 1) : rows * k]
         total = total + from_twin[rows * (k - 1) : rows * k].astype(f32)
@@ -101,7 +90,14 @@
     if arrived is not None:
         total = total + arrived.astype(f32)
     mine = total.astype(bf16)
-    return mine.astype(f32) + ring.across(mine).astype(f32), states
+    return mine, ring.across(mine), states
+
+
+def chip_block(ring, first_core, own):
+    other = ring.across(own)
+    return jnp.concatenate(
+        [jnp.where(first_core, own, other), jnp.where(first_core, other, own)], axis=0
+    )
 
 
 def in_vmem(x):
@@ -124,9 +120,9 @@
 
 def forward_kernel(count, step, *refs):
     pieces = refs[:count]
-    enc_ref, bias_ref, keep_ref, dec_ref = refs[count : count + 4]
-    act_ref, gate_ref, sum_ref = refs[count + 4 : count + 7]
-    outs = refs[count + 7 :]
+    enc_ref, bias_ref, token_ref, mask_ref, dec_ref = refs[count : count + 5]
+    act_ref, gate_ref, sum_ref = refs[count + 5 : count + 8]
+    outs = refs[count + 8 :]
     width = dec_ref.shape[1]
     preact = jnp.zeros(gate_ref.shape, f32)
     for at in range(0, width, step):
@@ -134,7 +130,10 @@
             stacked(pieces, slice(at, at + step)), enc_ref[at : at + step, :], preferred_element_type=f32
         )
     positive = jnp.maximum(preact + bias_ref[...], 0.0)
-    keep = keep_ref[...]
+    token_block = token_ref[...]
+    keep = jnp.zeros(gate_ref.shape, f32)
+    for b in range(mask_ref.shape[0]):
+        keep = jnp.where(token_block == b, mask_ref[b : b + 1, :], keep)
     act = (keep * positive * positive).astype(bf16)
     act_ref[...] = act
     gate_ref[...] = keep * 2.0 * positive
@@ -153,9 +152,9 @@
         last_ref[:, at : at + step] = part[rows + 2 * hop :]
 
 
-def forward(parts, encoder, bias, keep, decoder):
+def forward(parts, encoder, bias, token_block, mask, decoder):
     pieces = whole_pieces(parts)
-    total, features = keep.shape
+    total, features = token_block.shape[0], mask.shape[1]
     width = decoder.shape[1]
     shapes = [((total, features), bf16), ((total, features), f32), ((1, features), f32)]
     if len(pieces) == 4:
@@ -167,11 +166,11 @@
     outs = pl.pallas_call(
         functools.partial(forward_kernel, len(pieces), min(512, width)),
         out_shape=[pltpu.VMEM(shape, dtype) for shape, dtype in shapes],
-        in_specs=[VMEM_SPEC] * (len(pieces) + 4),
+        in_specs=[VMEM_SPEC] * (len(pieces) + 5),
         out_specs=[VMEM_SPEC] * len(shapes),
         compiler_params=pltpu.CompilerParams(vmem_limit_bytes=12 << 20),
         cost_estimate=pl.CostEstimate(flops=flops, bytes_accessed=1 << 20, transcendentals=0),
-    )(*[in_vmem(x) for x in (*pieces, encoder, bias, keep, decoder)])
+    )(*[in_vmem(x) for x in (*pieces, encoder, bias, token_block, mask, decoder)])
     act, gate, act_sum = outs[:3]
     if len(outs) > 4:
         return act, gate, act_sum, outs[3:]
@@ -276,12 +275,89 @@
     )(*[in_vmem(x) for x in operands])
 
 
-def split_three(value):
-    high = value.astype(bf16)
-    rest = value - high.astype(f32)
-    middle = rest.astype(bf16)
-    low = (rest - middle.astype(f32)).astype(bf16)
-    return [high, middle, low]
+def norm_kernel(halves, step, *refs):
+    sums, dec_ref = refs[:halves], refs[halves]
+    norm_ref, coef_ref, penalty_ref = refs[halves + 1 :]
+    features, width = dec_ref.shape
+    partial = jnp.zeros((features, 128), f32)
+    for at in range(0, width, 128):
+        part = dec_ref[:, at : at + 128].astype(f32)
+        partial = partial + part * part
+    squares = jnp.sum(partial.T, axis=0, keepdims=True)
+    norm = jnp.sqrt(squares + norm_epsilon)
+    act_sum = functools.reduce(jnp.add, [r[...] for r in sums])
+    norm_ref[...] = norm
+    penalty_ref[...] = penalty_weight * act_sum * norm
+    coef = penalty_weight * act_sum / norm
+    coef_ref[...] = jnp.broadcast_to(coef, (8, features)).T[:, :1]
+
+
+def norms(sums, decoder):
+    features = decoder.shape[0]
+    return pl.pallas_call(
+        functools.partial(norm_kernel, len(sums), 128),
+        out_shape=[pltpu.VMEM(shape, f32) for shape in ((1, features), (features, 1), (1, features))],
+        in_specs=[VMEM_SPEC] * (len(sums) + 1),
+        out_specs=[VMEM_SPEC] * 3,
+        compiler_params=pltpu.CompilerParams(vmem_limit_bytes=8 << 20),
+        cost_estimate=pl.CostEstimate(flops=0, bytes_accessed=4 << 20, transcendentals=0),
+    )(*[in_vmem(x) for x in (*sums, decoder)])
+
+
+def misfit_kernel(carries_loss, *refs):
+    mine_ref, other_ref, goal_ref = refs[:3]
+    rest, out_ref = refs[3:-2], refs[-2]
+    width = mine_ref.shape[1]
+    misfit = mine_ref[...].astype(f32) + other_ref[...].astype(f32) - goal_ref[...].astype(f32)
+    loss = 0.5 * jnp.sum(misfit * misfit, keepdims=True)
+    for ref in rest:
+        loss = loss + jnp.sum(ref[...], keepdims=True)
+    refs[-1][...] = loss
+    out_ref[:, :width] = misfit.astype(bf16)
+    if carries_loss:
+        high = loss.astype(bf16).astype(f32)
+        middle = (loss - high).astype(bf16).astype(f32)
+        low = loss - high - middle
+        lane = lax.broadcasted_iota(jnp.int32, (out_ref.shape[0], PAD), 1)
+        tail = jnp.where(lane == 0, high, jnp.where(lane == 1, middle, jnp.where(lane == 2, low, 0.0)))
+        out_ref[:, width:] = tail.astype(bf16)
+
+
+def misfits(mine, other, goal, rest, carries_loss):
+    rows, width = mine.shape
+    operands = (mine, other, goal, *rest)
+    return pl.pallas_call(
+        functools.partial(misfit_kernel, carries_loss),
+        out_shape=[
+            pltpu.VMEM((rows, width + PAD if carries_loss else width), bf16),
+            pltpu.VMEM((1, 1), f32),
+        ],
+        in_specs=[VMEM_SPEC] * len(operands),
+        out_specs=[VMEM_SPEC] * 2,
+        compiler_params=pltpu.CompilerParams(vmem_limit_bytes=8 << 20),
+        cost_estimate=pl.CostEstimate(flops=0, bytes_accessed=1 << 20, transcendentals=0),
+    )(*[in_vmem(x) for x in operands])
+
+
+def loss_kernel(scale, *refs):
+    pieces, out_ref = refs[:-1], refs[-1]
+    total = jnp.zeros((1, 1), f32)
+    for ref in pieces:
+        tail = ref[:, ref.shape[1] - PAD :].astype(f32)
+        total = total + jnp.sum(tail, keepdims=True)
+    out_ref[...] = jnp.broadcast_to(total * scale, out_ref.shape)
+
+
+def group_loss(parts, block_rows):
+    pieces = whole_pieces(parts)
+    return pl.pallas_call(
+        functools.partial(loss_kernel, 1.0 / block_rows),
+        out_shape=pltpu.VMEM((8, PAD), f32),
+        in_specs=[VMEM_SPEC] * len(pieces),
+        out_specs=VMEM_SPEC,
+        compiler_params=pltpu.CompilerParams(vmem_limit_bytes=8 << 20),
+        cost_estimate=pl.CostEstimate(flops=0, bytes_accessed=1 << 16, transcendentals=0),
+    )(*[in_vmem(x) for x in pieces])
 
 
 def body(residual, targets, w_enc, b_enc, w_dec, block_mask):
@@ -292,7 +368,7 @@
     tokens = row_count * feats
     ring = Ring(feats)
     device = lax.axis_index("feat")
-    core = device % 2
+    first_core = device % 2 == 0
     halves = 2 if row_count % 16 == 0 else 1
     rows = row_count // halves
     block_rows = 2 * rows
@@ -302,67 +378,47 @@
             [block[c * row_count + h * rows : c * row_count + (h + 1) * rows] for c in (0, 1)], axis=0
         )
 
-    own_block = chip_block(ring, core, residual[0])
+    tokens_of = ring.owners[:, None, :, None] * row_count + np.arange(halves)[:, None, None] * rows + np.arange(rows)
+    table = (tokens_of // TBLOCK).reshape(feats, halves, -1, 1).astype(np.int32)
+    token_blocks = jnp.asarray(table)[device]
+
+    own_block = chip_block(ring, first_core, residual[0])
     gathered, steps = [], []
     for h in range(halves):
-        parts, behind = gather(ring, core, half_of(own_block, h))
+        parts, behind = gather(ring, half_of(own_block, h))
         gathered.append(parts)
         steps.append(behind)
-    first = steps[0][0]
-    targets, b_enc, w_dec_later, block_mask = after((targets, b_enc, w_dec, block_mask), first)
-
+    targets, b_enc, block_mask = after((targets, b_enc, block_mask), steps[0][0])
     goal = lax.ppermute(targets[0], "layer", [(i, (i - 1) % layers) for i in range(layers)])
-    goal_block = chip_block(ring, core, goal)
-    row_norms = jnp.sqrt(jnp.sum(jnp.square(w_dec_later[0].astype(f32)), axis=1) + norm_epsilon)
-    owner = jnp.asarray(ring.owners)[device]
-    mask_columns = jnp.repeat(block_mask[0].astype(f32), FBLOCK, axis=1)
+    goal_block = chip_block(ring, first_core, goal)
+    mask = jnp.repeat(block_mask[0].astype(f32), FBLOCK, axis=1)
     encoder = w_enc[0]
     decoder = w_dec[0]
-    bias = b_enc[0][None, :]
-
-    acts, gates, shares, act_sum = [], [], [], None
+
+    acts, gates, shares, sums = [], [], [], []
     for h in range(halves):
-        token = (owner[:, None] * row_count + h * rows + jnp.arange(rows)[None, :]).reshape(-1)
-        token_block = token // TBLOCK
-        keep = jnp.zeros((token.shape[0], mask_columns.shape[1]), f32)
-        for b in range(mask_columns.shape[0]):
-            keep = jnp.where((token_block == b)[:, None], mask_columns[b][None, :], keep)
-        act, gate, half_sum, share = forward(gathered[h], encoder, bias, keep, decoder)
+        act, gate, act_sum, share = forward(gathered[h], encoder, b_enc, token_blocks[h], mask, decoder)
         acts.append(act)
         gates.append(gate)
         shares.append(share)
-        act_sum = half_sum if act_sum is None else act_sum + half_sum
-    act_sum = act_sum[0]
-    penalty = jnp.sum(act_sum * row_norms)
-    penalty_chip = penalty + ring.across(penalty)
+        sums.append(act_sum)
+    summed = [scatter_sum(ring, first_core, block_rows, *share) for share in shares]
+    norm, coef, penalty = norms(sums, after(decoder, summed[0][2][0]))
+    rest = [penalty, ring.across(penalty)]
     errors, turned_rows = [], []
-    loss_part = penalty_weight * penalty_chip
     for h in range(halves):
-        recon, states = scatter_sum(ring, block_rows, *shares[h])
+        mine, other, states = summed[h]
         turned_rows.append(turned(after(gathered[h], states[-1])))
-        misfit = recon - half_of(goal_block, h).astype(f32)
-        loss_part = loss_part + 0.5 * jnp.sum(misfit * misfit)
-        payload = misfit.astype(bf16)
-        if h == halves - 1:
-            three = jnp.stack(split_three(loss_part))
-            tail = jnp.broadcast_to(jnp.pad(three, (0, PAD - 3))[None, :], (block_rows, PAD))
-            payload = jnp.concatenate([payload, tail], axis=1)
-        errors.append(gather(ring, core, payload)[0])
-    loss_sum = sum(
-        jnp.sum(piece[::block_rows, width : width + 3].astype(f32)) for piece in errors[-1]
-    )
-    whole = loss_sum
+        last = h == halves - 1
+        payload, half_loss = misfits(mine, other, half_of(goal_block, h), rest if last else [], last)
+        rest.append(half_loss)
+        errors.append(gather(ring, payload)[0])
+    sent_loss = loss_row = group_loss(errors[-1], block_rows)
     for _ in range(layers - 1):
-        loss_sum = lax.ppermute(
-            loss_sum, "layer", [(i, (i + 1) % layers) for i in range(layers)]
-        )
-        whole = whole + loss_sum
-    loss = whole / (layers * tokens * width)
-
-    coef = (penalty_weight * act_sum / row_norms)[:, None]
-    enc_grad, bias_grad, dec_grad = backward(
-        errors, acts, gates, turned_rows, decoder, row_norms[None, :], coef
-    )
+        sent_loss = lax.ppermute(sent_loss, "layer", [(i, (i + 1) % layers) for i in range(layers)])
+        loss_row = loss_row + sent_loss
+    enc_grad, bias_grad, dec_grad = backward(errors, acts, gates, turned_rows, decoder, norm, coef)
+    loss = after(loss_row, bias_grad)[0, 0] / (layers * tokens * width)
     return enc_grad[None], bias_grad, dec_grad[None], loss
 
 

time: 123 us -> 87.4 us (0.71)
  other arithmetic: 21.7 us -> 2.32 us
  local copies, waits for them, and re-layouts: 13.2 us -> 4.5 us
  between operations: 8.01 us -> 2.81 us
  starting transfers between devices: 48 us -> 44.3 us
    ppermute x18 -> x24, starting transfers between devices: 24.2 us -> 40.1 us  [along(): return lax.ppermute(block, 'feat', self.step)]
    ppermute x15 -> x11, starting transfers between devices: 14.6 us -> 1.64 us  [across(): return lax.ppermute(block, 'feat', self.twin)]
    unnamed x50 -> x18, local copies, waits for them, and re-layouts: 11.3 us -> 3 us
    reduce_sum x7 -> x0, other arithmetic: 7.92 us -> none  [the longest x1 3.08 us: body(): jnp.sum(jnp.square(w_dec_later[0].astype(f32)), axis=1) + norm_epsilon]
    ppermute x7 -> x1, starting transfers between devices: 7.12 us -> 1.06 us  [body(): lax.ppermute(sent_loss, 'layer', [(i, (i + 1) % layers) for i in range(la...]
    convert_element_type x6, other arithmetic: 5.98 us -> 0.29 us  [scatter_sum(): arrived = ring.along(total.astype(bf16))]
    pallas_call x0 -> x4, Pallas kernels: none -> 3.27 us  [the longest x2 2.11 us: misfits(): pl.pallas_call(functools.partial(misfit_kernel, carries_loss), out_shape=...]
    ppermute x18 -> x24, waiting for transfers between devices: 17.6 us -> 19.8 us  [along(): return lax.ppermute(block, 'feat', self.step)]
  transfers between devices with their start and end apart: 41 -> 37, of which waited for: 20 -> 22; matrix products, arithmetic and copies ran while one was open for 17% -> 3% of each run, Pallas kernels for 10% -> 14%
where the time goes in v3:
time: 87.4 us; the launch traced here: 87.1 us
  starting transfers between devices  44.3 us (51%)
  waiting for transfers between devices  20.8 us (24%)
  Pallas kernels  12.3 us (14%)
  local copies, waits for them, and re-layouts  4.5 us (5%)
  between operations  2.81 us (3%)
  other arithmetic  2.32 us (3%)
    ppermute x24, starting transfers between devices, along(): return lax.ppermute(block, 'feat', self.step)  40.1 us
    ppermute x24, waiting for transfers between devices, along(): return lax.ppermute(block, 'feat', self.step)  19.8 us
    pallas_call x1, Pallas kernels, backward(): pl.pallas_call(functools.partial(backward_kernel, tuple((len(e) for e in...  5.51 us
    unnamed x18, local copies, waits for them, and re-layouts  3 us
    pallas_call x2, Pallas kernels, forward(): pl.pallas_call(functools.partial(forward_kernel, len(pieces), min(512, wi...  2.88 us
    pallas_call x2, Pallas kernels, misfits(): pl.pallas_call(functools.partial(misfit_kernel, carries_loss), out_shape=...  2.11 us
  transfers between devices with their start and end apart: 37, of which 22 were waited for; matrix products, arithmetic and copies ran while one was open for 3% of the time, Pallas kernels for 14%

profile of v3, /device:TPU:0, one launch (start us, length us, event | category | flops | bytes accessed | tf_op | source)
XLA Modules:
  0.0 87.1 jit_solution(13479490669211946416)
XLA Ops:
  3.5 3.1 %collective-permute-start.1 = (bf16[16,4096]{1,0:T(8,128)(2,1)S(1)}, bf16[16,4096]{1,0:T(8,128)(2,1)S(1)}, u32[]{:S(2)}, u32[]{:S(2)}) collective-permute-start(bf16[16,4096]{1,0:T(8,128)(2,1)S(1)} %pad_maximum_fusion.refs_0_), channel_id=1, source_target_pairs={{0,4},{1,3},{2,0},{3,7},{4,8},{5,1},{6,2},{7,11},{8,12},{9,5},{10,... | collective-permute-start | bytes 393224 | tf_op jit(solution)/shard_map/ppermute | solution.py:43
  6.6 1.6 %collective-permute-start.19 = (bf16[16,4096]{1,0:T(8,128)(2,1)S(1)}, bf16[16,4096]{1,0:T(8,128)(2,1)S(1)}, u32[]{:S(2)}, u32[]{:S(2)}) collective-permute-start(bf16[16,4096]{1,0:T(8,128)(2,1)S(1)} %pad_maximum_fusion.2.refs_0_), channel_id=1, source_target_pairs={{0,4},{1,3},{2,0},{3,7},{4,8},{5,1},{6,2},{7,11},{8,12},{9,5},{10,... | collective-permute-start | bytes 393224 | tf_op jit(solution)/shard_map/ppermute | solution.py:43
  9.5 2.2 %collective-permute-start.2 = (bf16[16,4096]{1,0:T(8,128)(2,1)S(1)}, bf16[16,4096]{1,0:T(8,128)(2,1)S(1)}, u32[]{:S(2)}, u32[]{:S(2)}) collective-permute-start(bf16[16,4096]{1,0:T(8,128)(2,1)S(1)} %collective-permute-done.1), channel_id=1, source_target_pairs={{0,4},{1,3},{2,0},{3,7},{4,8},{5,1},{6,2},{7,11},{8,12},{9,5},{10,... | collective-permute-start | bytes 393224 | tf_op jit(solution)/shard_map/ppermute | solution.py:43
  14.0 1.6 %collective-permute-start.20 = (bf16[16,4096]{1,0:T(8,128)(2,1)S(1)}, bf16[16,4096]{1,0:T(8,128)(2,1)S(1)}, u32[]{:S(2)}, u32[]{:S(2)}) collective-permute-start(bf16[16,4096]{1,0:T(8,128)(2,1)S(1)} %collective-permute-done.19), channel_id=1, source_target_pairs={{0,4},{1,3},{2,0},{3,7},{4,8},{5,1},{6,2},{7,11},{8,12},{9,5},{10,... | collective-permute-start | bytes 393224 | tf_op jit(solution)/shard_map/ppermute | solution.py:43
  15.6 1.6 %collective-permute-start.3 = (bf16[16,4096]{1,0:T(8,128)(2,1)S(1)}, bf16[16,4096]{1,0:T(8,128)(2,1)S(1)}, u32[]{:S(2)}, u32[]{:S(2)}) collective-permute-start(bf16[16,4096]{1,0:T(8,128)(2,1)S(1)} %collective-permute-done.2), channel_id=1, source_target_pairs={{0,4},{1,3},{2,0},{3,7},{4,8},{5,1},{6,2},{7,11},{8,12},{9,5},{10,... | collective-permute-start | bytes 393224 | tf_op jit(solution)/shard_map/ppermute | solution.py:43
  18.9 1.6 %collective-permute-start.21 = (bf16[16,4096]{1,0:T(8,128)(2,1)S(1)}, bf16[16,4096]{1,0:T(8,128)(2,1)S(1)}, u32[]{:S(2)}, u32[]{:S(2)}) collective-permute-start(bf16[16,4096]{1,0:T(8,128)(2,1)S(1)} %collective-permute-done.20), channel_id=1, source_target_pairs={{0,4},{1,3},{2,0},{3,7},{4,8},{5,1},{6,2},{7,11},{8,12},{9,5},{10,... | collective-permute-start | bytes 393224 | tf_op jit(solution)/shard_map/ppermute | solution.py:43
  20.7 1.6 %collective-permute-start.5 = (bf16[16,4096]{1,0:T(8,128)(2,1)S(1)}, bf16[16,4096]{1,0:T(8,128)(2,1)S(1)}, u32[]{:S(2)}, u32[]{:S(2)}) collective-permute-start(bf16[16,4096]{1,0:T(8,128)(2,1)S(1)} %collective-permute-done.3), channel_id=1, source_target_pairs={{0,4},{1,3},{2,0},{3,7},{4,8},{5,1},{6,2},{7,11},{8,12},{9,5},{10,... | collective-permute-start | bytes 393224 | tf_op jit(solution)/shard_map/ppermute | solution.py:43
  22.4 1.6 %collective-permute-done.21 = bf16[16,4096]{1,0:T(8,128)(2,1)S(1)} collective-permute-done((bf16[16,4096]{1,0:T(8,128)(2,1)S(1)}, bf16[16,4096]{1,0:T(8,128)(2,1)S(1)}, u32[]{:S(2)}, u32[]{:S(2)}) %collective-permute-start.21) | collective-permute-done | bytes 131104 | tf_op jit(solution)/shard_map/ppermute | solution.py:43
  24.0 1.6 %collective-permute-start.23 = (bf16[16,4096]{1,0:T(8,128)(2,1)S(1)}, bf16[16,4096]{1,0:T(8,128)(2,1)S(1)}, u32[]{:S(2)}, u32[]{:S(2)}) collective-permute-start(bf16[16,4096]{1,0:T(8,128)(2,1)S(1)} %collective-permute-done.21), channel_id=1, source_target_pairs={{0,4},{1,3},{2,0},{3,7},{4,8},{5,1},{6,2},{7,11},{8,12},{9,5},{10,... | collective-permute-start | bytes 393224 | tf_op jit(solution)/shard_map/ppermute | solution.py:43
  25.8 2.2 %copy-done.1 = bf16[1,4096,512]{2,1,0:T(8,128)(2,1)S(1)} copy-done((bf16[1,4096,512]{2,1,0:T(8,128)(2,1)S(1)}, bf16[1,4096,512]{2,1,0:T(8,128)(2,1)}, u32[]{:S(2)}) %copy-start.1) | copy-done | bytes 4194328
  31.8 1.6 %collective-permute-start.7 = (bf16[8,4096]{1,0:T(8,128)(2,1)S(1)}, bf16[8,4096]{1,0:T(8,128)(2,1)S(1)}, u32[]{:S(2)}, u32[]{:S(2)}) collective-permute-start(bf16[8,4096]{1,0:T(8,128)(2,1)S(1)} %fusion.1), channel_id=1, source_target_pairs={{0,4},{1,3},{2,0},{3,7},{4,8},{5,1},{6,2},{7,11},{8,12},{9,5},{10,... | collective-permute-start | bytes 196616 | tf_op jit(solution)/shard_map/ppermute | solution.py:43
  33.6 1.6 %collective-permute-start.25 = (bf16[8,4096]{1,0:T(8,128)(2,1)S(1)}, bf16[8,4096]{1,0:T(8,128)(2,1)S(1)}, u32[]{:S(2)}, u32[]{:S(2)}) collective-permute-start(bf16[8,4096]{1,0:T(8,128)(2,1)S(1)} %fusion), channel_id=1, source_target_pairs={{0,4},{1,3},{2,0},{3,7},{4,8},{5,1},{6,2},{7,11},{8,12},{9,5},{10,... | collective-permute-start | bytes 196616 | tf_op jit(solution)/shard_map/ppermute | solution.py:43
  36.1 1.6 %collective-permute-start.8 = (bf16[16,4096]{1,0:T(8,128)(2,1)S(1)}, bf16[16,4096]{1,0:T(8,128)(2,1)S(1)}, u32[]{:S(2)}, u32[]{:S(2)}) collective-permute-start(bf16[16,4096]{1,0:T(8,128)(2,1)S(1)} %add_convert_fusion.7), channel_id=1, source_target_pairs={{0,4},{1,3},{2,0},{3,7},{4,8},{5,1},{6,2},{7,11},{8,12},{9,5},{10,... | collective-permute-start | bytes 393224 | tf_op jit(solution)/shard_map/ppermute | solution.py:43
  38.0 1.6 %collective-permute-start.26 = (bf16[16,4096]{1,0:T(8,128)(2,1)S(1)}, bf16[16,4096]{1,0:T(8,128)(2,1)S(1)}, u32[]{:S(2)}, u32[]{:S(2)}) collective-permute-start(bf16[16,4096]{1,0:T(8,128)(2,1)S(1)} %add_convert_fusion.3), channel_id=1, source_target_pairs={{0,4},{1,3},{2,0},{3,7},{4,8},{5,1},{6,2},{7,11},{8,12},{9,5},{10,... | collective-permute-start | bytes 393224 | tf_op jit(solution)/shard_map/ppermute | solution.py:43
  41.2 1.6 %collective-permute-start.9 = (bf16[16,4096]{1,0:T(8,128)(2,1)S(1)}, bf16[16,4096]{1,0:T(8,128)(2,1)S(1)}, u32[]{:S(2)}, u32[]{:S(2)}) collective-permute-start(bf16[16,4096]{1,0:T(8,128)(2,1)S(1)} %add_convert_fusion.6), channel_id=1, source_target_pairs={{0,4},{1,3},{2,0},{3,7},{4,8},{5,1},{6,2},{7,11},{8,12},{9,5},{10,... | collective-permute-start | bytes 393224 | tf_op jit(solution)/shard_map/ppermute | solution.py:43
  43.1 1.6 %collective-permute-start.27 = (bf16[16,4096]{1,0:T(8,128)(2,1)S(1)}, bf16[16,4096]{1,0:T(8,128)(2,1)S(1)}, u32[]{:S(2)}, u32[]{:S(2)}) collective-permute-start(bf16[16,4096]{1,0:T(8,128)(2,1)S(1)} %add_convert_fusion.2), channel_id=1, source_target_pairs={{0,4},{1,3},{2,0},{3,7},{4,8},{5,1},{6,2},{7,11},{8,12},{9,5},{10,... | collective-permute-start | bytes 393224 | tf_op jit(solution)/shard_map/ppermute | solution.py:43
  46.3 1.6 %collective-permute-start.10 = (bf16[16,4096]{1,0:T(8,128)(2,1)S(1)}, bf16[16,4096]{1,0:T(8,128)(2,1)S(1)}, u32[]{:S(2)}, u32[]{:S(2)}) collective-permute-start(bf16[16,4096]{1,0:T(8,128)(2,1)S(1)} %add_convert_fusion.5), channel_id=1, source_target_pairs={{0,4},{1,3},{2,0},{3,7},{4,8},{5,1},{6,2},{7,11},{8,12},{9,5},{10,... | collective-permute-start | bytes 393224 | tf_op jit(solution)/shard_map/ppermute | solution.py:43
  48.2 1.6 %collective-permute-start.28 = (bf16[16,4096]{1,0:T(8,128)(2,1)S(1)}, bf16[16,4096]{1,0:T(8,128)(2,1)S(1)}, u32[]{:S(2)}, u32[]{:S(2)}) collective-permute-start(bf16[16,4096]{1,0:T(8,128)(2,1)S(1)} %add_convert_fusion.1), channel_id=1, source_target_pairs={{0,4},{1,3},{2,0},{3,7},{4,8},{5,1},{6,2},{7,11},{8,12},{9,5},{10,... | collective-permute-start | bytes 393224 | tf_op jit(solution)/shard_map/ppermute | solution.py:43
  51.4 1.8 %collective-permute-done.28 = bf16[16,4096]{1,0:T(8,128)(2,1)S(1)} collective-permute-done((bf16[16,4096]{1,0:T(8,128)(2,1)S(1)}, bf16[16,4096]{1,0:T(8,128)(2,1)S(1)}, u32[]{:S(2)}, u32[]{:S(2)}) %collective-permute-start.28) | collective-permute-done | bytes 131104 | tf_op jit(solution)/shard_map/ppermute | solution.py:43
  54.0 1.6 %collective-permute-start.14 = (bf16[16,4096]{1,0:T(8,128)(2,1)S(1)}, bf16[16,4096]{1,0:T(8,128)(2,1)S(1)}, u32[]{:S(2)}, u32[]{:S(2)}) collective-permute-start(bf16[16,4096]{1,0:T(8,128)(2,1)S(1)} %get-tuple-element.47.refs_0_), channel_id=1, source_target_pairs={{0,4},{1,3},{2,0},{3,7},{4,8},{5,1},{6,2},{7,11},{8,12},{9,5},{10,... | collective-permute-start | bytes 393224 | tf_op jit(solution)/shard_map/ppermute | solution.py:43
  59.0 1.6 %collective-permute-start.15 = (bf16[16,4096]{1,0:T(8,128)(2,1)S(1)}, bf16[16,4096]{1,0:T(8,128)(2,1)S(1)}, u32[]{:S(2)}, u32[]{:S(2)}) collective-permute-start(bf16[16,4096]{1,0:T(8,128)(2,1)S(1)} %collective-permute-done.14), channel_id=1, source_target_pairs={{0,4},{1,3},{2,0},{3,7},{4,8},{5,1},{6,2},{7,11},{8,12},{9,5},{10,... | collective-permute-start | bytes 393224 | tf_op jit(solution)/shard_map/ppermute | solution.py:43
  64.0 1.6 %collective-permute-start.16 = (bf16[16,4096]{1,0:T(8,128)(2,1)S(1)}, bf16[16,4096]{1,0:T(8,128)(2,1)S(1)}, u32[]{:S(2)}, u32[]{:S(2)}) collective-permute-start(bf16[16,4096]{1,0:T(8,128)(2,1)S(1)} %collective-permute-done.15), channel_id=1, source_target_pairs={{0,4},{1,3},{2,0},{3,7},{4,8},{5,1},{6,2},{7,11},{8,12},{9,5},{10,... | collective-permute-start | bytes 393224 | tf_op jit(solution)/shard_map/ppermute | solution.py:43
  68.6 3.5 %collective-permute-done.33 = bf16[16,4224]{1,0:T(8,128)(2,1)S(1)} collective-permute-done((bf16[16,4224]{1,0:T(8,128)(2,1)S(1)}, bf16[16,4224]{1,0:T(8,128)(2,1)S(1)}, u32[]{:S(2)}, u32[]{:S(2)}) %collective-permute-start.33) | collective-permute-done | bytes 135200 | tf_op jit(solution)/shard_map/ppermute | solution.py:43
  79.3 5.5 %shard_map.109 = (bf16[4096,512]{1,0:T(8,128)(2,1)}, f32[1,512]{1,0:T(1,128)}, bf16[512,4096]{1,0:T(8,128)(2,1)}) custom-call(bf16[16,4096]{1,0:T(8,128)(2,1)S(1)} %get-tuple-element.47.refs_0_, bf16[48,4096]{1,0:T(8,128)(2,1)S(1)} %constant_dynamic-update-slice_fusion.3.refs_1_, bf16[48,4096]{1,0:T(8,128)(2,1)S(1)} %collective-permute-done.17.refs_2_, ...), custom_call_target="tpu_custom_call" | custom-call | flops 3221225472 | bytes 8388608 | tf_op jit(solution)/shard_map/pallas_call | solution.py:258
  (110 shorter events, 37.0 us)
Async XLA Ops:
  3.5 6.0 %collective-permute-start.1 = (bf16[16,4096]{1,0:T(8,128)(2,1)S(1)}, bf16[16,4096]{1,0:T(8,128)(2,1)S(1)}, u32[]{:S(2)}, u32[]{:S(2)}) collective-permute-start(bf16[16,4096]{1,0:T(8,128)(2,1)S(1)} %pad_maximum_fusion.refs_0_), channel_id=1, source_target_pairs={{0,4},{1,3},{2,0},{3,7},{4,8},{5,1},{6,2},{7,11},{8,12},{9,5},{10,... | collective-permute-start | bytes 393224 | tf_op jit(solution)/shard_map/ppermute | solution.py:43
  6.6 5.7 %collective-permute-start.19 = (bf16[16,4096]{1,0:T(8,128)(2,1)S(1)}, bf16[16,4096]{1,0:T(8,128)(2,1)S(1)}, u32[]{:S(2)}, u32[]{:S(2)}) collective-permute-start(bf16[16,4096]{1,0:T(8,128)(2,1)S(1)} %pad_maximum_fusion.2.refs_0_), channel_id=1, source_target_pairs={{0,4},{1,3},{2,0},{3,7},{4,8},{5,1},{6,2},{7,11},{8,12},{9,5},{10,... | collective-permute-start | bytes 393224 | tf_op jit(solution)/shard_map/ppermute | solution.py:43
  9.5 6.0 %collective-permute-start.2 = (bf16[16,4096]{1,0:T(8,128)(2,1)S(1)}, bf16[16,4096]{1,0:T(8,128)(2,1)S(1)}, u32[]{:S(2)}, u32[]{:S(2)}) collective-permute-start(bf16[16,4096]{1,0:T(8,128)(2,1)S(1)} %collective-permute-done.1), channel_id=1, source_target_pairs={{0,4},{1,3},{2,0},{3,7},{4,8},{5,1},{6,2},{7,11},{8,12},{9,5},{10,... | collective-permute-start | bytes 393224 | tf_op jit(solution)/shard_map/ppermute | solution.py:43
  12.4 5.2 %collective-permute-start.12 = (bf16[16,4096]{1,0:T(8,128)(2,1)}, bf16[16,4096]{1,0:T(8,128)(2,1)S(1)}, u32[]{:S(2)}, u32[]{:S(2)}) collective-permute-start(bf16[16,4096]{1,0:T(8,128)(2,1)} %bitcast.29), channel_id=1, source_target_pairs={{0,16},{16,0},{1,17},{17,1},{2,18},{18,2},{3,19},{19,3},{4,20},{20... | collective-permute-start | bytes 393224 | tf_op jit(solution)/shard_map/ppermute | solution.py:392
  20.6 5.2 %collective-permute-start.4 = (bf16[48,4096]{1,0:T(8,128)(2,1)S(1)}, bf16[48,4096]{1,0:T(8,128)(2,1)S(1)}, u32[]{:S(2)}, u32[]{:S(2)}) collective-permute-start(bf16[48,4096]{1,0:T(8,128)(2,1)S(1)} %constant_dynamic-update-slice_fusion.refs_1_), channel_id=1, source_target_pairs={{0,1},{1,0},{2,3},{3,2},{4,5},{5,4},{6,7},{7,6},{8,9},{9,8},{10,11... | collective-permute-start | bytes 1179656 | tf_op jit(solution)/shard_map/ppermute | solution.py:46
  20.7 5.0 %collective-permute-start.5 = (bf16[16,4096]{1,0:T(8,128)(2,1)S(1)}, bf16[16,4096]{1,0:T(8,128)(2,1)S(1)}, u32[]{:S(2)}, u32[]{:S(2)}) collective-permute-start(bf16[16,4096]{1,0:T(8,128)(2,1)S(1)} %collective-permute-done.3), channel_id=1, source_target_pairs={{0,4},{1,3},{2,0},{3,7},{4,8},{5,1},{6,2},{7,11},{8,12},{9,5},{10,... | collective-permute-start | bytes 393224 | tf_op jit(solution)/shard_map/ppermute | solution.py:43
  23.9 5.6 %collective-permute-start.22 = (bf16[48,4096]{1,0:T(8,128)(2,1)S(1)}, bf16[48,4096]{1,0:T(8,128)(2,1)S(1)}, u32[]{:S(2)}, u32[]{:S(2)}) collective-permute-start(bf16[48,4096]{1,0:T(8,128)(2,1)S(1)} %constant_dynamic-update-slice_fusion.6.refs_1_), channel_id=1, source_target_pairs={{0,1},{1,0},{2,3},{3,2},{4,5},{5,4},{6,7},{7,6},{8,9},{9,8},{10,11... | collective-permute-start | bytes 1179656 | tf_op jit(solution)/shard_map/ppermute | solution.py:46
  24.0 5.5 %collective-permute-start.23 = (bf16[16,4096]{1,0:T(8,128)(2,1)S(1)}, bf16[16,4096]{1,0:T(8,128)(2,1)S(1)}, u32[]{:S(2)}, u32[]{:S(2)}) collective-permute-start(bf16[16,4096]{1,0:T(8,128)(2,1)S(1)} %collective-permute-done.21), channel_id=1, source_target_pairs={{0,4},{1,3},{2,0},{3,7},{4,8},{5,1},{6,2},{7,11},{8,12},{9,5},{10,... | collective-permute-start | bytes 393224 | tf_op jit(solution)/shard_map/ppermute | solution.py:43
  36.1 5.0 %collective-permute-start.8 = (bf16[16,4096]{1,0:T(8,128)(2,1)S(1)}, bf16[16,4096]{1,0:T(8,128)(2,1)S(1)}, u32[]{:S(2)}, u32[]{:S(2)}) collective-permute-start(bf16[16,4096]{1,0:T(8,128)(2,1)S(1)} %add_convert_fusion.7), channel_id=1, source_target_pairs={{0,4},{1,3},{2,0},{3,7},{4,8},{5,1},{6,2},{7,11},{8,12},{9,5},{10,... | collective-permute-start | bytes 393224 | tf_op jit(solution)/shard_map/ppermute | solution.py:43
  38.0 5.0 %collective-permute-start.26 = (bf16[16,4096]{1,0:T(8,128)(2,1)S(1)}, bf16[16,4096]{1,0:T(8,128)(2,1)S(1)}, u32[]{:S(2)}, u32[]{:S(2)}) collective-permute-start(bf16[16,4096]{1,0:T(8,128)(2,1)S(1)} %add_convert_fusion.3), channel_id=1, source_target_pairs={{0,4},{1,3},{2,0},{3,7},{4,8},{5,1},{6,2},{7,11},{8,12},{9,5},{10,... | collective-permute-start | bytes 393224 | tf_op jit(solution)/shard_map/ppermute | solution.py:43
  40.7 14.9 %collective-permute-start.30 = (f32[1,512]{1,0:T(1,128)S(1)}, f32[1,512]{1,0:T(1,128)S(1)}, u32[]{:S(2)}, u32[]{:S(2)}) collective-permute-start(f32[1,512]{1,0:T(1,128)S(1)} %get-tuple-element.55.refs_3_), channel_id=1, source_target_pairs={{0,1},{1,0},{2,3},{3,2},{4,5},{5,4},{6,7},{7,6},{8,9},{9,8},{10,11... | collective-permute-start | bytes 6152 | tf_op jit(solution)/shard_map/ppermute | solution.py:46
  41.2 5.0 %collective-permute-start.9 = (bf16[16,4096]{1,0:T(8,128)(2,1)S(1)}, bf16[16,4096]{1,0:T(8,128)(2,1)S(1)}, u32[]{:S(2)}, u32[]{:S(2)}) collective-permute-start(bf16[16,4096]{1,0:T(8,128)(2,1)S(1)} %add_convert_fusion.6), channel_id=1, source_target_pairs={{0,4},{1,3},{2,0},{3,7},{4,8},{5,1},{6,2},{7,11},{8,12},{9,5},{10,... | collective-permute-start | bytes 393224 | tf_op jit(solution)/shard_map/ppermute | solution.py:43
  43.1 5.0 %collective-permute-start.27 = (bf16[16,4096]{1,0:T(8,128)(2,1)S(1)}, bf16[16,4096]{1,0:T(8,128)(2,1)S(1)}, u32[]{:S(2)}, u32[]{:S(2)}) collective-permute-start(bf16[16,4096]{1,0:T(8,128)(2,1)S(1)} %add_convert_fusion.2), channel_id=1, source_target_pairs={{0,4},{1,3},{2,0},{3,7},{4,8},{5,1},{6,2},{7,11},{8,12},{9,5},{10,... | collective-permute-start | bytes 393224 | tf_op jit(solution)/shard_map/ppermute | solution.py:43
  46.3 5.0 %collective-permute-start.10 = (bf16[16,4096]{1,0:T(8,128)(2,1)S(1)}, bf16[16,4096]{1,0:T(8,128)(2,1)S(1)}, u32[]{:S(2)}, u32[]{:S(2)}) collective-permute-start(bf16[16,4096]{1,0:T(8,128)(2,1)S(1)} %add_convert_fusion.5), channel_id=1, source_target_pairs={{0,4},{1,3},{2,0},{3,7},{4,8},{5,1},{6,2},{7,11},{8,12},{9,5},{10,... | collective-permute-start | bytes 393224 | tf_op jit(solution)/shard_map/ppermute | solution.py:43
  48.2 5.0 %collective-permute-start.28 = (bf16[16,4096]{1,0:T(8,128)(2,1)S(1)}, bf16[16,4096]{1,0:T(8,128)(2,1)S(1)}, u32[]{:S(2)}, u32[]{:S(2)}) collective-permute-start(bf16[16,4096]{1,0:T(8,128)(2,1)S(1)} %add_convert_fusion.1), channel_id=1, source_target_pairs={{0,4},{1,3},{2,0},{3,7},{4,8},{5,1},{6,2},{7,11},{8,12},{9,5},{10,... | collective-permute-start | bytes 393224 | tf_op jit(solution)/shard_map/ppermute | solution.py:43
  57.0 5.0 %collective-permute-start.31 = (bf16[16,4224]{1,0:T(8,128)(2,1)S(1)}, bf16[16,4224]{1,0:T(8,128)(2,1)S(1)}, u32[]{:S(2)}, u32[]{:S(2)}) collective-permute-start(bf16[16,4224]{1,0:T(8,128)(2,1)S(1)} %get-tuple-element.57.refs_4_.refs_0_), channel_id=1, source_target_pairs={{0,4},{1,3},{2,0},{3,7},{4,8},{5,1},{6,2},{7,11},{8,12},{9,5},{10,... | collective-permute-start | bytes 405512 | tf_op jit(solution)/shard_map/ppermute | solution.py:43
  59.0 5.0 %collective-permute-start.15 = (bf16[16,4096]{1,0:T(8,128)(2,1)S(1)}, bf16[16,4096]{1,0:T(8,128)(2,1)S(1)}, u32[]{:S(2)}, u32[]{:S(2)}) collective-permute-start(bf16[16,4096]{1,0:T(8,128)(2,1)S(1)} %collective-permute-done.14), channel_id=1, source_target_pairs={{0,4},{1,3},{2,0},{3,7},{4,8},{5,1},{6,2},{7,11},{8,12},{9,5},{10,... | collective-permute-start | bytes 393224 | tf_op jit(solution)/shard_map/ppermute | solution.py:43
  62.1 5.1 %collective-permute-start.32 = (bf16[16,4224]{1,0:T(8,128)(2,1)S(1)}, bf16[16,4224]{1,0:T(8,128)(2,1)S(1)}, u32[]{:S(2)}, u32[]{:S(2)}) collective-permute-start(bf16[16,4224]{1,0:T(8,128)(2,1)S(1)} %collective-permute-done.31), channel_id=1, source_target_pairs={{0,4},{1,3},{2,0},{3,7},{4,8},{5,1},{6,2},{7,11},{8,12},{9,5},{10,... | collective-permute-start | bytes 405512 | tf_op jit(solution)/shard_map/ppermute | solution.py:43
  64.0 8.2 %collective-permute-start.16 = (bf16[16,4096]{1,0:T(8,128)(2,1)S(1)}, bf16[16,4096]{1,0:T(8,128)(2,1)S(1)}, u32[]{:S(2)}, u32[]{:S(2)}) collective-permute-start(bf16[16,4096]{1,0:T(8,128)(2,1)S(1)} %collective-permute-done.15), channel_id=1, source_target_pairs={{0,4},{1,3},{2,0},{3,7},{4,8},{5,1},{6,2},{7,11},{8,12},{9,5},{10,... | collective-permute-start | bytes 393224 | tf_op jit(solution)/shard_map/ppermute | solution.py:43
  67.1 5.0 %collective-permute-start.33 = (bf16[16,4224]{1,0:T(8,128)(2,1)S(1)}, bf16[16,4224]{1,0:T(8,128)(2,1)S(1)}, u32[]{:S(2)}, u32[]{:S(2)}) collective-permute-start(bf16[16,4224]{1,0:T(8,128)(2,1)S(1)} %collective-permute-done.32), channel_id=1, source_target_pairs={{0,4},{1,3},{2,0},{3,7},{4,8},{5,1},{6,2},{7,11},{8,12},{9,5},{10,... | collective-permute-start | bytes 405512 | tf_op jit(solution)/shard_map/ppermute | solution.py:43
  72.2 5.7 %collective-permute-start.34 = (bf16[48,4224]{1,0:T(8,128)(2,1)S(1)}, bf16[48,4224]{1,0:T(8,128)(2,1)S(1)}, u32[]{:S(2)}, u32[]{:S(2)}) collective-permute-start(bf16[48,4224]{1,0:T(8,128)(2,1)S(1)} %constant_dynamic-update-slice_fusion.9.refs_5_.refs_1_), channel_id=1, source_target_pairs={{0,1},{1,0},{2,3},{3,2},{4,5},{5,4},{6,7},{7,6},{8,9},{9,8},{10,11... | collective-permute-start | bytes 1216520 | tf_op jit(solution)/shard_map/ppermute | solution.py:46
  72.3 7.0 %collective-permute-start.17 = (bf16[48,4096]{1,0:T(8,128)(2,1)S(1)}, bf16[48,4096]{1,0:T(8,128)(2,1)S(1)}, u32[]{:S(2)}, u32[]{:S(2)}) collective-permute-start(bf16[48,4096]{1,0:T(8,128)(2,1)S(1)} %constant_dynamic-update-slice_fusion.3.refs_1_), channel_id=1, source_target_pairs={{0,1},{1,0},{2,3},{3,2},{4,5},{5,4},{6,7},{7,6},{8,9},{9,8},{10,11... | collective-permute-start | bytes 1179656 | tf_op jit(solution)/shard_map/ppermute | solution.py:46
  72.8 5.0 %collective-permute-start.35 = (bf16[16,4224]{1,0:T(8,128)(2,1)S(1)}, bf16[16,4224]{1,0:T(8,128)(2,1)S(1)}, u32[]{:S(2)}, u32[]{:S(2)}) collective-permute-start(bf16[16,4224]{1,0:T(8,128)(2,1)S(1)} %collective-permute-done.33), channel_id=1, source_target_pairs={{0,4},{1,3},{2,0},{3,7},{4,8},{5,1},{6,2},{7,11},{8,12},{9,5},{10,... | collective-permute-start | bytes 405512 | tf_op jit(solution)/shard_map/ppermute | solution.py:43
  78.0 6.8 %collective-permute-start.36 = (f32[8,128]{1,0:T(8,128)S(1)}, f32[8,128]{1,0:T(8,128)S(1)}, u32[]{:S(2)}, u32[]{:S(2)}) collective-permute-start(f32[8,128]{1,0:T(8,128)S(1)} %shard_map.110), channel_id=1, source_target_pairs={{0,16},{16,0},{1,17},{17,1},{2,18},{18,2},{3,19},{19,3},{4,20},{20... | collective-permute-start | bytes 12296 | tf_op jit(solution)/shard_map/ppermute | solution.py:418
  (17 other events, 100.1 us)

commit v4 on v3

v4 whole, which is shorter than its diff:
```python
import functools

import jax
import jax.numpy as jnp
import numpy as np
from jax import lax
from jax.experimental import pallas as pl
from jax.experimental.pallas import tpu as pltpu
from jax.sharding import PartitionSpec as P

TBLOCK = 128
FBLOCK = 128
PAD = 128

penalty_weight = 0.5
norm_epsilon = 1e-06
f32 = jnp.float32
bf16 = jnp.bfloat16


class Ring:
    def __init__(self, size):
        chips = size // 2
        self.hops = (chips - 1) // 2
        self.far = chips % 2 == 0
        order = list(range(0, chips, 2)) + list(range(1, chips, 2))[::-1]
        place = {chip: at for at, chip in enumerate(order)}
        self.step = []
        owners = []
        for device in range(size):
            chip, core = divmod(device, 2)
            at = place[chip]
            ahead = 1 if core == 0 else -1
            self.step.append((device, order[(at + ahead) % chips] * 2 + core))
            behind = [order[(at - ahead * k) % chips] for k in range(1, self.hops + 1)]
            front = [order[(at + ahead * k) % chips] for k in range(1, self.hops + 1)]
            last = [order[(at + self.hops + 1) % chips]] if self.far else []
            owners.append([2 * c + i for c in [chip] + behind + front + last for i in (0, 1)])
        self.owners = np.array(owners, np.int32)
        self.twin = [(device, device ^ 1) for device in range(size)]

    def along(self, block):
        return lax.ppermute(block, "feat", self.step)

    def across(self, block):
        return lax.ppermute(block, "feat", self.twin)


def after(value, *signals):
    return lax.optimization_barrier((value, *signals))[0]


class Turns:
    def __init__(self, halves, pins):
        self.ended = [[] for _ in range(halves)]
        self.pins = pins

    def enter(self, half, block):
        hop = len(self.ended[half])
        signals = [ends[hop - 2] for ends in self.ended if ends is not self.ended[half] and hop >= 2]
        if half == 0 and hop + 1 in self.pins:
            signals += self.pins[hop + 1](self.ended)
        return after(block, *signals)

    def leave(self, half, block):
        self.ended[half].append(block)


def gather(ring, blocks, pins, joint):
    halves = len(blocks)
    turns = Turns(halves, pins)
    moving = list(blocks)
    front = [[] for _ in blocks]
    for k in range(ring.hops + ring.far):
        for h in range(halves):
            block = after(moving[h], front[h][k - 2]) if k >= 2 else moving[h]
            moving[h] = ring.along(turns.enter(h, block))
            turns.leave(h, moving[h])
            if k < ring.hops:
                front[h].append(ring.across(moving[h]))
    parts = [[blocks[h]] + turns.ended[h][: ring.hops] + front[h] + turns.ended[h][ring.hops :] for h in range(halves)]
    if joint:
        last = ring.hops + ring.far + 1
        parts = after(parts, *(pins[last](turns.ended) if last in pins else []))
    return parts


def scatter_sums(ring, first_core, rows, shares, pins):
    halves = len(shares)
    turns = Turns(halves, pins)
    from_twin = [ring.across(sent) for _, sent, _, _ in shares]
    arrived = [None] * halves
    for k in range(ring.hops + ring.far, 0, -1):
        for h in range(halves):
            _, _, front, last = shares[h]
            if k > ring.hops:
                total = last + from_twin[h][rows * ring.hops :].astype(f32)
                half = rows // 2
                total = jnp.where(first_core, total[:half], total[half:])
            else:
                total = front[rows * (k - 1) : rows * k]
                total = total + from_twin[h][rows * (k - 1) : rows * k].astype(f32)
                if arrived[h] is not None:
                    total = total + arrived[h].astype(f32)
            came = ring.along(turns.enter(h, total.astype(bf16)))
            turns.leave(h, came)
            if k > ring.hops:
                nothing = jnp.zeros_like(came)
                came = jnp.concatenate(
                    [jnp.where(first_core, came, nothing), jnp.where(first_core, nothing, came)], axis=0
                )
            arrived[h] = came
    results = []
    for h in range(halves):
        total = shares[h][0]
        if arrived[h] is not None:
            total = total + arrived[h].astype(f32)
        mine = total.astype(bf16)
        results.append((mine, ring.across(mine)))
    return results


def pair_kernel(halves, own_ref, other_ref, *outs):
    first = lax.axis_index("feat") % 2 == 0
    own, other = own_ref[...].astype(f32), other_ref[...].astype(f32)
    low = jnp.where(first, own, other)
    high = jnp.where(first, other, own)
    rows = own.shape[0] // halves
    for h in range(halves):
        here = slice(h * rows, (h + 1) * rows)
        outs[h][...] = jnp.concatenate([low[here], high[here]], axis=0).astype(bf16)


def chip_blocks(own, other, halves):
    rows, width = own.shape[0] // halves, own.shape[1]
    return pl.pallas_call(
        functools.partial(pair_kernel, halves),
        out_shape=[pltpu.VMEM((2 * rows, width), own.dtype)] * halves,
        in_specs=[VMEM_SPEC] * 2,
        out_specs=[VMEM_SPEC] * halves,
        compiler_params=pltpu.CompilerParams(vmem_limit_bytes=8 << 20),
        cost_estimate=SHORT,
    )(in_vmem(own), in_vmem(other))


def in_vmem(x):
    return pltpu.with_memory_space_constraint(x, pltpu.VMEM)


def in_hbm(x):
    return pltpu.with_memory_space_constraint(x, pltpu.HBM)


VMEM_SPEC = pl.BlockSpec(memory_space=pltpu.VMEM)
ANY_SPEC = pl.BlockSpec(memory_space=pl.ANY)
HBM_SPEC = pl.BlockSpec(memory_space=pltpu.HBM)
SHORT = pl.CostEstimate(flops=0, bytes_accessed=0, transcendentals=0)
SMEM_SPEC = pl.BlockSpec(memory_space=pltpu.SMEM)


def stacked(refs, columns):
    return jnp.concatenate([ref[:, columns] for ref in refs], axis=0)


def whole_pieces(parts):
    if all(p.shape[0] % 16 == 0 for p in parts):
        return parts
    return [jnp.concatenate(parts, axis=0)]


def forward_kernel(count, step, *refs):
    pieces = refs[:count]
    enc_ref, bias_ref, keep_ref, dec_ref = refs[count : count + 4]
    act_ref, gate_ref, sum_ref = refs[count + 4 : count + 7]
    outs = refs[count + 7 :]
    width = dec_ref.shape[1]
    preact = jnp.zeros(gate_ref.shape, f32)
    for at in range(0, width, step):
        preact = preact + jnp.dot(
            stacked(pieces, slice(at, at + step)), enc_ref[at : at + step, :], preferred_element_type=f32
        )
    positive = jnp.maximum(preact + bias_ref[...], 0.0)
    keep = keep_ref[...]
    act = (keep * positive * positive).astype(bf16)
    act_ref[...] = act
    gate_ref[...] = keep * 2.0 * positive
    sum_ref[...] = jnp.sum(act.astype(f32), axis=0, keepdims=True)
    for at in range(0, width, step):
        part = jnp.dot(act, dec_ref[:, at : at + step], preferred_element_type=f32)
        if len(outs) == 1:
            outs[0][:, at : at + step] = part
            continue
        own_ref, sent_ref, front_ref, last_ref = outs
        rows, hop = own_ref.shape[0], front_ref.shape[0]
        own_ref[:, at : at + step] = part[:rows]
        sent_ref[:hop, at : at + step] = part[rows : rows + hop].astype(bf16)
        sent_ref[hop:, at : at + step] = part[rows + 2 * hop :].astype(bf16)
        front_ref[:, at : at + step] = part[rows + hop : rows + 2 * hop]
        last_ref[:, at : at + step] = part[rows + 2 * hop :]


def forward(ring, parts, encoder, bias, keep, decoder):
    pieces = whole_pieces(parts)
    rows, features = parts[0].shape[0], encoder.shape[1]
    total = sum(p.shape[0] for p in parts)
    hop = rows * ring.hops
    width = decoder.shape[1]
    shapes = [((total, features), bf16), ((total, features), f32), ((1, features), f32)]
    apart = rows % 16 == 0 and ring.hops > 0 and ring.far
    if apart:
        shapes += [((rows, width), f32), ((hop + rows, width), bf16), ((hop, width), f32), ((rows, width), f32)]
    else:
        shapes += [((total, width), f32)]
    outs = pl.pallas_call(
        functools.partial(forward_kernel, len(pieces), min(512, width)),
        out_shape=[pltpu.VMEM(shape, dtype) for shape, dtype in shapes],
        in_specs=[VMEM_SPEC] * (len(pieces) + 4),
        out_specs=[VMEM_SPEC] * len(shapes),
        compiler_params=pltpu.CompilerParams(vmem_limit_bytes=12 << 20),
        cost_estimate=SHORT,
    )(*[in_vmem(x) for x in (*pieces, encoder, bias, keep, decoder)])
    act, gate, act_sum = outs[:3]
    if apart:
        return act, gate, act_sum, outs[3:]
    full = outs[3]
    own, behind, front, last = (
        full[:rows], full[rows : rows + hop], full[rows + hop : rows + 2 * hop], full[rows + 2 * hop :]
    )
    return act, gate, act_sum, (own, jnp.concatenate([behind, last], axis=0).astype(bf16), front, last)


def turn_kernel(*refs):
    pieces, out_ref = refs[:-1], refs[-1]
    step = 128 if out_ref.shape[0] % 128 == 0 else out_ref.shape[0]
    for at in range(0, out_ref.shape[0], step):
        out_ref[at : at + step, :] = stacked(pieces, slice(at, at + step)).T


def turned(parts):
    pieces = whole_pieces(parts)
    total = sum(p.shape[0] for p in pieces)
    width = pieces[0].shape[1]
    return pl.pallas_call(
        turn_kernel,
        out_shape=pltpu.VMEM((width, total), bf16),
        in_specs=[VMEM_SPEC] * len(pieces),
        out_specs=VMEM_SPEC,
        compiler_params=pltpu.CompilerParams(vmem_limit_bytes=12 << 20),
        cost_estimate=SHORT,
    )(*[in_vmem(x) for x in pieces])


def backward_kernel(counts, step, *refs):
    halves = len(counts)
    at = sum(counts)
    errors = refs[:at]
    acts, gates, rows = (refs[at + halves * i : at + halves * (i + 1)] for i in range(3))
    dec_ref, norm_ref, sum_ref = refs[at + 3 * halves : at + 3 * halves + 3]
    enc_out, bias_out, dec_out = refs[at + 3 * halves + 3 : at + 3 * halves + 6]
    enc_stage, dec_stage, enc_sems, dec_sems = refs[at + 3 * halves + 6 :]
    features, width = dec_ref.shape
    turned_act = jnp.concatenate([a[...] for a in acts], axis=0).T
    coef = penalty_weight * sum_ref[...] / norm_ref[...]
    coef = jnp.broadcast_to(coef, (8, features)).T[:, :1]
    copies = []
    for i, at in enumerate(range(0, width, step)):
        columns = slice(at, at + step)
        grad = jnp.dot(turned_act, stacked(errors, columns), preferred_element_type=f32)
        grad = grad + coef * dec_ref[:, columns].astype(f32)
        dec_stage[:, columns] = grad.astype(bf16)
        copy = pltpu.make_async_copy(dec_stage.at[:, columns], dec_out.at[:, columns], dec_sems.at[i])
        copy.start()
        copies.append(copy)
    total = turned_act.shape[1]
    act_grad = jnp.zeros((total, features), f32)
    for at in range(0, width, step):
        columns = slice(at, at + step)
        act_grad = act_grad + lax.dot_general(
            stacked(errors, columns), dec_ref[:, columns], (((1,), (1,)), ((), ())), preferred_element_type=f32
        )
    gate = jnp.concatenate([g[...] for g in gates], axis=0)
    pre_grad = ((act_grad + penalty_weight * norm_ref[...]) * gate).astype(bf16)
    bias_out[...] = jnp.sum(pre_grad.astype(f32), axis=0, keepdims=True)
    for i, at in enumerate(range(0, width, step)):
        here = slice(at, at + step)
        left = jnp.concatenate([r[here, :] for r in rows], axis=1)
        enc_stage[here, :] = jnp.dot(left, pre_grad, preferred_element_type=f32).astype(bf16)
        copy = pltpu.make_async_copy(enc_stage.at[here, :], enc_out.at[here, :], enc_sems.at[i])
        copy.start()
        copies.append(copy)
    for copy in copies:
        copy.wait()


def backward(errors, acts, gates, rows, decoder, norms, act_sum):
    errors = [whole_pieces(e) for e in errors]
    features, width = decoder.shape
    step = min(512, width)
    operands = [x for e in errors for x in e] + acts + gates + rows + [decoder, norms, act_sum]
    total = sum(a.shape[0] for a in acts)
    return pl.pallas_call(
        functools.partial(backward_kernel, tuple(len(e) for e in errors), step),
        out_shape=[
            jax.ShapeDtypeStruct((width, features), bf16),
            jax.ShapeDtypeStruct((1, features), f32),
            jax.ShapeDtypeStruct((features, width), bf16),
        ],
        in_specs=[VMEM_SPEC] * len(operands),
        out_specs=[ANY_SPEC, VMEM_SPEC, ANY_SPEC],
        scratch_shapes=[
            pltpu.VMEM((width, features), bf16),
            pltpu.VMEM((features, width), bf16),
            pltpu.SemaphoreType.DMA((width // step,)),
            pltpu.SemaphoreType.DMA((width // step,)),
        ],
        compiler_params=pltpu.CompilerParams(vmem_limit_bytes=24 << 20),
        cost_estimate=SHORT,
    )(*[in_vmem(x) for x in operands])


def start_kernel(table_ref, own_ref, row_ref, out_ref, sems):
    copies = [
        pltpu.make_async_copy(own_ref, out_ref, sems.at[0]),
        pltpu.make_async_copy(table_ref.at[lax.axis_index("feat")], row_ref, sems.at[1]),
    ]
    for copy in copies:
        copy.start()
    for copy in copies:
        copy.wait()


def start(table, own):
    return pl.pallas_call(
        start_kernel,
        out_shape=[pltpu.VMEM((1, table.shape[2]), f32), pltpu.VMEM(own.shape, own.dtype)],
        in_specs=[HBM_SPEC] * 2,
        out_specs=[VMEM_SPEC] * 2,
        scratch_shapes=[pltpu.SemaphoreType.DMA((2,))],
        compiler_params=pltpu.CompilerParams(vmem_limit_bytes=4 << 20),
        cost_estimate=SHORT,
    )(in_hbm(table), in_hbm(own))


def load_kernel(source_ref, signal_ref, out_ref, sems):
    pieces = sems.shape[0]
    rows = out_ref.shape[0] // pieces
    copies = []
    for i in range(pieces):
        here = slice(i * rows, (i + 1) * rows)
        copy = pltpu.make_async_copy(source_ref.at[here], out_ref.at[here], sems.at[i])
        copy.start()
        copies.append(copy)
    for copy in copies:
        copy.wait()


def loaded(array, signal):
    return pl.pallas_call(
        load_kernel,
        out_shape=pltpu.VMEM(array.shape, array.dtype),
        in_specs=[HBM_SPEC, VMEM_SPEC],
        out_specs=VMEM_SPEC,
        scratch_shapes=[pltpu.SemaphoreType.DMA((8,))],
        compiler_params=pltpu.CompilerParams(vmem_limit_bytes=4 << 20),
        cost_estimate=SHORT,
    )(in_hbm(array), in_vmem(signal))


def keep_kernel(mask_ref, token_ref, signal_ref, *outs):
    token_block = jnp.broadcast_to(token_ref[...], (8, token_ref.shape[1])).T[:, :1]
    for h, out_ref in enumerate(outs):
        total = out_ref.shape[0]
        here = token_block[h * total : (h + 1) * total]
        for j in range(mask_ref.shape[1]):
            column = jnp.zeros((total, FBLOCK), f32)
            for b in range(mask_ref.shape[0]):
                column = jnp.where(here == b, mask_ref[b, j].astype(f32), column)
            out_ref[:, j * FBLOCK : (j + 1) * FBLOCK] = column


def keeps(mask, token_block, signal, halves):
    total, features = token_block.shape[1] // halves, mask.shape[1] * FBLOCK
    return pl.pallas_call(
        keep_kernel,
        out_shape=[pltpu.VMEM((total, features), f32)] * halves,
        in_specs=[SMEM_SPEC, VMEM_SPEC, VMEM_SPEC],
        out_specs=[VMEM_SPEC] * halves,
        compiler_params=pltpu.CompilerParams(vmem_limit_bytes=4 << 20),
        cost_estimate=SHORT,
    )(mask, in_vmem(token_block), in_vmem(signal))


def norm_kernel(dec_ref, signal_ref, norm_ref):
    features, width = dec_ref.shape
    partial = jnp.zeros((features, 128), f32)
    for at in range(0, width, 128):
        part = dec_ref[:, at : at + 128].astype(f32)
        partial = partial + part * part
    norm_ref[...] = jnp.sqrt(jnp.sum(partial.T, axis=0, keepdims=True) + norm_epsilon)


def norms(decoder, signal):
    return pl.pallas_call(
        norm_kernel,
        out_shape=pltpu.VMEM((1, decoder.shape[0]), f32),
        in_specs=[VMEM_SPEC] * 2,
        out_specs=VMEM_SPEC,
        compiler_params=pltpu.CompilerParams(vmem_limit_bytes=4 << 20),
        cost_estimate=SHORT,
    )(in_vmem(decoder), in_vmem(signal))


def misfit_kernel(*refs):
    mine_ref, other_ref, goal_ref = refs[:3]
    rest, out_ref = refs[3:-1], refs[-1]
    width = mine_ref.shape[1]
    misfit = mine_ref[...].astype(f32) + other_ref[...].astype(f32) - goal_ref[...].astype(f32)
    loss = 0.5 * jnp.sum(misfit * misfit, keepdims=True)
    for ref in rest:
        loss = loss + jnp.sum(ref[...], keepdims=True)
    high = loss.astype(bf16).astype(f32)
    middle = (loss - high).astype(bf16).astype(f32)
    low = loss - high - middle
    lane = lax.broadcasted_iota(jnp.int32, (out_ref.shape[0], PAD), 1)
    tail = jnp.where(lane == 0, high, jnp.where(lane == 1, middle, jnp.where(lane == 2, low, 0.0)))
    out_ref[:, :width] = misfit.astype(bf16)
    out_ref[:, width:] = tail.astype(bf16)


def misfits(mine, other, goal, rest):
    rows, width = mine.shape
    operands = (mine, other, goal, *rest)
    return pl.pallas_call(
        misfit_kernel,
        out_shape=pltpu.VMEM((rows, width + PAD), bf16),
        in_specs=[VMEM_SPEC] * len(operands),
        out_specs=VMEM_SPEC,
        compiler_params=pltpu.CompilerParams(vmem_limit_bytes=8 << 20),
        cost_estimate=SHORT,
    )(*[in_vmem(x) for x in operands])


def loss_kernel(scale, *refs):
    pieces, out_ref = refs[:-1], refs[-1]
    total = jnp.zeros((1, 1), f32)
    for ref in pieces:
        tail = ref[:, ref.shape[1] - PAD :].astype(f32)
        total = total + jnp.sum(tail, keepdims=True)
    out_ref[...] = jnp.broadcast_to(total * scale, out_ref.shape)


def group_loss(pieces, block_rows):
    return pl.pallas_call(
        functools.partial(loss_kernel, 1.0 / block_rows),
        out_shape=pltpu.VMEM((8, PAD), f32),
        in_specs=[VMEM_SPEC] * len(pieces),
        out_specs=VMEM_SPEC,
        compiler_params=pltpu.CompilerParams(vmem_limit_bytes=8 << 20),
        cost_estimate=SHORT,
    )(*[in_vmem(x) for x in pieces])


def body(residual, targets, w_enc, b_enc, w_dec, block_mask):
    row_count = residual.shape[1]
    width = residual.shape[2]
    layers = lax.axis_size("layer")
    feats = lax.axis_size("feat")
    tokens = row_count * feats
    ring = Ring(feats)
    device = lax.axis_index("feat")
    first_core = device % 2 == 0
    halves = 2 if row_count % 16 == 0 else 1
    rows = row_count // halves
    block_rows = 2 * rows

    tokens_of = ring.owners[:, None, :, None] * row_count + np.arange(halves)[:, None, None] * rows + np.arange(rows)
    table = jnp.asarray((tokens_of // TBLOCK).reshape(feats, 1, -1).astype(np.float32))

    own = residual[0]
    other = ring.across(own)
    token_block, own = start(table, own)
    other, first_core = lax.optimization_barrier((other, first_core))
    goal = after(targets[0], own)
    goal = lax.ppermute(goal, "layer", [(i, (i - 1) % layers) for i in range(layers)])
    held = {}

    def keep_in(ended):
        held["keep"] = keeps(block_mask[0], token_block, own_blocks[0], halves)
        return [goal, *held["keep"]]

    def encoder_in(ended):
        held["encoder"] = loaded(w_enc[0], ended[-1][0])
        return [held["encoder"]]

    def decoder_in(ended):
        held["decoder"] = loaded(w_dec[0], ended[-1][1])
        return [held["decoder"]]

    own_blocks = chip_blocks(own, other, halves)
    pins = {2: keep_in, 3: encoder_in, 4: decoder_in}
    gathered = gather(ring, own_blocks, pins, True)
    encoder, decoder = held["encoder"], held["decoder"]

    acts, gates, shares, sums = [], [], [], []
    for h in range(halves):
        act, gate, act_sum, share = forward(ring, gathered[h], encoder, b_enc, held["keep"][h], decoder)
        acts.append(act)
        gates.append(gate)
        shares.append(share)
        sums.append(act_sum)
    act_sum = sum(sums[1:], sums[0])

    def goals_in(ended):
        other_goal = ring.across(after(goal, ended[-1][0]))
        held["goal"] = chip_blocks(goal, other_goal, halves)
        return list(held["goal"])

    def norm_in(ended):
        held["norm"] = norms(decoder, ended[-1][0])
        return [held["norm"]]

    def rows_in(ended):
        penalty = penalty_weight * act_sum * held["norm"]
        held["rest"] = [penalty, ring.across(penalty)]
        held["turned"] = [turned(after(parts, ended[-1][1])) for parts in gathered]
        return held["turned"] + held["rest"]

    pins = {3: lambda ended: goals_in(ended) + norm_in(ended), 4: rows_in}
    summed = scatter_sums(ring, first_core, block_rows, shares, pins)
    norm = held["norm"]
    rest = held["rest"]
    payloads = [misfits(*summed[h], held["goal"][h], rest if h == 0 else []) for h in range(halves)]
    errors = gather(ring, payloads, {}, False)
    turned_rows = held["turned"]
    sent_loss = loss_row = group_loss([piece for parts in errors for piece in parts], block_rows)
    for _ in range(layers - 1):
        sent_loss = lax.ppermute(sent_loss, "layer", [(i, (i + 1) % layers) for i in range(layers)])
        loss_row = loss_row + sent_loss
    enc_grad, bias_grad, dec_grad = backward(errors, acts, gates, turned_rows, decoder, norm, act_sum)
    loss = after(loss_row, bias_grad)[0, 0] / (layers * tokens * width)
    return enc_grad[None], bias_grad, dec_grad[None], loss


def solution(mesh):
    return jax.shard_map(
        body,
        mesh=mesh,
        in_specs=(
            P("layer", "feat", None),
            P("layer", "feat", None),
            P("layer", None, "feat"),
            P("layer", "feat"),
            P("layer", "feat", None),
            P("layer", None, "feat"),
        ),
        out_specs=(P("layer", None, "feat"), P("layer", "feat"), P("layer", "feat", None), P()),
        check_vma=False,
    )
```

time: 87.4 us -> 84.1 us (0.962)
  Pallas kernels: 12.3 us -> 16.9 us
  starting transfers between devices: 44.3 us -> 39.9 us
  local copies, waits for them, and re-layouts: 4.5 us -> 1.2 us
  waiting for transfers between devices: 20.8 us -> 22.7 us
  other arithmetic: 2.32 us -> 0.49 us
    ppermute x24, starting transfers between devices: 40.1 us -> 33.8 us  [along(): return lax.ppermute(block, 'feat', self.step)]
    pallas_call x3 -> x9, Pallas kernels: 3.14 us -> 7.72 us  [the longest x2 4.44 us: loaded(): pl.pallas_call(load_kernel, out_shape=pltpu.VMEM(array.shape, array.dtype...]
    ppermute x24, waiting for transfers between devices: 19.8 us -> 22.5 us  [along(): return lax.ppermute(block, 'feat', self.step)]
    unnamed x18 -> x4, local copies, waits for them, and re-layouts: 3 us -> 0.68 us
    select_n x4 -> x2, other arithmetic: 1.14 us -> 0.03 us  [scatter_sums(): jnp.where(first_core, came, nothing)]
    ppermute x1, starting transfers between devices: 1.53 us -> 2.6 us  [body(): lax.ppermute(goal, 'layer', [(i, (i - 1) % layers) for i in range(layers)])]
    squeeze x3 -> x0, local copies, waits for them, and re-layouts: 0.9 us -> none  [body(): token_blocks[h]]
    ppermute x11 -> x19, starting transfers between devices: 1.64 us -> 2.41 us  [across(): return lax.ppermute(block, 'feat', self.twin)]
  transfers between devices with their start and end apart: 37 -> 45, of which waited for: 22 -> 20; matrix products, arithmetic and copies ran while one was open for 3% -> 1% of each run, Pallas kernels for 14% -> 18%
where the time goes in v4:
time: 84.1 us; the launch traced here: 83.9 us
  starting transfers between devices  39.9 us (47%)
  waiting for transfers between devices  22.7 us (27%)
  Pallas kernels  16.9 us (20%)
  between operations  2.72 us (3%)
  local copies, waits for them, and re-layouts  1.2 us (1%)
    ppermute x24, starting transfers between devices, along(): return lax.ppermute(block, 'feat', self.step)  33.8 us
    ppermute x24, waiting for transfers between devices, along(): return lax.ppermute(block, 'feat', self.step)  22.5 us
    pallas_call x1, Pallas kernels, backward(): pl.pallas_call(functools.partial(backward_kernel, tuple((len(e) for e in...  5.55 us
    pallas_call x2, Pallas kernels, loaded(): pl.pallas_call(load_kernel, out_shape=pltpu.VMEM(array.shape, array.dtype...  4.44 us
    pallas_call x2, Pallas kernels, forward(): pl.pallas_call(functools.partial(forward_kernel, len(pieces), min(512, wi...  2.84 us
    ppermute x1, starting transfers between devices, body(): lax.ppermute(goal, 'layer', [(i, (i - 1) % layers) for i in range(layers)])  2.6 us
    ppermute x19, starting transfers between devices, across(): return lax.ppermute(block, 'feat', self.twin)  2.41 us
  transfers between devices with their start and end apart: 45, of which 20 were waited for; matrix products, arithmetic and copies ran while one was open for 1% of the time, Pallas kernels for 18%

profile of v4, /device:TPU:0, one launch (start us, length us, event | category | flops | bytes accessed | tf_op | source)
XLA Modules:
  0.0 83.9 jit_solution(14528382104211985783)
XLA Ops:
  2.1 2.6 %collective-permute-start.2 = (bf16[16,4096]{1,0:T(8,128)(2,1)}, bf16[16,4096]{1,0:T(8,128)(2,1)S(1)}, u32[]{:S(2)}, u32[]{:S(2)}) collective-permute-start(bf16[16,4096]{1,0:T(8,128)(2,1)} %bitcast.15), channel_id=1, source_target_pairs={{0,16},{16,0},{1,17},{17,1},{2,18},{18,2},{3,19},{19,3},{4,20},{20... | collective-permute-start | bytes 393224 | tf_op jit(solution)/shard_map/ppermute | solution.py:484
  4.8 1.6 %collective-permute-start.1 = (bf16[16,4096]{1,0:T(8,128)(2,1)S(1)}, bf16[16,4096]{1,0:T(8,128)(2,1)S(1)}, u32[]{:S(2)}, u32[]{:S(2)}) collective-permute-start(bf16[16,4096]{1,0:T(8,128)(2,1)S(1)} %get-tuple-element.132.signal_ref.refs_0_), channel_id=1, source_target_pairs={{0,4},{1,3},{2,0},{3,7},{4,8},{5,1},{6,2},{7,11},{8,12},{9,5},{10,... | collective-permute-start | bytes 393224 | tf_op jit(solution)/shard_map/ppermute | solution.py:43
  6.4 1.6 %collective-permute-start.5 = (bf16[16,4096]{1,0:T(8,128)(2,1)S(1)}, bf16[16,4096]{1,0:T(8,128)(2,1)S(1)}, u32[]{:S(2)}, u32[]{:S(2)}) collective-permute-start(bf16[16,4096]{1,0:T(8,128)(2,1)S(1)} %get-tuple-element.140.refs_0_), channel_id=1, source_target_pairs={{0,4},{1,3},{2,0},{3,7},{4,8},{5,1},{6,2},{7,11},{8,12},{9,5},{10,... | collective-permute-start | bytes 393224 | tf_op jit(solution)/shard_map/ppermute | solution.py:43
  9.8 1.6 %collective-permute-start.3 = (bf16[16,4096]{1,0:T(8,128)(2,1)S(1)}, bf16[16,4096]{1,0:T(8,128)(2,1)S(1)}, u32[]{:S(2)}, u32[]{:S(2)}) collective-permute-start(bf16[16,4096]{1,0:T(8,128)(2,1)S(1)} %collective-permute-done.1.refs_1_), channel_id=1, source_target_pairs={{0,4},{1,3},{2,0},{3,7},{4,8},{5,1},{6,2},{7,11},{8,12},{9,5},{10,... | collective-permute-start | bytes 393224 | tf_op jit(solution)/shard_map/ppermute | solution.py:43
  11.4 1.6 %collective-permute-start.9 = (bf16[16,4096]{1,0:T(8,128)(2,1)S(1)}, bf16[16,4096]{1,0:T(8,128)(2,1)S(1)}, u32[]{:S(2)}, u32[]{:S(2)}) collective-permute-start(bf16[16,4096]{1,0:T(8,128)(2,1)S(1)} %collective-permute-done.5.signal_ref.refs_1_), channel_id=1, source_target_pairs={{0,4},{1,3},{2,0},{3,7},{4,8},{5,1},{6,2},{7,11},{8,12},{9,5},{10,... | collective-permute-start | bytes 393224 | tf_op jit(solution)/shard_map/ppermute | solution.py:43
  12.9 2.2 %shard_map.105.refs_8_ = bf16[4096,512]{1,0:T(8,128)(2,1)S(1)} custom-call(bf16[4096,512]{1,0:T(8,128)(2,1)} %bitcast.9, bf16[16,4096]{1,0:T(8,128)(2,1)S(1)} %collective-permute-done.5.signal_ref.refs_1_), custom_call_target="tpu_custom_call" | custom-call | tf_op jit(solution)/shard_map/pallas_call | solution.py:358
  15.2 1.6 %collective-permute-start.6 = (bf16[16,4096]{1,0:T(8,128)(2,1)S(1)}, bf16[16,4096]{1,0:T(8,128)(2,1)S(1)}, u32[]{:S(2)}, u32[]{:S(2)}) collective-permute-start(bf16[16,4096]{1,0:T(8,128)(2,1)S(1)} %collective-permute-done.3.refs_2_), channel_id=1, source_target_pairs={{0,4},{1,3},{2,0},{3,7},{4,8},{5,1},{6,2},{7,11},{8,12},{9,5},{10,... | collective-permute-start | bytes 393224 | tf_op jit(solution)/shard_map/ppermute | solution.py:43
  16.8 1.5 %collective-permute-start.12 = (bf16[16,4096]{1,0:T(8,128)(2,1)S(1)}, bf16[16,4096]{1,0:T(8,128)(2,1)S(1)}, u32[]{:S(2)}, u32[]{:S(2)}) collective-permute-start(bf16[16,4096]{1,0:T(8,128)(2,1)S(1)} %collective-permute-done.9.signal_ref.refs_2_), channel_id=1, source_target_pairs={{0,4},{1,3},{2,0},{3,7},{4,8},{5,1},{6,2},{7,11},{8,12},{9,5},{10,... | collective-permute-start | bytes 393224 | tf_op jit(solution)/shard_map/ppermute | solution.py:43
  18.4 2.2 %shard_map.106.refs_11_.dec_ref.refs_22_ = bf16[512,4096]{1,0:T(8,128)(2,1)S(1)} custom-call(bf16[512,4096]{1,0:T(8,128)(2,1)} %bitcast.10, bf16[16,4096]{1,0:T(8,128)(2,1)S(1)} %collective-permute-done.9.signal_ref.refs_2_), custom_call_target="tpu_custom_call" | custom-call | tf_op jit(solution)/shard_map/pallas_call | solution.py:358
  20.6 1.4 %collective-permute-start.10 = (bf16[16,4096]{1,0:T(8,128)(2,1)S(1)}, bf16[16,4096]{1,0:T(8,128)(2,1)S(1)}, u32[]{:S(2)}, u32[]{:S(2)}) collective-permute-start(bf16[16,4096]{1,0:T(8,128)(2,1)S(1)} %collective-permute-done.6.refs_3_), channel_id=1, source_target_pairs={{0,4},{1,3},{2,0},{3,7},{4,8},{5,1},{6,2},{7,11},{8,12},{9,5},{10,... | collective-permute-start | bytes 393224 | tf_op jit(solution)/shard_map/ppermute | solution.py:43
  23.9 1.8 %collective-permute-done.10.refs_7_ = bf16[16,4096]{1,0:T(8,128)(2,1)S(1)} collective-permute-done((bf16[16,4096]{1,0:T(8,128)(2,1)S(1)}, bf16[16,4096]{1,0:T(8,128)(2,1)S(1)}, u32[]{:S(2)}, u32[]{:S(2)}) %collective-permute-start.10) | collective-permute-done | bytes 131104 | tf_op jit(solution)/shard_map/ppermute | solution.py:43
  25.7 1.9 %collective-permute-done.15.refs_7_ = bf16[16,4096]{1,0:T(8,128)(2,1)S(1)} collective-permute-done((bf16[16,4096]{1,0:T(8,128)(2,1)S(1)}, bf16[16,4096]{1,0:T(8,128)(2,1)S(1)}, u32[]{:S(2)}, u32[]{:S(2)}) %collective-permute-start.15) | collective-permute-done | bytes 131104 | tf_op jit(solution)/shard_map/ppermute | solution.py:43
  27.6 1.4 %shard_map.107 = (bf16[128,512]{1,0:T(8,128)(2,1)S(1)}, f32[128,512]{1,0:T(8,128)S(1)}, f32[1,512]{1,0:T(1,128)S(1)}, f32[16,4096]{1,0:T(8,128)S(1)}, bf16[64,40...) custom-call(bf16[16,4096]{1,0:T(8,128)(2,1)S(1)} %get-tuple-element.132.signal_ref.refs_0_, ...), custom_call_target="tpu_custom_call" | custom-call | tf_op jit(solution)/shard_map/pallas_call | solution.py:214
  29.1 1.4 %shard_map.108 = (bf16[128,512]{1,0:T(8,128)(2,1)S(1)}, f32[128,512]{1,0:T(8,128)S(1)}, f32[1,512]{1,0:T(1,128)S(1)}, f32[16,4096]{1,0:T(8,128)S(1)}, bf16[64,40...) custom-call(bf16[16,4096]{1,0:T(8,128)(2,1)S(1)} %get-tuple-element.140.refs_0_, ...), custom_call_target="tpu_custom_call" | custom-call | tf_op jit(solution)/shard_map/pallas_call | solution.py:214
  34.0 1.5 %collective-permute-done.17 = bf16[8,4096]{1,0:T(8,128)(2,1)S(1)} collective-permute-done((bf16[8,4096]{1,0:T(8,128)(2,1)S(1)}, bf16[8,4096]{1,0:T(8,128)(2,1)S(1)}, u32[]{:S(2)}, u32[]{:S(2)}) %collective-permute-start.17) | collective-permute-done | bytes 65568 | tf_op jit(solution)/shard_map/ppermute | solution.py:43
  44.1 1.5 %collective-permute-done.22 = bf16[16,4096]{1,0:T(8,128)(2,1)S(1)} collective-permute-done((bf16[16,4096]{1,0:T(8,128)(2,1)S(1)}, bf16[16,4096]{1,0:T(8,128)(2,1)S(1)}, u32[]{:S(2)}, u32[]{:S(2)}) %collective-permute-start.22) | collective-permute-done | bytes 131104 | tf_op jit(solution)/shard_map/ppermute | solution.py:43
  48.6 2.2 %collective-permute-done.25 = bf16[16,4096]{1,0:T(8,128)(2,1)S(1)} collective-permute-done((bf16[16,4096]{1,0:T(8,128)(2,1)S(1)}, bf16[16,4096]{1,0:T(8,128)(2,1)S(1)}, u32[]{:S(2)}, u32[]{:S(2)}) %collective-permute-start.25) | collective-permute-done | bytes 131104 | tf_op jit(solution)/shard_map/ppermute | solution.py:43
  54.2 1.4 %collective-permute-start.33 = (bf16[16,4224]{1,0:T(8,128)(2,1)S(1)}, bf16[16,4224]{1,0:T(8,128)(2,1)S(1)}, u32[]{:S(2)}, u32[]{:S(2)}) collective-permute-start(bf16[16,4224]{1,0:T(8,128)(2,1)S(1)} %shard_map.114.refs_8_), channel_id=1, source_target_pairs={{0,4},{1,3},{2,0},{3,7},{4,8},{5,1},{6,2},{7,11},{8,12},{9,5},{10,... | collective-permute-start | bytes 405512 | tf_op jit(solution)/shard_map/ppermute | solution.py:43
  55.6 2.0 %collective-permute-done.27.refs_1_ = bf16[16,4224]{1,0:T(8,128)(2,1)S(1)} collective-permute-done((bf16[16,4224]{1,0:T(8,128)(2,1)S(1)}, bf16[16,4224]{1,0:T(8,128)(2,1)S(1)}, u32[]{:S(2)}, u32[]{:S(2)}) %collective-permute-start.27) | collective-permute-done | bytes 135200 | tf_op jit(solution)/shard_map/ppermute | solution.py:43
  60.6 2.0 %collective-permute-done.28.refs_2_ = bf16[16,4224]{1,0:T(8,128)(2,1)S(1)} collective-permute-done((bf16[16,4224]{1,0:T(8,128)(2,1)S(1)}, bf16[16,4224]{1,0:T(8,128)(2,1)S(1)}, u32[]{:S(2)}, u32[]{:S(2)}) %collective-permute-start.28) | collective-permute-done | bytes 135200 | tf_op jit(solution)/shard_map/ppermute | solution.py:43
  65.7 2.0 %collective-permute-done.34.refs_3_ = bf16[16,4224]{1,0:T(8,128)(2,1)S(1)} collective-permute-done((bf16[16,4224]{1,0:T(8,128)(2,1)S(1)}, bf16[16,4224]{1,0:T(8,128)(2,1)S(1)}, u32[]{:S(2)}, u32[]{:S(2)}) %collective-permute-start.34) | collective-permute-done | bytes 135200 | tf_op jit(solution)/shard_map/ppermute | solution.py:43
  71.2 1.5 %collective-permute-done.38.refs_7_ = bf16[16,4224]{1,0:T(8,128)(2,1)S(1)} collective-permute-done((bf16[16,4224]{1,0:T(8,128)(2,1)S(1)}, bf16[16,4224]{1,0:T(8,128)(2,1)S(1)}, u32[]{:S(2)}, u32[]{:S(2)}) %collective-permute-start.38) | collective-permute-done | bytes 135200 | tf_op jit(solution)/shard_map/ppermute | solution.py:43
  72.7 2.1 %collective-permute-done.43.refs_15_ = bf16[16,4224]{1,0:T(8,128)(2,1)S(1)} collective-permute-done((bf16[16,4224]{1,0:T(8,128)(2,1)S(1)}, bf16[16,4224]{1,0:T(8,128)(2,1)S(1)}, u32[]{:S(2)}, u32[]{:S(2)}) %collective-permute-start.43) | collective-permute-done | bytes 135200 | tf_op jit(solution)/shard_map/ppermute | solution.py:43
  76.0 5.6 %shard_map.115 = (bf16[4096,512]{1,0:T(8,128)(2,1)}, f32[1,512]{1,0:T(1,128)}, bf16[512,4096]{1,0:T(8,128)(2,1)}) custom-call(bf16[16,4224]{1,0:T(8,128)(2,1)S(1)} %shard_map.113.refs_0_, bf16[16,4224]{1,0:T(8,128)(2,1)S(1)} %collective-permute-done.27.refs_1_, bf16[16,4224]{1,0:T(8,128)(2,1)S(1)} %collective-permute-done.28.refs_2_, ...), custom_call_target="tpu_custom_call" | custom-call | tf_op jit(solution)/shard_map/pallas_call | solution.py:301
  (102 shorter events, 34.7 us)
Async XLA Ops:
  2.1 7.4 %collective-permute-start.2 = (bf16[16,4096]{1,0:T(8,128)(2,1)}, bf16[16,4096]{1,0:T(8,128)(2,1)S(1)}, u32[]{:S(2)}, u32[]{:S(2)}) collective-permute-start(bf16[16,4096]{1,0:T(8,128)(2,1)} %bitcast.15), channel_id=1, source_target_pairs={{0,16},{16,0},{1,17},{17,1},{2,18},{18,2},{3,19},{19,3},{4,20},{20... | collective-permute-start | bytes 393224 | tf_op jit(solution)/shard_map/ppermute | solution.py:484
  4.8 5.0 %collective-permute-start.1 = (bf16[16,4096]{1,0:T(8,128)(2,1)S(1)}, bf16[16,4096]{1,0:T(8,128)(2,1)S(1)}, u32[]{:S(2)}, u32[]{:S(2)}) collective-permute-start(bf16[16,4096]{1,0:T(8,128)(2,1)S(1)} %get-tuple-element.132.signal_ref.refs_0_), channel_id=1, source_target_pairs={{0,4},{1,3},{2,0},{3,7},{4,8},{5,1},{6,2},{7,11},{8,12},{9,5},{10,... | collective-permute-start | bytes 393224 | tf_op jit(solution)/shard_map/ppermute | solution.py:43
  6.4 5.0 %collective-permute-start.5 = (bf16[16,4096]{1,0:T(8,128)(2,1)S(1)}, bf16[16,4096]{1,0:T(8,128)(2,1)S(1)}, u32[]{:S(2)}, u32[]{:S(2)}) collective-permute-start(bf16[16,4096]{1,0:T(8,128)(2,1)S(1)} %get-tuple-element.140.refs_0_), channel_id=1, source_target_pairs={{0,4},{1,3},{2,0},{3,7},{4,8},{5,1},{6,2},{7,11},{8,12},{9,5},{10,... | collective-permute-start | bytes 393224 | tf_op jit(solution)/shard_map/ppermute | solution.py:43
  9.8 5.4 %collective-permute-start.3 = (bf16[16,4096]{1,0:T(8,128)(2,1)S(1)}, bf16[16,4096]{1,0:T(8,128)(2,1)S(1)}, u32[]{:S(2)}, u32[]{:S(2)}) collective-permute-start(bf16[16,4096]{1,0:T(8,128)(2,1)S(1)} %collective-permute-done.1.refs_1_), channel_id=1, source_target_pairs={{0,4},{1,3},{2,0},{3,7},{4,8},{5,1},{6,2},{7,11},{8,12},{9,5},{10,... | collective-permute-start | bytes 393224 | tf_op jit(solution)/shard_map/ppermute | solution.py:43
  11.4 5.5 %collective-permute-start.9 = (bf16[16,4096]{1,0:T(8,128)(2,1)S(1)}, bf16[16,4096]{1,0:T(8,128)(2,1)S(1)}, u32[]{:S(2)}, u32[]{:S(2)}) collective-permute-start(bf16[16,4096]{1,0:T(8,128)(2,1)S(1)} %collective-permute-done.5.signal_ref.refs_1_), channel_id=1, source_target_pairs={{0,4},{1,3},{2,0},{3,7},{4,8},{5,1},{6,2},{7,11},{8,12},{9,5},{10,... | collective-permute-start | bytes 393224 | tf_op jit(solution)/shard_map/ppermute | solution.py:43
  15.2 5.4 %collective-permute-start.6 = (bf16[16,4096]{1,0:T(8,128)(2,1)S(1)}, bf16[16,4096]{1,0:T(8,128)(2,1)S(1)}, u32[]{:S(2)}, u32[]{:S(2)}) collective-permute-start(bf16[16,4096]{1,0:T(8,128)(2,1)S(1)} %collective-permute-done.3.refs_2_), channel_id=1, source_target_pairs={{0,4},{1,3},{2,0},{3,7},{4,8},{5,1},{6,2},{7,11},{8,12},{9,5},{10,... | collective-permute-start | bytes 393224 | tf_op jit(solution)/shard_map/ppermute | solution.py:43
  16.8 5.3 %collective-permute-start.12 = (bf16[16,4096]{1,0:T(8,128)(2,1)S(1)}, bf16[16,4096]{1,0:T(8,128)(2,1)S(1)}, u32[]{:S(2)}, u32[]{:S(2)}) collective-permute-start(bf16[16,4096]{1,0:T(8,128)(2,1)S(1)} %collective-permute-done.9.signal_ref.refs_2_), channel_id=1, source_target_pairs={{0,4},{1,3},{2,0},{3,7},{4,8},{5,1},{6,2},{7,11},{8,12},{9,5},{10,... | collective-permute-start | bytes 393224 | tf_op jit(solution)/shard_map/ppermute | solution.py:43
  20.6 5.0 %collective-permute-start.10 = (bf16[16,4096]{1,0:T(8,128)(2,1)S(1)}, bf16[16,4096]{1,0:T(8,128)(2,1)S(1)}, u32[]{:S(2)}, u32[]{:S(2)}) collective-permute-start(bf16[16,4096]{1,0:T(8,128)(2,1)S(1)} %collective-permute-done.6.refs_3_), channel_id=1, source_target_pairs={{0,4},{1,3},{2,0},{3,7},{4,8},{5,1},{6,2},{7,11},{8,12},{9,5},{10,... | collective-permute-start | bytes 393224 | tf_op jit(solution)/shard_map/ppermute | solution.py:43
  35.5 5.0 %collective-permute-start.18 = (bf16[16,4096]{1,0:T(8,128)(2,1)S(1)}, bf16[16,4096]{1,0:T(8,128)(2,1)S(1)}, u32[]{:S(2)}, u32[]{:S(2)}) collective-permute-start(bf16[16,4096]{1,0:T(8,128)(2,1)S(1)} %add_convert_fusion.7), channel_id=1, source_target_pairs={{0,4},{1,3},{2,0},{3,7},{4,8},{5,1},{6,2},{7,11},{8,12},{9,5},{10,... | collective-permute-start | bytes 393224 | tf_op jit(solution)/shard_map/ppermute | solution.py:43
  37.0 5.0 %collective-permute-start.23 = (bf16[16,4096]{1,0:T(8,128)(2,1)S(1)}, bf16[16,4096]{1,0:T(8,128)(2,1)S(1)}, u32[]{:S(2)}, u32[]{:S(2)}) collective-permute-start(bf16[16,4096]{1,0:T(8,128)(2,1)S(1)} %add_convert_fusion.4), channel_id=1, source_target_pairs={{0,4},{1,3},{2,0},{3,7},{4,8},{5,1},{6,2},{7,11},{8,12},{9,5},{10,... | collective-permute-start | bytes 393224 | tf_op jit(solution)/shard_map/ppermute | solution.py:43
  39.3 6.5 %collective-permute-start.24 = (f32[1,512]{1,0:T(1,128)S(1)}, f32[1,512]{1,0:T(1,128)S(1)}, u32[]{:S(2)}, u32[]{:S(2)}) collective-permute-start(f32[1,512]{1,0:T(1,128)S(1)} %get-tuple-element.170.refs_3_), channel_id=1, source_target_pairs={{0,1},{1,0},{2,3},{3,2},{4,5},{5,4},{6,7},{7,6},{8,9},{9,8},{10,11... | collective-permute-start | bytes 6152 | tf_op jit(solution)/shard_map/ppermute | solution.py:46
  40.7 5.0 %collective-permute-start.22 = (bf16[16,4096]{1,0:T(8,128)(2,1)S(1)}, bf16[16,4096]{1,0:T(8,128)(2,1)S(1)}, u32[]{:S(2)}, u32[]{:S(2)}) collective-permute-start(bf16[16,4096]{1,0:T(8,128)(2,1)S(1)} %add_convert_fusion.6), channel_id=1, source_target_pairs={{0,4},{1,3},{2,0},{3,7},{4,8},{5,1},{6,2},{7,11},{8,12},{9,5},{10,... | collective-permute-start | bytes 393224 | tf_op jit(solution)/shard_map/ppermute | solution.py:43
  42.1 5.0 %collective-permute-start.30 = (bf16[16,4096]{1,0:T(8,128)(2,1)S(1)}, bf16[16,4096]{1,0:T(8,128)(2,1)S(1)}, u32[]{:S(2)}, u32[]{:S(2)}) collective-permute-start(bf16[16,4096]{1,0:T(8,128)(2,1)S(1)} %add_convert_fusion.2), channel_id=1, source_target_pairs={{0,4},{1,3},{2,0},{3,7},{4,8},{5,1},{6,2},{7,11},{8,12},{9,5},{10,... | collective-permute-start | bytes 393224 | tf_op jit(solution)/shard_map/ppermute | solution.py:43
  45.8 5.0 %collective-permute-start.25 = (bf16[16,4096]{1,0:T(8,128)(2,1)S(1)}, bf16[16,4096]{1,0:T(8,128)(2,1)S(1)}, u32[]{:S(2)}, u32[]{:S(2)}) collective-permute-start(bf16[16,4096]{1,0:T(8,128)(2,1)S(1)} %add_convert_fusion.5), channel_id=1, source_target_pairs={{0,4},{1,3},{2,0},{3,7},{4,8},{5,1},{6,2},{7,11},{8,12},{9,5},{10,... | collective-permute-start | bytes 393224 | tf_op jit(solution)/shard_map/ppermute | solution.py:43
  47.2 5.0 %collective-permute-start.31 = (bf16[16,4096]{1,0:T(8,128)(2,1)S(1)}, bf16[16,4096]{1,0:T(8,128)(2,1)S(1)}, u32[]{:S(2)}, u32[]{:S(2)}) collective-permute-start(bf16[16,4096]{1,0:T(8,128)(2,1)S(1)} %add_convert_fusion.1), channel_id=1, source_target_pairs={{0,4},{1,3},{2,0},{3,7},{4,8},{5,1},{6,2},{7,11},{8,12},{9,5},{10,... | collective-permute-start | bytes 393224 | tf_op jit(solution)/shard_map/ppermute | solution.py:43
  52.6 5.1 %collective-permute-start.27 = (bf16[16,4224]{1,0:T(8,128)(2,1)S(1)}, bf16[16,4224]{1,0:T(8,128)(2,1)S(1)}, u32[]{:S(2)}, u32[]{:S(2)}) collective-permute-start(bf16[16,4224]{1,0:T(8,128)(2,1)S(1)} %shard_map.113.refs_0_), channel_id=1, source_target_pairs={{0,4},{1,3},{2,0},{3,7},{4,8},{5,1},{6,2},{7,11},{8,12},{9,5},{10,... | collective-permute-start | bytes 405512 | tf_op jit(solution)/shard_map/ppermute | solution.py:43
  54.2 5.1 %collective-permute-start.33 = (bf16[16,4224]{1,0:T(8,128)(2,1)S(1)}, bf16[16,4224]{1,0:T(8,128)(2,1)S(1)}, u32[]{:S(2)}, u32[]{:S(2)}) collective-permute-start(bf16[16,4224]{1,0:T(8,128)(2,1)S(1)} %shard_map.114.refs_8_), channel_id=1, source_target_pairs={{0,4},{1,3},{2,0},{3,7},{4,8},{5,1},{6,2},{7,11},{8,12},{9,5},{10,... | collective-permute-start | bytes 405512 | tf_op jit(solution)/shard_map/ppermute | solution.py:43
  57.7 5.0 %collective-permute-start.28 = (bf16[16,4224]{1,0:T(8,128)(2,1)S(1)}, bf16[16,4224]{1,0:T(8,128)(2,1)S(1)}, u32[]{:S(2)}, u32[]{:S(2)}) collective-permute-start(bf16[16,4224]{1,0:T(8,128)(2,1)S(1)} %collective-permute-done.27.refs_1_), channel_id=1, source_target_pairs={{0,4},{1,3},{2,0},{3,7},{4,8},{5,1},{6,2},{7,11},{8,12},{9,5},{10,... | collective-permute-start | bytes 405512 | tf_op jit(solution)/shard_map/ppermute | solution.py:43
  59.3 5.0 %collective-permute-start.37 = (bf16[16,4224]{1,0:T(8,128)(2,1)S(1)}, bf16[16,4224]{1,0:T(8,128)(2,1)S(1)}, u32[]{:S(2)}, u32[]{:S(2)}) collective-permute-start(bf16[16,4224]{1,0:T(8,128)(2,1)S(1)} %collective-permute-done.33.refs_9_), channel_id=1, source_target_pairs={{0,4},{1,3},{2,0},{3,7},{4,8},{5,1},{6,2},{7,11},{8,12},{9,5},{10,... | collective-permute-start | bytes 405512 | tf_op jit(solution)/shard_map/ppermute | solution.py:43
  62.7 5.0 %collective-permute-start.34 = (bf16[16,4224]{1,0:T(8,128)(2,1)S(1)}, bf16[16,4224]{1,0:T(8,128)(2,1)S(1)}, u32[]{:S(2)}, u32[]{:S(2)}) collective-permute-start(bf16[16,4224]{1,0:T(8,128)(2,1)S(1)} %collective-permute-done.28.refs_2_), channel_id=1, source_target_pairs={{0,4},{1,3},{2,0},{3,7},{4,8},{5,1},{6,2},{7,11},{8,12},{9,5},{10,... | collective-permute-start | bytes 405512 | tf_op jit(solution)/shard_map/ppermute | solution.py:43
  64.3 5.0 %collective-permute-start.40 = (bf16[16,4224]{1,0:T(8,128)(2,1)S(1)}, bf16[16,4224]{1,0:T(8,128)(2,1)S(1)}, u32[]{:S(2)}, u32[]{:S(2)}) collective-permute-start(bf16[16,4224]{1,0:T(8,128)(2,1)S(1)} %collective-permute-done.37.refs_10_), channel_id=1, source_target_pairs={{0,4},{1,3},{2,0},{3,7},{4,8},{5,1},{6,2},{7,11},{8,12},{9,5},{10,... | collective-permute-start | bytes 405512 | tf_op jit(solution)/shard_map/ppermute | solution.py:43
  67.7 5.0 %collective-permute-start.38 = (bf16[16,4224]{1,0:T(8,128)(2,1)S(1)}, bf16[16,4224]{1,0:T(8,128)(2,1)S(1)}, u32[]{:S(2)}, u32[]{:S(2)}) collective-permute-start(bf16[16,4224]{1,0:T(8,128)(2,1)S(1)} %collective-permute-done.34.refs_3_), channel_id=1, source_target_pairs={{0,4},{1,3},{2,0},{3,7},{4,8},{5,1},{6,2},{7,11},{8,12},{9,5},{10,... | collective-permute-start | bytes 405512 | tf_op jit(solution)/shard_map/ppermute | solution.py:43
  69.8 5.0 %collective-permute-start.43 = (bf16[16,4224]{1,0:T(8,128)(2,1)S(1)}, bf16[16,4224]{1,0:T(8,128)(2,1)S(1)}, u32[]{:S(2)}, u32[]{:S(2)}) collective-permute-start(bf16[16,4224]{1,0:T(8,128)(2,1)S(1)} %collective-permute-done.40.refs_11_), channel_id=1, source_target_pairs={{0,4},{1,3},{2,0},{3,7},{4,8},{5,1},{6,2},{7,11},{8,12},{9,5},{10,... | collective-permute-start | bytes 405512 | tf_op jit(solution)/shard_map/ppermute | solution.py:43
  75.0 6.6 %collective-permute-start.44 = (f32[8,128]{1,0:T(8,128)S(1)}, f32[8,128]{1,0:T(8,128)S(1)}, u32[]{:S(2)}, u32[]{:S(2)}) collective-permute-start(f32[8,128]{1,0:T(8,128)S(1)} %shard_map.116), channel_id=1, source_target_pairs={{0,16},{16,0},{1,17},{17,1},{2,18},{18,2},{3,19},{19,3},{4,20},{20... | collective-permute-start | bytes 12296 | tf_op jit(solution)/shard_map/ppermute | solution.py:537
  (23 other events, 79.1 us)

commit v5 on v4

v5 whole, which is shorter than its diff:
```python
import functools

import jax
import jax.numpy as jnp
import numpy as np
from jax import lax
from jax.experimental import pallas as pl
from jax.experimental.pallas import tpu as pltpu
from jax.sharding import PartitionSpec as P

TBLOCK = 128
FBLOCK = 128
PAD = 128

penalty_weight = 0.5
norm_epsilon = 1e-06
f32 = jnp.float32
bf16 = jnp.bfloat16


class Ring:
    def __init__(self, size):
        chips = size // 2
        self.hops = (chips - 1) // 2
        self.far = chips % 2 == 0
        order = list(range(0, chips, 2)) + list(range(1, chips, 2))[::-1]
        place = {chip: at for at, chip in enumerate(order)}
        self.step = []
        owners = []
        for device in range(size):
            chip, core = divmod(device, 2)
            at = place[chip]
            ahead = 1 if core == 0 else -1
            self.step.append((device, order[(at + ahead) % chips] * 2 + core))
            behind = [order[(at - ahead * k) % chips] for k in range(1, self.hops + 1)]
            front = [order[(at + ahead * k) % chips] for k in range(1, self.hops + 1)]
            last = [order[(at + self.hops + 1) % chips]] if self.far else []
            owners.append([[2 * c + i for c in [chip] + behind + front + last] for i in (core, 1 - core)])
        self.owners = np.array(owners, np.int32)
        self.twin = [(device, device ^ 1) for device in range(size)]

    def along(self, block):
        return lax.ppermute(block, "feat", self.step)

    def across(self, block):
        return lax.ppermute(block, "feat", self.twin)


def after(value, *signals):
    return lax.optimization_barrier((value, *signals))[0]


class Turns:
    def __init__(self, pins, leading):
        self.ended = [[], []]
        self.pins = pins
        self.leading = leading

    def enter(self, chain, block):
        hop = len(self.ended[chain])
        signals = self.ended[1 - chain][hop - 2 : hop - 1] if hop >= 2 else []
        if chain == self.leading and hop + 1 in self.pins:
            signals = signals + self.pins[hop + 1](self.ended)
        return after(block, *signals)

    def leave(self, chain, block):
        self.ended[chain].append(block)


def gather(ring, mine, twins, pins, direct):
    turns = Turns(pins, 0)
    moving = [mine, twins]
    front = [[], []]
    for k in range(ring.hops + ring.far):
        for chain in (0, 1):
            if k == ring.hops and chain == 1 and not direct:
                continue
            block = after(moving[chain], front[chain][k - 2]) if k >= 2 else moving[chain]
            moving[chain] = ring.along(turns.enter(chain, block))
            turns.leave(chain, moving[chain])
            if k < ring.hops:
                front[chain].append(ring.across(moving[chain]))
    last = [[], []]
    if ring.far:
        last = [[moving[0]], [moving[1] if direct else ring.across(moving[0])]]
    parts = [
        [block] + turns.ended[chain][: ring.hops] + front[1 - chain] + last[chain]
        for chain, block in enumerate((mine, twins))
    ]
    if 0 in pins:
        parts = after(parts, *pins[0](turns.ended))
    return parts


def scatter_sums(ring, rows, shares, pins):
    turns = Turns(pins, 1)
    (own, sent, front, last), (own_twin, sent_twin, front_twin, _) = shares
    received = [ring.across(sent), ring.across(sent_twin)]
    arrived = [None, None]

    def send(chain, share, addend):
        total = share + addend.astype(f32)
        if arrived[chain] is not None:
            total = total + arrived[chain].astype(f32)
        arrived[chain] = ring.along(turns.enter(chain, total.astype(bf16)))
        turns.leave(chain, arrived[chain])

    def part(array, k):
        return array[rows * (k - 1) : rows * k]

    for k in range(ring.hops, -1, -1):
        if k > 0:
            send(0, part(front_twin, k), part(received[0], k))
        if k < ring.hops:
            send(1, part(front, k + 1), part(received[1], k + 1))
        elif ring.far:
            send(1, last, received[1][rows * ring.hops :])
    totals = []
    for share, came in ((own, arrived[1]), (own_twin, arrived[0])):
        totals.append((share if came is None else share + came.astype(f32)).astype(bf16))
    from_twin = [ring.across(total) for total in totals]
    return [(totals[0], from_twin[1]), (totals[1], from_twin[0])]


def in_vmem(x):
    return pltpu.with_memory_space_constraint(x, pltpu.VMEM)


def in_hbm(x):
    return pltpu.with_memory_space_constraint(x, pltpu.HBM)


VMEM_SPEC = pl.BlockSpec(memory_space=pltpu.VMEM)
ANY_SPEC = pl.BlockSpec(memory_space=pl.ANY)
HBM_SPEC = pl.BlockSpec(memory_space=pltpu.HBM)
SHORT = pl.CostEstimate(flops=0, bytes_accessed=0, transcendentals=0)
SMEM_SPEC = pl.BlockSpec(memory_space=pltpu.SMEM)


def stacked(refs, columns):
    return jnp.concatenate([ref[:, columns] for ref in refs], axis=0)


def whole_pieces(parts):
    if all(p.shape[0] % 16 == 0 for p in parts):
        return parts
    return [jnp.concatenate(parts, axis=0)]


def forward_kernel(count, step, *refs):
    pieces = refs[:count]
    enc_refs, dec_refs = refs[count : count + 2], refs[count + 2 : count + 4]
    bias_ref, keep_ref, act_ref, gate_ref, sum_ref = refs[count + 4 : count + 9]
    outs = refs[count + 9 :]
    width = dec_refs[0].shape[1]
    cut = width // 2
    preact = bias_ref[...]
    for i, enc_ref in enumerate(enc_refs):
        for at in range(0, cut, 512):
            preact = preact + jnp.dot(
                stacked(pieces, slice(i * cut + at, i * cut + at + 512)),
                enc_ref[at : at + 512, :],
                preferred_element_type=f32,
            )
    positive = jnp.maximum(preact, 0.0)
    keep = keep_ref[...]
    act = (keep * positive * positive).astype(bf16)
    act_ref[...] = act
    gate_ref[...] = keep * 2.0 * positive
    sum_ref[...] = jnp.sum(act.astype(f32), axis=0, keepdims=True)
    for at in range(0, width, step):
        columns = jnp.concatenate([ref[:, at : at + step] for ref in dec_refs], axis=0)
        part = jnp.dot(act, columns, preferred_element_type=f32)
        if len(outs) == 1:
            outs[0][:, at : at + step] = part
            continue
        own_ref, sent_ref, front_ref = outs[:3]
        rows, hop = own_ref.shape[0], front_ref.shape[0]
        own_ref[:, at : at + step] = part[:rows]
        sent_ref[:hop, at : at + step] = part[rows : rows + hop].astype(bf16)
        front_ref[:, at : at + step] = part[rows + hop : rows + 2 * hop]
        if len(outs) == 4:
            outs[3][:, at : at + step] = part[rows + 2 * hop :]
        else:
            sent_ref[hop:, at : at + step] = part[rows + 2 * hop :].astype(bf16)


def forward(ring, parts, encoder, bias, keep, decoder, keeps_last):
    pieces = whole_pieces(parts)
    rows, features = parts[0].shape[0], encoder[0].shape[1]
    total = sum(p.shape[0] for p in parts)
    hop = rows * ring.hops
    end = rows + 2 * hop
    width = decoder[0].shape[1]
    shapes = [((total, features), bf16), ((total, features), f32), ((1, features), f32)]
    apart = rows % 16 == 0 and ring.hops > 0 and ring.far
    if apart and keeps_last:
        shapes += [((rows, width), f32), ((hop, width), bf16), ((hop, width), f32), ((rows, width), f32)]
    elif apart:
        shapes += [((rows, width), f32), ((hop + rows, width), bf16), ((hop, width), f32)]
    else:
        shapes += [((total, width), f32)]
    outs = pl.pallas_call(
        functools.partial(forward_kernel, len(pieces), min(512, width)),
        out_shape=[pltpu.VMEM(shape, dtype) for shape, dtype in shapes],
        in_specs=[VMEM_SPEC] * (len(pieces) + 6),
        out_specs=[VMEM_SPEC] * len(shapes),
        compiler_params=pltpu.CompilerParams(vmem_limit_bytes=12 << 20),
        cost_estimate=SHORT,
    )(*[in_vmem(x) for x in (*pieces, *encoder, *decoder, bias, keep)])
    act, gate, act_sum = outs[:3]
    if apart:
        own, sent, front, *last = outs[3:]
        return act, gate, act_sum, (own, sent, front, last[0] if last else None)
    full = outs[3]
    sent = full[rows : rows + hop]
    if not keeps_last:
        sent = jnp.concatenate([sent, full[end:]], axis=0)
    return act, gate, act_sum, (full[:rows], sent.astype(bf16), full[rows + hop : end], full[end:])


def turn_kernel(*refs):
    pieces, out_ref = refs[:-1], refs[-1]
    step = 128 if out_ref.shape[0] % 128 == 0 else out_ref.shape[0]
    for at in range(0, out_ref.shape[0], step):
        out_ref[at : at + step, :] = stacked(pieces, slice(at, at + step)).T


def turned(parts):
    pieces = whole_pieces(parts)
    total = sum(p.shape[0] for p in pieces)
    width = pieces[0].shape[1]
    return pl.pallas_call(
        turn_kernel,
        out_shape=pltpu.VMEM((width, total), bf16),
        in_specs=[VMEM_SPEC] * len(pieces),
        out_specs=VMEM_SPEC,
        compiler_params=pltpu.CompilerParams(vmem_limit_bytes=12 << 20),
        cost_estimate=SHORT,
    )(*[in_vmem(x) for x in pieces])


def backward_kernel(counts, step, *refs):
    halves = len(counts)
    at = sum(counts)
    errors = refs[:at]
    acts, gates, rows = (refs[at + halves * i : at + halves * (i + 1)] for i in range(3))
    *dec_refs, norm_ref, sum_ref = refs[at + 3 * halves : at + 3 * halves + 4]
    enc_out, bias_out, dec_out = refs[at + 3 * halves + 4 : at + 3 * halves + 7]
    enc_stage, dec_stage, enc_sems, dec_sems = refs[at + 3 * halves + 7 :]
    features, width = dec_stage.shape
    turned_act = jnp.concatenate([a[...] for a in acts], axis=0).T
    coef = penalty_weight * sum_ref[...] / norm_ref[...]
    coef = jnp.broadcast_to(coef, (8, features)).T[:, :1]
    copies = []
    for i, at in enumerate(range(0, width, step)):
        columns = slice(at, at + step)
        grad = jnp.dot(turned_act, stacked(errors, columns), preferred_element_type=f32)
        grad = grad + coef * jnp.concatenate([ref[:, columns] for ref in dec_refs], axis=0).astype(f32)
        dec_stage[:, columns] = grad.astype(bf16)
        copy = pltpu.make_async_copy(dec_stage.at[:, columns], dec_out.at[:, columns], dec_sems.at[i])
        copy.start()
        copies.append(copy)
    total = turned_act.shape[1]
    act_grad = jnp.zeros((total, features), f32)
    for at in range(0, width, 512):
        columns = slice(at, at + 512)
        act_grad = act_grad + lax.dot_general(
            stacked(errors, columns), stacked(dec_refs, columns), (((1,), (1,)), ((), ())), preferred_element_type=f32
        )
    gate = jnp.concatenate([g[...] for g in gates], axis=0)
    pre_grad = ((act_grad + penalty_weight * norm_ref[...]) * gate).astype(bf16)
    bias_out[...] = jnp.sum(pre_grad.astype(f32), axis=0, keepdims=True)
    for i, at in enumerate(range(0, width, step)):
        here = slice(at, at + step)
        left = jnp.concatenate([r[here, :] for r in rows], axis=1)
        enc_stage[here, :] = jnp.dot(left, pre_grad, preferred_element_type=f32).astype(bf16)
        copy = pltpu.make_async_copy(enc_stage.at[here, :], enc_out.at[here, :], enc_sems.at[i])
        copy.start()
        copies.append(copy)
    for copy in copies:
        copy.wait()


def backward(errors, acts, gates, rows, decoder, norms, act_sum):
    errors = [whole_pieces(e) for e in errors]
    features, width = sum(d.shape[0] for d in decoder), decoder[0].shape[1]
    step = min(512, width)
    operands = [x for e in errors for x in e] + acts + gates + rows + [*decoder, norms, act_sum]
    total = sum(a.shape[0] for a in acts)
    return pl.pallas_call(
        functools.partial(backward_kernel, tuple(len(e) for e in errors), step),
        out_shape=[
            jax.ShapeDtypeStruct((width, features), bf16),
            jax.ShapeDtypeStruct((1, features), f32),
            jax.ShapeDtypeStruct((features, width), bf16),
        ],
        in_specs=[VMEM_SPEC] * len(operands),
        out_specs=[ANY_SPEC, VMEM_SPEC, ANY_SPEC],
        scratch_shapes=[
            pltpu.VMEM((width, features), bf16),
            pltpu.VMEM((features, width), bf16),
            pltpu.SemaphoreType.DMA((width // step,)),
            pltpu.SemaphoreType.DMA((width // step,)),
        ],
        compiler_params=pltpu.CompilerParams(vmem_limit_bytes=24 << 20),
        cost_estimate=SHORT,
    )(*[in_vmem(x) for x in operands])


def load_kernel(first, source_ref, signal_ref, out_ref, sems):
    pieces = sems.shape[0]
    rows = out_ref.shape[0] // pieces
    copies = []
    for i in range(pieces):
        copy = pltpu.make_async_copy(
            source_ref.at[first + i * rows : first + (i + 1) * rows], out_ref.at[i * rows : (i + 1) * rows], sems.at[i]
        )
        copy.start()
        copies.append(copy)
    for copy in copies:
        copy.wait()


def loaded(array, part, signal):
    rows = array.shape[0] // 2
    return pl.pallas_call(
        functools.partial(load_kernel, part * rows),
        out_shape=pltpu.VMEM((rows, array.shape[1]), array.dtype),
        in_specs=[HBM_SPEC, VMEM_SPEC],
        out_specs=VMEM_SPEC,
        scratch_shapes=[pltpu.SemaphoreType.DMA((4,))],
        compiler_params=pltpu.CompilerParams(vmem_limit_bytes=4 << 20),
        cost_estimate=SHORT,
    )(in_hbm(array), in_vmem(signal))


def prepare_kernel(mask_ref, table_ref, half_ref, source_ref, signal_ref, dec_ref, norm_ref, *rest):
    keep_refs, (row_ref, row_sem, sems) = rest[:-3], rest[-3:]
    row = pltpu.make_async_copy(table_ref.at[lax.axis_index("feat")], row_ref, row_sem)
    row.start()
    pieces = sems.shape[0]
    rows, width = dec_ref.shape[0] // pieces, dec_ref.shape[1]
    copies = []
    for i in range(pieces):
        here = slice(i * rows, (i + 1) * rows)
        there = slice(dec_ref.shape[0] + i * rows, dec_ref.shape[0] + (i + 1) * rows)
        copy = pltpu.make_async_copy(source_ref.at[there], dec_ref.at[here], sems.at[i])
        copy.start()
        copies.append(copy)
    row.wait()
    token_block = jnp.broadcast_to(row_ref[...], (8, row_ref.shape[1])).T[:, :1]
    for i, out_ref in enumerate(keep_refs):
        total = out_ref.shape[0]
        here = token_block[i * total : (i + 1) * total]
        for j in range(mask_ref.shape[1]):
            column = jnp.zeros((total, FBLOCK), f32)
            for b in range(mask_ref.shape[0]):
                column = jnp.where(here == b, mask_ref[b, j].astype(f32), column)
            out_ref[:, j * FBLOCK : (j + 1) * FBLOCK] = column
    for half, ref in enumerate((half_ref, dec_ref)):
        for i in range(pieces):
            if half:
                copies[i].wait()
            here = slice(i * rows, (i + 1) * rows)
            partial = jnp.zeros((rows, 128), f32)
            for at in range(0, width, 128):
                part = ref[here, at : at + 128].astype(f32)
                partial = partial + part * part
            there = slice(half * dec_ref.shape[0] + i * rows, half * dec_ref.shape[0] + (i + 1) * rows)
            norm_ref[:, there] = jnp.sqrt(jnp.sum(partial.T, axis=0, keepdims=True) + norm_epsilon)


def prepared(mask, table, half, decoder, signal):
    features = decoder.shape[0]
    total = table.shape[2] // 2
    dec, norm, *keep = pl.pallas_call(
        prepare_kernel,
        out_shape=[
            pltpu.VMEM(half.shape, half.dtype),
            pltpu.VMEM((1, features), f32),
            pltpu.VMEM((total, features), f32),
            pltpu.VMEM((total, features), f32),
        ],
        in_specs=[SMEM_SPEC, HBM_SPEC, VMEM_SPEC, HBM_SPEC, VMEM_SPEC],
        out_specs=[VMEM_SPEC] * 4,
        scratch_shapes=[
            pltpu.VMEM((1, table.shape[2]), f32),
            pltpu.SemaphoreType.DMA,
            pltpu.SemaphoreType.DMA((max(1, half.shape[0] // 128),)),
        ],
        compiler_params=pltpu.CompilerParams(vmem_limit_bytes=4 << 20),
        cost_estimate=SHORT,
    )(mask, in_hbm(table), in_vmem(half), in_hbm(decoder), in_vmem(signal))
    return dec, norm, keep


def misfit_kernel(*refs):
    mine_ref, other_ref, goal_ref = refs[:3]
    rest, out_ref = refs[3:-1], refs[-1]
    width = mine_ref.shape[1]
    misfit = mine_ref[...].astype(f32) + other_ref[...].astype(f32) - goal_ref[...].astype(f32)
    loss = 0.5 * jnp.sum(misfit * misfit, keepdims=True)
    for ref in rest:
        loss = loss + jnp.sum(ref[...], keepdims=True)
    high = loss.astype(bf16).astype(f32)
    middle = (loss - high).astype(bf16).astype(f32)
    low = loss - high - middle
    lane = lax.broadcasted_iota(jnp.int32, (out_ref.shape[0], PAD), 1)
    tail = jnp.where(lane == 0, high, jnp.where(lane == 1, middle, jnp.where(lane == 2, low, 0.0)))
    out_ref[:, :width] = misfit.astype(bf16)
    out_ref[:, width:] = tail.astype(bf16)


def misfits(mine, other, goal, rest):
    rows, width = mine.shape
    operands = (mine, other, goal, *rest)
    return pl.pallas_call(
        misfit_kernel,
        out_shape=pltpu.VMEM((rows, width + PAD), bf16),
        in_specs=[VMEM_SPEC] * len(operands),
        out_specs=VMEM_SPEC,
        compiler_params=pltpu.CompilerParams(vmem_limit_bytes=8 << 20),
        cost_estimate=SHORT,
    )(*[in_vmem(x) for x in operands])


def loss_kernel(scale, *refs):
    pieces, out_ref = refs[:-1], refs[-1]
    total = jnp.zeros((1, 1), f32)
    for ref in pieces:
        tail = ref[:, ref.shape[1] - PAD :].astype(f32)
        total = total + jnp.sum(tail, keepdims=True)
    out_ref[...] = jnp.broadcast_to(total * scale, out_ref.shape)


def group_loss(pieces, block_rows):
    return pl.pallas_call(
        functools.partial(loss_kernel, 1.0 / block_rows),
        out_shape=pltpu.VMEM((8, PAD), f32),
        in_specs=[VMEM_SPEC] * len(pieces),
        out_specs=VMEM_SPEC,
        compiler_params=pltpu.CompilerParams(vmem_limit_bytes=8 << 20),
        cost_estimate=SHORT,
    )(*[in_vmem(x) for x in pieces])


def body(residual, targets, w_enc, b_enc, w_dec, block_mask):
    rows = residual.shape[1]
    width = residual.shape[2]
    layers = lax.axis_size("layer")
    feats = lax.axis_size("feat")
    tokens = rows * feats
    ring = Ring(feats)

    tokens_of = ring.owners[..., None] * rows + np.arange(rows)
    table = jnp.asarray((tokens_of // TBLOCK).reshape(feats, 1, -1).astype(np.float32))

    own = residual[0]
    twins = ring.across(own)
    held = {}

    def load_in(name, array, part, hop):
        def pin(ended):
            signal = ended[0][hop - 1] if hop else twins
            held[name, part] = loaded(array, part, signal)
            return [held[name, part]]

        return pin

    def rest_in(ended):
        held["decoder", 1], held["norm"], held["keep"] = prepared(
            block_mask[0], table, held["decoder", 0], w_dec[0], ended[1][ring.hops - 1]
        )
        return [held["decoder", 1], held["norm"], *held["keep"]]

    pins = {
        2: load_in("encoder", w_enc[0], 0, 0),
        3: load_in("encoder", w_enc[0], 1, 1),
        4: load_in("decoder", w_dec[0], 0, 2),
        0: rest_in,
    }
    gathered = gather(ring, own, twins, pins, True)
    encoder = [held["encoder", i] for i in (0, 1)]
    decoder = [held["decoder", i] for i in (0, 1)]

    acts, gates, sums, shares = zip(
        *[forward(ring, gathered[i], encoder, b_enc, held["keep"][i], decoder, i == 0) for i in (0, 1)]
    )
    act_sum = sums[0] + sums[1]

    def goals_in(ended):
        goal = after(targets[0], ended[0][0])
        goal = lax.ppermute(goal, "layer", [(i, (i - 1) % layers) for i in range(layers)])
        held["goal"] = [goal, ring.across(goal)]
        return list(held["goal"])

    def rest_in(ended):
        penalty = penalty_weight * act_sum * held["norm"]
        held["rest"] = [penalty, ring.across(penalty)]
        return held["rest"]

    pins = {4: lambda ended: goals_in(ended) + rest_in(ended)}
    summed = scatter_sums(ring, rows, shares, pins)
    payloads = [misfits(*summed[i], held["goal"][i], held["rest"][i : i + 1]) for i in (0, 1)]
    held["turned"] = []

    def rows_in(ended):
        chain = len(held["turned"])
        held["turned"].append(turned(after(gathered[chain], ended[1][chain])))
        return held["turned"][-1:]

    errors = gather(ring, *payloads, {3: rows_in, 4: rows_in}, False)
    sent_loss = loss_row = group_loss([piece for parts in errors for piece in parts], rows)
    for _ in range(layers - 1):
        sent_loss = lax.ppermute(sent_loss, "layer", [(i, (i + 1) % layers) for i in range(layers)])
        loss_row = loss_row + sent_loss
    enc_grad, bias_grad, dec_grad = backward(
        errors, list(acts), list(gates), held["turned"], decoder, held["norm"], act_sum
    )
    loss = after(loss_row, bias_grad)[0, 0] / (layers * tokens * width)
    return enc_grad[None], bias_grad, dec_grad[None], loss


def solution(mesh):
    return jax.shard_map(
        body,
        mesh=mesh,
        in_specs=(
            P("layer", "feat", None),
            P("layer", "feat", None),
            P("layer", None, "feat"),
            P("layer", "feat"),
            P("layer", "feat", None),
            P("layer", None, "feat"),
        ),
        out_specs=(P("layer", None, "feat"), P("layer", "feat"), P("layer", "feat", None), P()),
        check_vma=False,
    )
```

time: 84.1 us -> 80.4 us (0.956)
  waiting for transfers between devices: 22.7 us -> 19.1 us
    ppermute x24 -> x22, waiting for transfers between devices: 22.5 us -> 16.3 us  [along(): return lax.ppermute(block, 'feat', self.step)]
    ppermute x19 -> x20, waiting for transfers between devices: 0.2 us -> 2.72 us  [across(): return lax.ppermute(block, 'feat', self.twin)]
    ppermute x1, starting transfers between devices: 2.6 us -> 1.51 us  [goals_in(): lax.ppermute(goal, 'layer', [(i, (i - 1) % layers) for i in range(layers)])]
    pallas_call x7 -> x4, Pallas kernels: 7.24 us -> 7.72 us  [the longest x3 4.64 us: loaded(): pl.pallas_call(functools.partial(load_kernel, part * rows), out_shape=plt...]
    ppermute x24 -> x22, starting transfers between devices: 33.8 us -> 34.2 us  [along(): return lax.ppermute(block, 'feat', self.step)]
    ppermute x19 -> x20, starting transfers between devices: 2.41 us -> 2.69 us  [across(): return lax.ppermute(block, 'feat', self.twin)]
  transfers between devices with their start and end apart: 45 -> 44, of which waited for: 20 -> 16; matrix products, arithmetic and copies ran while one was open for 1% -> 0% of each run, Pallas kernels for 18% -> 20%
where the time goes in v5:
time: 80.4 us; the launch traced here: 80.2 us
  starting transfers between devices  39.9 us (50%)
  waiting for transfers between devices  19.1 us (24%)
  Pallas kernels  17.6 us (22%)
  between operations  2.71 us (3%)
    ppermute x22, starting transfers between devices, along(): return lax.ppermute(block, 'feat', self.step)  34.2 us
    ppermute x22, waiting for transfers between devices, along(): return lax.ppermute(block, 'feat', self.step)  16.3 us
    pallas_call x1, Pallas kernels, backward(): pl.pallas_call(functools.partial(backward_kernel, tuple((len(e) for e in...  5.69 us
    pallas_call x3, Pallas kernels, loaded(): pl.pallas_call(functools.partial(load_kernel, part * rows), out_shape=plt...  4.64 us
    pallas_call x1, Pallas kernels, prepared(): pl.pallas_call(prepare_kernel, out_shape=[pltpu.VMEM(half.shape, half.dty...  3.08 us
    pallas_call x2, Pallas kernels, forward(): pl.pallas_call(functools.partial(forward_kernel, len(pieces), min(512, wi...  2.91 us
    ppermute x20, waiting for transfers between devices, across(): return lax.ppermute(block, 'feat', self.twin)  2.72 us
    ppermute x20, starting transfers between devices, across(): return lax.ppermute(block, 'feat', self.twin)  2.69 us
  transfers between devices with their start and end apart: 44, of which 16 were waited for; matrix products, arithmetic and copies ran while one was open for 0% of the time, Pallas kernels for 20%

profile of v5, /device:TPU:0, one launch (start us, length us, event | category | flops | bytes accessed | tf_op | source)
XLA Modules:
  0.0 80.2 jit_solution(14806009055207319137)
XLA Ops:
  1.1 2.6 %collective-permute-start = (bf16[16,4096]{1,0:T(8,128)(2,1)}, bf16[16,4096]{1,0:T(8,128)(2,1)S(1)}, u32[]{:S(2)}, u32[]{:S(2)}) collective-permute-start(bf16[16,4096]{1,0:T(8,128)(2,1)} %bitcast.9), channel_id=1, source_target_pairs={{0,4},{1,3},{2,0},{3,7},{4,8},{5,1},{6,2},{7,11},{8,12},{9,5},{10,... | collective-permute-start | bytes 393224 | tf_op jit(solution)/shard_map/ppermute | solution.py:43
  3.8 1.6 %collective-permute-start.4 = (bf16[16,4096]{1,0:T(8,128)(2,1)S(1)}, bf16[16,4096]{1,0:T(8,128)(2,1)S(1)}, u32[]{:S(2)}, u32[]{:S(2)}) collective-permute-start(bf16[16,4096]{1,0:T(8,128)(2,1)S(1)} %collective-permute-done.1.signal_ref.refs_0_), channel_id=1, source_target_pairs={{0,4},{1,3},{2,0},{3,7},{4,8},{5,1},{6,2},{7,11},{8,12},{9,5},{10,... | collective-permute-start | bytes 393224 | tf_op jit(solution)/shard_map/ppermute | solution.py:43
  5.4 1.5 %shard_map.102.refs_8_ = bf16[2048,512]{1,0:T(8,128)(2,1)S(1)} custom-call(bf16[4096,512]{1,0:T(8,128)(2,1)} %bitcast.13, bf16[16,4096]{1,0:T(8,128)(2,1)S(1)} %collective-permute-done.1.signal_ref.refs_0_), custom_call_target="tpu_custom_call" | custom-call | tf_op jit(solution)/shard_map/pallas_call | solution.py:327
  6.9 2.0 %collective-permute-start.2 = (bf16[16,4096]{1,0:T(8,128)(2,1)S(1)}, bf16[16,4096]{1,0:T(8,128)(2,1)S(1)}, u32[]{:S(2)}, u32[]{:S(2)}) collective-permute-start(bf16[16,4096]{1,0:T(8,128)(2,1)S(1)} %collective-permute-done.signal_ref.refs_1_), channel_id=1, source_target_pairs={{0,4},{1,3},{2,0},{3,7},{4,8},{5,1},{6,2},{7,11},{8,12},{9,5},{10,... | collective-permute-start | bytes 393224 | tf_op jit(solution)/shard_map/ppermute | solution.py:43
  9.5 1.6 %collective-permute-start.7 = (bf16[16,4096]{1,0:T(8,128)(2,1)S(1)}, bf16[16,4096]{1,0:T(8,128)(2,1)S(1)}, u32[]{:S(2)}, u32[]{:S(2)}) collective-permute-start(bf16[16,4096]{1,0:T(8,128)(2,1)S(1)} %collective-permute-done.4.refs_1_), channel_id=1, source_target_pairs={{0,4},{1,3},{2,0},{3,7},{4,8},{5,1},{6,2},{7,11},{8,12},{9,5},{10,... | collective-permute-start | bytes 393224 | tf_op jit(solution)/shard_map/ppermute | solution.py:43
  11.1 1.5 %shard_map.103.refs_9_ = bf16[2048,512]{1,0:T(8,128)(2,1)S(1)} custom-call(bf16[4096,512]{1,0:T(8,128)(2,1)} %bitcast.14, bf16[16,4096]{1,0:T(8,128)(2,1)S(1)} %collective-permute-done.signal_ref.refs_1_), custom_call_target="tpu_custom_call" | custom-call | tf_op jit(solution)/shard_map/pallas_call | solution.py:327
  12.6 1.6 %collective-permute-start.5 = (bf16[16,4096]{1,0:T(8,128)(2,1)S(1)}, bf16[16,4096]{1,0:T(8,128)(2,1)S(1)}, u32[]{:S(2)}, u32[]{:S(2)}) collective-permute-start(bf16[16,4096]{1,0:T(8,128)(2,1)S(1)} %collective-permute-done.2.signal_ref.refs_2_), channel_id=1, source_target_pairs={{0,4},{1,3},{2,0},{3,7},{4,8},{5,1},{6,2},{7,11},{8,12},{9,5},{10,... | collective-permute-start | bytes 393224 | tf_op jit(solution)/shard_map/ppermute | solution.py:43
  16.3 1.5 %shard_map.104.half_ref.refs_10_.refs_22_ = bf16[256,4096]{1,0:T(8,128)(2,1)S(1)} custom-call(bf16[512,4096]{1,0:T(8,128)(2,1)} %bitcast.15, bf16[16,4096]{1,0:T(8,128)(2,1)S(1)} %collective-permute-done.2.signal_ref.refs_2_), custom_call_target="tpu_custom_call" | custom-call | tf_op jit(solution)/shard_map/pallas_call | solution.py:327
  21.3 3.1 %shard_map.105 = (bf16[256,4096]{1,0:T(8,128)(2,1)S(1)}, f32[1,512]{1,0:T(1,128)S(1)}, f32[128,512]{1,0:T(8,128)S(1)}, f32[128,512]{1,0:T(8,128)S(1)}) custom-call(s32[2,4]{1,0:T(2,128)S(1)} %bitcast.12, f32[16,1,256]{2,1,0:T(1,128)} %constant.8.clone.table_ref, bf16[256,4096]{1,0:T(8,128)(2,1)S(1)} %shard_map.104.half_ref.refs_10_.refs_22_, ...), custom_call_target="tpu_custom_call" | custom-call | tf_op jit(solution)/shard_map/pallas_call | solution.py:377
  28.4 1.6 %collective-permute-start.16 = (bf16[16,4096]{1,0:T(8,128)(2,1)S(1)}, bf16[16,4096]{1,0:T(8,128)(2,1)S(1)}, u32[]{:S(2)}, u32[]{:S(2)}) collective-permute-start(bf16[16,4096]{1,0:T(8,128)(2,1)S(1)} %add_convert_fusion.8), channel_id=1, source_target_pairs={{0,4},{1,3},{2,0},{3,7},{4,8},{5,1},{6,2},{7,11},{8,12},{9,5},{10,... | collective-permute-start | bytes 393224 | tf_op jit(solution)/shard_map/ppermute | solution.py:43
  31.4 2.1 %collective-permute-done.16 = bf16[16,4096]{1,0:T(8,128)(2,1)S(1)} collective-permute-done((bf16[16,4096]{1,0:T(8,128)(2,1)S(1)}, bf16[16,4096]{1,0:T(8,128)(2,1)S(1)}, u32[]{:S(2)}, u32[]{:S(2)}) %collective-permute-start.16) | collective-permute-done | bytes 131104 | tf_op jit(solution)/shard_map/ppermute | solution.py:43
  33.5 1.6 %collective-permute-start.17 = (bf16[16,4096]{1,0:T(8,128)(2,1)S(1)}, bf16[16,4096]{1,0:T(8,128)(2,1)S(1)}, u32[]{:S(2)}, u32[]{:S(2)}) collective-permute-start(bf16[16,4096]{1,0:T(8,128)(2,1)S(1)} %add_convert_fusion.7), channel_id=1, source_target_pairs={{0,4},{1,3},{2,0},{3,7},{4,8},{5,1},{6,2},{7,11},{8,12},{9,5},{10,... | collective-permute-start | bytes 393224 | tf_op jit(solution)/shard_map/ppermute | solution.py:43
  36.5 1.5 %collective-permute-start.22 = (bf16[16,4096]{1,0:T(8,128)(2,1)S(1)}, bf16[16,4096]{1,0:T(8,128)(2,1)S(1)}, u32[]{:S(2)}, u32[]{:S(2)}) collective-permute-start(bf16[16,4096]{1,0:T(8,128)(2,1)S(1)} %bitcast.19), channel_id=1, source_target_pairs={{0,16},{16,0},{1,17},{17,1},{2,18},{18,2},{3,19},{19,3},{4,20},{20... | collective-permute-start | bytes 393224 | tf_op jit(solution)/shard_map/ppermute | solution.py:494
  38.6 1.6 %collective-permute-start.20 = (bf16[16,4096]{1,0:T(8,128)(2,1)S(1)}, bf16[16,4096]{1,0:T(8,128)(2,1)S(1)}, u32[]{:S(2)}, u32[]{:S(2)}) collective-permute-start(bf16[16,4096]{1,0:T(8,128)(2,1)S(1)} %add_convert_fusion.6), channel_id=1, source_target_pairs={{0,4},{1,3},{2,0},{3,7},{4,8},{5,1},{6,2},{7,11},{8,12},{9,5},{10,... | collective-permute-start | bytes 393224 | tf_op jit(solution)/shard_map/ppermute | solution.py:43
  41.6 2.0 %collective-permute-done.20 = bf16[16,4096]{1,0:T(8,128)(2,1)S(1)} collective-permute-done((bf16[16,4096]{1,0:T(8,128)(2,1)S(1)}, bf16[16,4096]{1,0:T(8,128)(2,1)S(1)}, u32[]{:S(2)}, u32[]{:S(2)}) %collective-permute-start.20) | collective-permute-done | bytes 131104 | tf_op jit(solution)/shard_map/ppermute | solution.py:43
  43.7 1.6 %collective-permute-start.25 = (bf16[16,4096]{1,0:T(8,128)(2,1)S(1)}, bf16[16,4096]{1,0:T(8,128)(2,1)S(1)}, u32[]{:S(2)}, u32[]{:S(2)}) collective-permute-start(bf16[16,4096]{1,0:T(8,128)(2,1)S(1)} %add_convert_fusion.4), channel_id=1, source_target_pairs={{0,4},{1,3},{2,0},{3,7},{4,8},{5,1},{6,2},{7,11},{8,12},{9,5},{10,... | collective-permute-start | bytes 393224 | tf_op jit(solution)/shard_map/ppermute | solution.py:43
  45.3 3.3 %collective-permute-done.25 = bf16[16,4096]{1,0:T(8,128)(2,1)S(1)} collective-permute-done((bf16[16,4096]{1,0:T(8,128)(2,1)S(1)}, bf16[16,4096]{1,0:T(8,128)(2,1)S(1)}, u32[]{:S(2)}, u32[]{:S(2)}) %collective-permute-start.25) | collective-permute-done | bytes 131104 | tf_op jit(solution)/shard_map/ppermute | solution.py:43
  49.0 1.6 %collective-permute-start.28 = (bf16[16,4224]{1,0:T(8,128)(2,1)S(1)}, bf16[16,4224]{1,0:T(8,128)(2,1)S(1)}, u32[]{:S(2)}, u32[]{:S(2)}) collective-permute-start(bf16[16,4224]{1,0:T(8,128)(2,1)S(1)} %shard_map.108.refs_0_), channel_id=1, source_target_pairs={{0,4},{1,3},{2,0},{3,7},{4,8},{5,1},{6,2},{7,11},{8,12},{9,5},{10,... | collective-permute-start | bytes 405512 | tf_op jit(solution)/shard_map/ppermute | solution.py:43
  55.5 1.6 %collective-permute-done.32.refs_9_ = bf16[16,4224]{1,0:T(8,128)(2,1)S(1)} collective-permute-done((bf16[16,4224]{1,0:T(8,128)(2,1)S(1)}, bf16[16,4224]{1,0:T(8,128)(2,1)S(1)}, u32[]{:S(2)}, u32[]{:S(2)}) %collective-permute-start.32) | collective-permute-done | bytes 135200 | tf_op jit(solution)/shard_map/ppermute | solution.py:43
  60.5 1.6 %collective-permute-done.35.refs_10_ = bf16[16,4224]{1,0:T(8,128)(2,1)S(1)} collective-permute-done((bf16[16,4224]{1,0:T(8,128)(2,1)S(1)}, bf16[16,4224]{1,0:T(8,128)(2,1)S(1)}, u32[]{:S(2)}, u32[]{:S(2)}) %collective-permute-start.35) | collective-permute-done | bytes 135200 | tf_op jit(solution)/shard_map/ppermute | solution.py:43
  64.1 1.5 %collective-permute-start.40 = (bf16[16,4224]{1,0:T(8,128)(2,1)S(1)}, bf16[16,4224]{1,0:T(8,128)(2,1)S(1)}, u32[]{:S(2)}, u32[]{:S(2)}) collective-permute-start(bf16[16,4224]{1,0:T(8,128)(2,1)S(1)} %collective-permute-done.33.refs_3_), channel_id=1, source_target_pairs={{0,4},{1,3},{2,0},{3,7},{4,8},{5,1},{6,2},{7,11},{8,12},{9,5},{10,... | collective-permute-start | bytes 405512 | tf_op jit(solution)/shard_map/ppermute | solution.py:43
  67.2 1.9 %collective-permute-done.40.refs_7_ = bf16[16,4224]{1,0:T(8,128)(2,1)S(1)} collective-permute-done((bf16[16,4224]{1,0:T(8,128)(2,1)S(1)}, bf16[16,4224]{1,0:T(8,128)(2,1)S(1)}, u32[]{:S(2)}, u32[]{:S(2)}) %collective-permute-start.40) | collective-permute-done | bytes 135200 | tf_op jit(solution)/shard_map/ppermute | solution.py:43
  70.6 1.6 %collective-permute-start.43 = (f32[8,128]{1,0:T(8,128)S(1)}, f32[8,128]{1,0:T(8,128)S(1)}, u32[]{:S(2)}, u32[]{:S(2)}) collective-permute-start(f32[8,128]{1,0:T(8,128)S(1)} %shard_map.113), channel_id=1, source_target_pairs={{0,16},{16,0},{1,17},{17,1},{2,18},{18,2},{3,19},{19,3},{4,20},{20... | collective-permute-start | bytes 12296 | tf_op jit(solution)/shard_map/ppermute | solution.py:516
  72.2 5.7 %shard_map.112 = (bf16[4096,512]{1,0:T(8,128)(2,1)}, f32[1,512]{1,0:T(1,128)}, bf16[512,4096]{1,0:T(8,128)(2,1)}) custom-call(bf16[16,4224]{1,0:T(8,128)(2,1)S(1)} %shard_map.108.refs_0_, bf16[16,4224]{1,0:T(8,128)(2,1)S(1)} %collective-permute-done.28.refs_1_, bf16[16,4224]{1,0:T(8,128)(2,1)S(1)} %collective-permute-done.29.refs_2_, ...), custom_call_target="tpu_custom_call" | custom-call | tf_op jit(solution)/shard_map/pallas_call | solution.py:291
  (96 shorter events, 29.6 us)
Async XLA Ops:
  1.1 5.8 %collective-permute-start = (bf16[16,4096]{1,0:T(8,128)(2,1)}, bf16[16,4096]{1,0:T(8,128)(2,1)S(1)}, u32[]{:S(2)}, u32[]{:S(2)}) collective-permute-start(bf16[16,4096]{1,0:T(8,128)(2,1)} %bitcast.9), channel_id=1, source_target_pairs={{0,4},{1,3},{2,0},{3,7},{4,8},{5,1},{6,2},{7,11},{8,12},{9,5},{10,... | collective-permute-start | bytes 393224 | tf_op jit(solution)/shard_map/ppermute | solution.py:43
  3.8 5.2 %collective-permute-start.4 = (bf16[16,4096]{1,0:T(8,128)(2,1)S(1)}, bf16[16,4096]{1,0:T(8,128)(2,1)S(1)}, u32[]{:S(2)}, u32[]{:S(2)}) collective-permute-start(bf16[16,4096]{1,0:T(8,128)(2,1)S(1)} %collective-permute-done.1.signal_ref.refs_0_), channel_id=1, source_target_pairs={{0,4},{1,3},{2,0},{3,7},{4,8},{5,1},{6,2},{7,11},{8,12},{9,5},{10,... | collective-permute-start | bytes 393224 | tf_op jit(solution)/shard_map/ppermute | solution.py:43
  6.9 5.7 %collective-permute-start.2 = (bf16[16,4096]{1,0:T(8,128)(2,1)S(1)}, bf16[16,4096]{1,0:T(8,128)(2,1)S(1)}, u32[]{:S(2)}, u32[]{:S(2)}) collective-permute-start(bf16[16,4096]{1,0:T(8,128)(2,1)S(1)} %collective-permute-done.signal_ref.refs_1_), channel_id=1, source_target_pairs={{0,4},{1,3},{2,0},{3,7},{4,8},{5,1},{6,2},{7,11},{8,12},{9,5},{10,... | collective-permute-start | bytes 393224 | tf_op jit(solution)/shard_map/ppermute | solution.py:43
  9.0 5.3 %collective-permute-start.6 = (bf16[16,4096]{1,0:T(8,128)(2,1)S(1)}, bf16[16,4096]{1,0:T(8,128)(2,1)S(1)}, u32[]{:S(2)}, u32[]{:S(2)}) collective-permute-start(bf16[16,4096]{1,0:T(8,128)(2,1)S(1)} %collective-permute-done.4.refs_1_), channel_id=1, source_target_pairs={{0,1},{1,0},{2,3},{3,2},{4,5},{5,4},{6,7},{7,6},{8,9},{9,8},{10,11... | collective-permute-start | bytes 393224 | tf_op jit(solution)/shard_map/ppermute | solution.py:46
  12.6 5.2 %collective-permute-start.5 = (bf16[16,4096]{1,0:T(8,128)(2,1)S(1)}, bf16[16,4096]{1,0:T(8,128)(2,1)S(1)}, u32[]{:S(2)}, u32[]{:S(2)}) collective-permute-start(bf16[16,4096]{1,0:T(8,128)(2,1)S(1)} %collective-permute-done.2.signal_ref.refs_2_), channel_id=1, source_target_pairs={{0,4},{1,3},{2,0},{3,7},{4,8},{5,1},{6,2},{7,11},{8,12},{9,5},{10,... | collective-permute-start | bytes 393224 | tf_op jit(solution)/shard_map/ppermute | solution.py:43
  17.9 6.5 %collective-permute-start.12 = (bf16[16,4096]{1,0:T(8,128)(2,1)S(1)}, bf16[16,4096]{1,0:T(8,128)(2,1)S(1)}, u32[]{:S(2)}, u32[]{:S(2)}) collective-permute-start(bf16[16,4096]{1,0:T(8,128)(2,1)S(1)} %collective-permute-done.5.refs_3_), channel_id=1, source_target_pairs={{0,4},{1,3},{2,0},{3,7},{4,8},{5,1},{6,2},{7,11},{8,12},{9,5},{10,... | collective-permute-start | bytes 393224 | tf_op jit(solution)/shard_map/ppermute | solution.py:43
  19.3 5.1 %collective-permute-start.13 = (bf16[16,4096]{1,0:T(8,128)(2,1)S(1)}, bf16[16,4096]{1,0:T(8,128)(2,1)S(1)}, u32[]{:S(2)}, u32[]{:S(2)}) collective-permute-start(bf16[16,4096]{1,0:T(8,128)(2,1)S(1)} %collective-permute-done.5.refs_3_), channel_id=1, source_target_pairs={{0,1},{1,0},{2,3},{3,2},{4,5},{5,4},{6,7},{7,6},{8,9},{9,8},{10,11... | collective-permute-start | bytes 393224 | tf_op jit(solution)/shard_map/ppermute | solution.py:46
  28.3 15.3 %collective-permute-start.24 = (f32[1,512]{1,0:T(1,128)S(1)}, f32[1,512]{1,0:T(1,128)S(1)}, u32[]{:S(2)}, u32[]{:S(2)}) collective-permute-start(f32[1,512]{1,0:T(1,128)S(1)} %get-tuple-element.148.refs_3_), channel_id=1, source_target_pairs={{0,1},{1,0},{2,3},{3,2},{4,5},{5,4},{6,7},{7,6},{8,9},{9,8},{10,11... | collective-permute-start | bytes 6152 | tf_op jit(solution)/shard_map/ppermute | solution.py:46
  28.4 5.0 %collective-permute-start.16 = (bf16[16,4096]{1,0:T(8,128)(2,1)S(1)}, bf16[16,4096]{1,0:T(8,128)(2,1)S(1)}, u32[]{:S(2)}, u32[]{:S(2)}) collective-permute-start(bf16[16,4096]{1,0:T(8,128)(2,1)S(1)} %add_convert_fusion.8), channel_id=1, source_target_pairs={{0,4},{1,3},{2,0},{3,7},{4,8},{5,1},{6,2},{7,11},{8,12},{9,5},{10,... | collective-permute-start | bytes 393224 | tf_op jit(solution)/shard_map/ppermute | solution.py:43
  30.0 5.0 %collective-permute-start.19 = (bf16[16,4096]{1,0:T(8,128)(2,1)S(1)}, bf16[16,4096]{1,0:T(8,128)(2,1)S(1)}, u32[]{:S(2)}, u32[]{:S(2)}) collective-permute-start(bf16[16,4096]{1,0:T(8,128)(2,1)S(1)} %add_convert_fusion.5), channel_id=1, source_target_pairs={{0,4},{1,3},{2,0},{3,7},{4,8},{5,1},{6,2},{7,11},{8,12},{9,5},{10,... | collective-permute-start | bytes 393224 | tf_op jit(solution)/shard_map/ppermute | solution.py:43
  33.5 5.0 %collective-permute-start.17 = (bf16[16,4096]{1,0:T(8,128)(2,1)S(1)}, bf16[16,4096]{1,0:T(8,128)(2,1)S(1)}, u32[]{:S(2)}, u32[]{:S(2)}) collective-permute-start(bf16[16,4096]{1,0:T(8,128)(2,1)S(1)} %add_convert_fusion.7), channel_id=1, source_target_pairs={{0,4},{1,3},{2,0},{3,7},{4,8},{5,1},{6,2},{7,11},{8,12},{9,5},{10,... | collective-permute-start | bytes 393224 | tf_op jit(solution)/shard_map/ppermute | solution.py:43
  35.1 5.0 %collective-permute-start.21 = (bf16[16,4096]{1,0:T(8,128)(2,1)S(1)}, bf16[16,4096]{1,0:T(8,128)(2,1)S(1)}, u32[]{:S(2)}, u32[]{:S(2)}) collective-permute-start(bf16[16,4096]{1,0:T(8,128)(2,1)S(1)} %add_convert_fusion.3), channel_id=1, source_target_pairs={{0,4},{1,3},{2,0},{3,7},{4,8},{5,1},{6,2},{7,11},{8,12},{9,5},{10,... | collective-permute-start | bytes 393224 | tf_op jit(solution)/shard_map/ppermute | solution.py:43
  36.5 5.1 %collective-permute-start.22 = (bf16[16,4096]{1,0:T(8,128)(2,1)S(1)}, bf16[16,4096]{1,0:T(8,128)(2,1)S(1)}, u32[]{:S(2)}, u32[]{:S(2)}) collective-permute-start(bf16[16,4096]{1,0:T(8,128)(2,1)S(1)} %bitcast.19), channel_id=1, source_target_pairs={{0,16},{16,0},{1,17},{17,1},{2,18},{18,2},{3,19},{19,3},{4,20},{20... | collective-permute-start | bytes 393224 | tf_op jit(solution)/shard_map/ppermute | solution.py:494
  38.6 5.0 %collective-permute-start.20 = (bf16[16,4096]{1,0:T(8,128)(2,1)S(1)}, bf16[16,4096]{1,0:T(8,128)(2,1)S(1)}, u32[]{:S(2)}, u32[]{:S(2)}) collective-permute-start(bf16[16,4096]{1,0:T(8,128)(2,1)S(1)} %add_convert_fusion.6), channel_id=1, source_target_pairs={{0,4},{1,3},{2,0},{3,7},{4,8},{5,1},{6,2},{7,11},{8,12},{9,5},{10,... | collective-permute-start | bytes 393224 | tf_op jit(solution)/shard_map/ppermute | solution.py:43
  40.2 5.0 %collective-permute-start.26 = (bf16[16,4096]{1,0:T(8,128)(2,1)S(1)}, bf16[16,4096]{1,0:T(8,128)(2,1)S(1)}, u32[]{:S(2)}, u32[]{:S(2)}) collective-permute-start(bf16[16,4096]{1,0:T(8,128)(2,1)S(1)} %add_convert_fusion.1), channel_id=1, source_target_pairs={{0,4},{1,3},{2,0},{3,7},{4,8},{5,1},{6,2},{7,11},{8,12},{9,5},{10,... | collective-permute-start | bytes 393224 | tf_op jit(solution)/shard_map/ppermute | solution.py:43
  43.7 5.0 %collective-permute-start.25 = (bf16[16,4096]{1,0:T(8,128)(2,1)S(1)}, bf16[16,4096]{1,0:T(8,128)(2,1)S(1)}, u32[]{:S(2)}, u32[]{:S(2)}) collective-permute-start(bf16[16,4096]{1,0:T(8,128)(2,1)S(1)} %add_convert_fusion.4), channel_id=1, source_target_pairs={{0,4},{1,3},{2,0},{3,7},{4,8},{5,1},{6,2},{7,11},{8,12},{9,5},{10,... | collective-permute-start | bytes 393224 | tf_op jit(solution)/shard_map/ppermute | solution.py:43
  49.0 5.1 %collective-permute-start.28 = (bf16[16,4224]{1,0:T(8,128)(2,1)S(1)}, bf16[16,4224]{1,0:T(8,128)(2,1)S(1)}, u32[]{:S(2)}, u32[]{:S(2)}) collective-permute-start(bf16[16,4224]{1,0:T(8,128)(2,1)S(1)} %shard_map.108.refs_0_), channel_id=1, source_target_pairs={{0,4},{1,3},{2,0},{3,7},{4,8},{5,1},{6,2},{7,11},{8,12},{9,5},{10,... | collective-permute-start | bytes 405512 | tf_op jit(solution)/shard_map/ppermute | solution.py:43
  52.1 5.1 %collective-permute-start.32 = (bf16[16,4224]{1,0:T(8,128)(2,1)S(1)}, bf16[16,4224]{1,0:T(8,128)(2,1)S(1)}, u32[]{:S(2)}, u32[]{:S(2)}) collective-permute-start(bf16[16,4224]{1,0:T(8,128)(2,1)S(1)} %shard_map.109.refs_8_), channel_id=1, source_target_pairs={{0,4},{1,3},{2,0},{3,7},{4,8},{5,1},{6,2},{7,11},{8,12},{9,5},{10,... | collective-permute-start | bytes 405512 | tf_op jit(solution)/shard_map/ppermute | solution.py:43
  54.0 5.0 %collective-permute-start.29 = (bf16[16,4224]{1,0:T(8,128)(2,1)S(1)}, bf16[16,4224]{1,0:T(8,128)(2,1)S(1)}, u32[]{:S(2)}, u32[]{:S(2)}) collective-permute-start(bf16[16,4224]{1,0:T(8,128)(2,1)S(1)} %collective-permute-done.28.refs_1_), channel_id=1, source_target_pairs={{0,4},{1,3},{2,0},{3,7},{4,8},{5,1},{6,2},{7,11},{8,12},{9,5},{10,... | collective-permute-start | bytes 405512 | tf_op jit(solution)/shard_map/ppermute | solution.py:43
  57.2 5.0 %collective-permute-start.35 = (bf16[16,4224]{1,0:T(8,128)(2,1)S(1)}, bf16[16,4224]{1,0:T(8,128)(2,1)S(1)}, u32[]{:S(2)}, u32[]{:S(2)}) collective-permute-start(bf16[16,4224]{1,0:T(8,128)(2,1)S(1)} %collective-permute-done.32.refs_9_), channel_id=1, source_target_pairs={{0,4},{1,3},{2,0},{3,7},{4,8},{5,1},{6,2},{7,11},{8,12},{9,5},{10,... | collective-permute-start | bytes 405512 | tf_op jit(solution)/shard_map/ppermute | solution.py:43
  59.0 5.0 %collective-permute-start.33 = (bf16[16,4224]{1,0:T(8,128)(2,1)S(1)}, bf16[16,4224]{1,0:T(8,128)(2,1)S(1)}, u32[]{:S(2)}, u32[]{:S(2)}) collective-permute-start(bf16[16,4224]{1,0:T(8,128)(2,1)S(1)} %collective-permute-done.29.refs_2_), channel_id=1, source_target_pairs={{0,4},{1,3},{2,0},{3,7},{4,8},{5,1},{6,2},{7,11},{8,12},{9,5},{10,... | collective-permute-start | bytes 405512 | tf_op jit(solution)/shard_map/ppermute | solution.py:43
  62.2 5.0 %collective-permute-start.37 = (bf16[16,4224]{1,0:T(8,128)(2,1)S(1)}, bf16[16,4224]{1,0:T(8,128)(2,1)S(1)}, u32[]{:S(2)}, u32[]{:S(2)}) collective-permute-start(bf16[16,4224]{1,0:T(8,128)(2,1)S(1)} %collective-permute-done.35.refs_10_), channel_id=1, source_target_pairs={{0,4},{1,3},{2,0},{3,7},{4,8},{5,1},{6,2},{7,11},{8,12},{9,5},{10,... | collective-permute-start | bytes 405512 | tf_op jit(solution)/shard_map/ppermute | solution.py:43
  64.1 5.0 %collective-permute-start.40 = (bf16[16,4224]{1,0:T(8,128)(2,1)S(1)}, bf16[16,4224]{1,0:T(8,128)(2,1)S(1)}, u32[]{:S(2)}, u32[]{:S(2)}) collective-permute-start(bf16[16,4224]{1,0:T(8,128)(2,1)S(1)} %collective-permute-done.33.refs_3_), channel_id=1, source_target_pairs={{0,4},{1,3},{2,0},{3,7},{4,8},{5,1},{6,2},{7,11},{8,12},{9,5},{10,... | collective-permute-start | bytes 405512 | tf_op jit(solution)/shard_map/ppermute | solution.py:43
  70.6 7.3 %collective-permute-start.43 = (f32[8,128]{1,0:T(8,128)S(1)}, f32[8,128]{1,0:T(8,128)S(1)}, u32[]{:S(2)}, u32[]{:S(2)}) collective-permute-start(f32[8,128]{1,0:T(8,128)S(1)} %shard_map.113), channel_id=1, source_target_pairs={{0,16},{16,0},{1,17},{17,1},{2,18},{18,2},{3,19},{19,3},{4,20},{20... | collective-permute-start | bytes 12296 | tf_op jit(solution)/shard_map/ppermute | solution.py:516
  (24 other events, 92.9 us)

commit v6 on v5

--- a/solution.py
+++ b/solution.py
@@ -445,6 +445,22 @@
     )(*[in_vmem(x) for x in pieces])
 
 
+def total_kernel(count, own_ref, *refs):
+    total = functools.reduce(jnp.add, [ref[...] for ref in refs[:-1]], own_ref[...])
+    refs[-1][...] = total[:1, :1] / count
+
+
+def mean_loss(parts, count):
+    return pl.pallas_call(
+        functools.partial(total_kernel, count),
+        out_shape=pltpu.VMEM((1, 1), f32),
+        in_specs=[VMEM_SPEC] * len(parts),
+        out_specs=VMEM_SPEC,
+        compiler_params=pltpu.CompilerParams(vmem_limit_bytes=4 << 20),
+        cost_estimate=SHORT,
+    )(*[in_vmem(x) for x in parts])
+
+
 def body(residual, targets, w_enc, b_enc, w_dec, block_mask):
     rows = residual.shape[1]
     width = residual.shape[2]
@@ -511,14 +527,15 @@
         return held["turned"][-1:]
 
     errors = gather(ring, *payloads, {3: rows_in, 4: rows_in}, False)
-    sent_loss = loss_row = group_loss([piece for parts in errors for piece in parts], rows)
+    group_losses = [group_loss([piece for parts in errors for piece in parts], rows)]
     for _ in range(layers - 1):
-        sent_loss = lax.ppermute(sent_loss, "layer", [(i, (i + 1) % layers) for i in range(layers)])
-        loss_row = loss_row + sent_loss
+        route = [(i, (i + 1) % layers) for i in range(layers)]
+        group_losses.append(lax.ppermute(group_losses[-1], "layer", route))
     enc_grad, bias_grad, dec_grad = backward(
         errors, list(acts), list(gates), held["turned"], decoder, held["norm"], act_sum
     )
-    loss = after(loss_row, bias_grad)[0, 0] / (layers * tokens * width)
+    group_losses[0] = after(group_losses[0], bias_grad)
+    loss = mean_loss(group_losses, layers * tokens * width).reshape(())
     return enc_grad[None], bias_grad, dec_grad[None], loss
 
 

time: 80.4 us -> 79.3 us (0.986)
  no operation moved by 1% of the time
where the time goes in v6:
time: 79.3 us; the launch traced here: 79 us
  starting transfers between devices  39.9 us (50%)
  waiting for transfers between devices  19 us (24%)
  Pallas kernels  17.6 us (22%)
  between operations  2.1 us (3%)
    ppermute x22, starting transfers between devices, along(): return lax.ppermute(block, 'feat', self.step)  34.2 us
    ppermute x22, waiting for transfers between devices, along(): return lax.ppermute(block, 'feat', self.step)  16.3 us
    pallas_call x1, Pallas kernels, backward(): pl.pallas_call(functools.partial(backward_kernel, tuple((len(e) for e in...  5.67 us
    pallas_call x3, Pallas kernels, loaded(): pl.pallas_call(functools.partial(load_kernel, part * rows), out_shape=plt...  4.64 us
    pallas_call x1, Pallas kernels, prepared(): pl.pallas_call(prepare_kernel, out_shape=[pltpu.VMEM(half.shape, half.dty...  3.08 us
    pallas_call x2, Pallas kernels, forward(): pl.pallas_call(functools.partial(forward_kernel, len(pieces), min(512, wi...  2.91 us
    ppermute x20, waiting for transfers between devices, across(): return lax.ppermute(block, 'feat', self.twin)  2.72 us
    ppermute x20, starting transfers between devices, across(): return lax.ppermute(block, 'feat', self.twin)  2.69 us
  transfers between devices with their start and end apart: 44, of which 16 were waited for; matrix products, arithmetic and copies ran while one was open for 0% of the time, Pallas kernels for 20%

profile of v6, /device:TPU:0, one launch (start us, length us, event | category | flops | bytes accessed | tf_op | source)
XLA Modules:
  0.0 79.0 jit_solution(1961150454716531348)
XLA Ops:
  1.1 2.6 %collective-permute-start = (bf16[16,4096]{1,0:T(8,128)(2,1)}, bf16[16,4096]{1,0:T(8,128)(2,1)S(1)}, u32[]{:S(2)}, u32[]{:S(2)}) collective-permute-start(bf16[16,4096]{1,0:T(8,128)(2,1)} %bitcast.10), channel_id=1, source_target_pairs={{0,4},{1,3},{2,0},{3,7},{4,8},{5,1},{6,2},{7,11},{8,12},{9,5},{10,... | collective-permute-start | bytes 393224 | tf_op jit(solution)/shard_map/ppermute | solution.py:43
  3.8 1.6 %collective-permute-start.4 = (bf16[16,4096]{1,0:T(8,128)(2,1)S(1)}, bf16[16,4096]{1,0:T(8,128)(2,1)S(1)}, u32[]{:S(2)}, u32[]{:S(2)}) collective-permute-start(bf16[16,4096]{1,0:T(8,128)(2,1)S(1)} %collective-permute-done.1.signal_ref.refs_0_), channel_id=1, source_target_pairs={{0,4},{1,3},{2,0},{3,7},{4,8},{5,1},{6,2},{7,11},{8,12},{9,5},{10,... | collective-permute-start | bytes 393224 | tf_op jit(solution)/shard_map/ppermute | solution.py:43
  5.4 1.5 %shard_map.102.refs_8_ = bf16[2048,512]{1,0:T(8,128)(2,1)S(1)} custom-call(bf16[4096,512]{1,0:T(8,128)(2,1)} %bitcast.14, bf16[16,4096]{1,0:T(8,128)(2,1)S(1)} %collective-permute-done.1.signal_ref.refs_0_), custom_call_target="tpu_custom_call" | custom-call | tf_op jit(solution)/shard_map/pallas_call | solution.py:327
  6.9 2.0 %collective-permute-start.2 = (bf16[16,4096]{1,0:T(8,128)(2,1)S(1)}, bf16[16,4096]{1,0:T(8,128)(2,1)S(1)}, u32[]{:S(2)}, u32[]{:S(2)}) collective-permute-start(bf16[16,4096]{1,0:T(8,128)(2,1)S(1)} %collective-permute-done.signal_ref.refs_1_), channel_id=1, source_target_pairs={{0,4},{1,3},{2,0},{3,7},{4,8},{5,1},{6,2},{7,11},{8,12},{9,5},{10,... | collective-permute-start | bytes 393224 | tf_op jit(solution)/shard_map/ppermute | solution.py:43
  9.5 1.6 %collective-permute-start.7 = (bf16[16,4096]{1,0:T(8,128)(2,1)S(1)}, bf16[16,4096]{1,0:T(8,128)(2,1)S(1)}, u32[]{:S(2)}, u32[]{:S(2)}) collective-permute-start(bf16[16,4096]{1,0:T(8,128)(2,1)S(1)} %collective-permute-done.4.refs_1_), channel_id=1, source_target_pairs={{0,4},{1,3},{2,0},{3,7},{4,8},{5,1},{6,2},{7,11},{8,12},{9,5},{10,... | collective-permute-start | bytes 393224 | tf_op jit(solution)/shard_map/ppermute | solution.py:43
  11.1 1.5 %shard_map.103.refs_9_ = bf16[2048,512]{1,0:T(8,128)(2,1)S(1)} custom-call(bf16[4096,512]{1,0:T(8,128)(2,1)} %bitcast.15, bf16[16,4096]{1,0:T(8,128)(2,1)S(1)} %collective-permute-done.signal_ref.refs_1_), custom_call_target="tpu_custom_call" | custom-call | tf_op jit(solution)/shard_map/pallas_call | solution.py:327
  12.6 1.6 %collective-permute-start.5 = (bf16[16,4096]{1,0:T(8,128)(2,1)S(1)}, bf16[16,4096]{1,0:T(8,128)(2,1)S(1)}, u32[]{:S(2)}, u32[]{:S(2)}) collective-permute-start(bf16[16,4096]{1,0:T(8,128)(2,1)S(1)} %collective-permute-done.2.signal_ref.refs_2_), channel_id=1, source_target_pairs={{0,4},{1,3},{2,0},{3,7},{4,8},{5,1},{6,2},{7,11},{8,12},{9,5},{10,... | collective-permute-start | bytes 393224 | tf_op jit(solution)/shard_map/ppermute | solution.py:43
  16.3 1.5 %shard_map.104.half_ref.refs_10_.refs_22_ = bf16[256,4096]{1,0:T(8,128)(2,1)S(1)} custom-call(bf16[512,4096]{1,0:T(8,128)(2,1)} %bitcast.16, bf16[16,4096]{1,0:T(8,128)(2,1)S(1)} %collective-permute-done.2.signal_ref.refs_2_), custom_call_target="tpu_custom_call" | custom-call | tf_op jit(solution)/shard_map/pallas_call | solution.py:327
  21.3 3.1 %shard_map.105 = (bf16[256,4096]{1,0:T(8,128)(2,1)S(1)}, f32[1,512]{1,0:T(1,128)S(1)}, f32[128,512]{1,0:T(8,128)S(1)}, f32[128,512]{1,0:T(8,128)S(1)}) custom-call(s32[2,4]{1,0:T(2,128)S(1)} %bitcast.13, f32[16,1,256]{2,1,0:T(1,128)} %constant.4.clone.table_ref, bf16[256,4096]{1,0:T(8,128)(2,1)S(1)} %shard_map.104.half_ref.refs_10_.refs_22_, ...), custom_call_target="tpu_custom_call" | custom-call | tf_op jit(solution)/shard_map/pallas_call | solution.py:377
  28.4 1.6 %collective-permute-start.16 = (bf16[16,4096]{1,0:T(8,128)(2,1)S(1)}, bf16[16,4096]{1,0:T(8,128)(2,1)S(1)}, u32[]{:S(2)}, u32[]{:S(2)}) collective-permute-start(bf16[16,4096]{1,0:T(8,128)(2,1)S(1)} %add_convert_fusion.8), channel_id=1, source_target_pairs={{0,4},{1,3},{2,0},{3,7},{4,8},{5,1},{6,2},{7,11},{8,12},{9,5},{10,... | collective-permute-start | bytes 393224 | tf_op jit(solution)/shard_map/ppermute | solution.py:43
  31.4 2.1 %collective-permute-done.16 = bf16[16,4096]{1,0:T(8,128)(2,1)S(1)} collective-permute-done((bf16[16,4096]{1,0:T(8,128)(2,1)S(1)}, bf16[16,4096]{1,0:T(8,128)(2,1)S(1)}, u32[]{:S(2)}, u32[]{:S(2)}) %collective-permute-start.16) | collective-permute-done | bytes 131104 | tf_op jit(solution)/shard_map/ppermute | solution.py:43
  33.5 1.6 %collective-permute-start.17 = (bf16[16,4096]{1,0:T(8,128)(2,1)S(1)}, bf16[16,4096]{1,0:T(8,128)(2,1)S(1)}, u32[]{:S(2)}, u32[]{:S(2)}) collective-permute-start(bf16[16,4096]{1,0:T(8,128)(2,1)S(1)} %add_convert_fusion.7), channel_id=1, source_target_pairs={{0,4},{1,3},{2,0},{3,7},{4,8},{5,1},{6,2},{7,11},{8,12},{9,5},{10,... | collective-permute-start | bytes 393224 | tf_op jit(solution)/shard_map/ppermute | solution.py:43
  36.5 1.5 %collective-permute-start.22 = (bf16[16,4096]{1,0:T(8,128)(2,1)S(1)}, bf16[16,4096]{1,0:T(8,128)(2,1)S(1)}, u32[]{:S(2)}, u32[]{:S(2)}) collective-permute-start(bf16[16,4096]{1,0:T(8,128)(2,1)S(1)} %bitcast.20), channel_id=1, source_target_pairs={{0,16},{16,0},{1,17},{17,1},{2,18},{18,2},{3,19},{19,3},{4,20},{20... | collective-permute-start | bytes 393224 | tf_op jit(solution)/shard_map/ppermute | solution.py:510
  38.6 1.6 %collective-permute-start.20 = (bf16[16,4096]{1,0:T(8,128)(2,1)S(1)}, bf16[16,4096]{1,0:T(8,128)(2,1)S(1)}, u32[]{:S(2)}, u32[]{:S(2)}) collective-permute-start(bf16[16,4096]{1,0:T(8,128)(2,1)S(1)} %add_convert_fusion.6), channel_id=1, source_target_pairs={{0,4},{1,3},{2,0},{3,7},{4,8},{5,1},{6,2},{7,11},{8,12},{9,5},{10,... | collective-permute-start | bytes 393224 | tf_op jit(solution)/shard_map/ppermute | solution.py:43
  41.6 2.0 %collective-permute-done.20 = bf16[16,4096]{1,0:T(8,128)(2,1)S(1)} collective-permute-done((bf16[16,4096]{1,0:T(8,128)(2,1)S(1)}, bf16[16,4096]{1,0:T(8,128)(2,1)S(1)}, u32[]{:S(2)}, u32[]{:S(2)}) %collective-permute-start.20) | collective-permute-done | bytes 131104 | tf_op jit(solution)/shard_map/ppermute | solution.py:43
  43.7 1.6 %collective-permute-start.25 = (bf16[16,4096]{1,0:T(8,128)(2,1)S(1)}, bf16[16,4096]{1,0:T(8,128)(2,1)S(1)}, u32[]{:S(2)}, u32[]{:S(2)}) collective-permute-start(bf16[16,4096]{1,0:T(8,128)(2,1)S(1)} %add_convert_fusion.4), channel_id=1, source_target_pairs={{0,4},{1,3},{2,0},{3,7},{4,8},{5,1},{6,2},{7,11},{8,12},{9,5},{10,... | collective-permute-start | bytes 393224 | tf_op jit(solution)/shard_map/ppermute | solution.py:43
  45.3 3.3 %collective-permute-done.25 = bf16[16,4096]{1,0:T(8,128)(2,1)S(1)} collective-permute-done((bf16[16,4096]{1,0:T(8,128)(2,1)S(1)}, bf16[16,4096]{1,0:T(8,128)(2,1)S(1)}, u32[]{:S(2)}, u32[]{:S(2)}) %collective-permute-start.25) | collective-permute-done | bytes 131104 | tf_op jit(solution)/shard_map/ppermute | solution.py:43
  49.0 1.6 %collective-permute-start.28 = (bf16[16,4224]{1,0:T(8,128)(2,1)S(1)}, bf16[16,4224]{1,0:T(8,128)(2,1)S(1)}, u32[]{:S(2)}, u32[]{:S(2)}) collective-permute-start(bf16[16,4224]{1,0:T(8,128)(2,1)S(1)} %shard_map.108.refs_0_), channel_id=1, source_target_pairs={{0,4},{1,3},{2,0},{3,7},{4,8},{5,1},{6,2},{7,11},{8,12},{9,5},{10,... | collective-permute-start | bytes 405512 | tf_op jit(solution)/shard_map/ppermute | solution.py:43
  55.5 1.6 %collective-permute-done.32.refs_9_ = bf16[16,4224]{1,0:T(8,128)(2,1)S(1)} collective-permute-done((bf16[16,4224]{1,0:T(8,128)(2,1)S(1)}, bf16[16,4224]{1,0:T(8,128)(2,1)S(1)}, u32[]{:S(2)}, u32[]{:S(2)}) %collective-permute-start.32) | collective-permute-done | bytes 135200 | tf_op jit(solution)/shard_map/ppermute | solution.py:43
  60.5 1.6 %collective-permute-done.35.refs_10_ = bf16[16,4224]{1,0:T(8,128)(2,1)S(1)} collective-permute-done((bf16[16,4224]{1,0:T(8,128)(2,1)S(1)}, bf16[16,4224]{1,0:T(8,128)(2,1)S(1)}, u32[]{:S(2)}, u32[]{:S(2)}) %collective-permute-start.35) | collective-permute-done | bytes 135200 | tf_op jit(solution)/shard_map/ppermute | solution.py:43
  64.1 1.5 %collective-permute-start.40 = (bf16[16,4224]{1,0:T(8,128)(2,1)S(1)}, bf16[16,4224]{1,0:T(8,128)(2,1)S(1)}, u32[]{:S(2)}, u32[]{:S(2)}) collective-permute-start(bf16[16,4224]{1,0:T(8,128)(2,1)S(1)} %collective-permute-done.33.refs_3_), channel_id=1, source_target_pairs={{0,4},{1,3},{2,0},{3,7},{4,8},{5,1},{6,2},{7,11},{8,12},{9,5},{10,... | collective-permute-start | bytes 405512 | tf_op jit(solution)/shard_map/ppermute | solution.py:43
  67.2 1.9 %collective-permute-done.40.refs_7_ = bf16[16,4224]{1,0:T(8,128)(2,1)S(1)} collective-permute-done((bf16[16,4224]{1,0:T(8,128)(2,1)S(1)}, bf16[16,4224]{1,0:T(8,128)(2,1)S(1)}, u32[]{:S(2)}, u32[]{:S(2)}) %collective-permute-start.40) | collective-permute-done | bytes 135200 | tf_op jit(solution)/shard_map/ppermute | solution.py:43
  70.6 1.6 %collective-permute-start.43 = (f32[8,128]{1,0:T(8,128)S(1)}, f32[8,128]{1,0:T(8,128)S(1)}, u32[]{:S(2)}, u32[]{:S(2)}) collective-permute-start(f32[8,128]{1,0:T(8,128)S(1)} %shard_map.113.own_ref), channel_id=1, source_target_pairs={{0,16},{16,0},{1,17},{17,1},{2,18},{18,2},{3,19},{19,3},{4,20},{20... | collective-permute-start | bytes 12296 | tf_op jit(solution)/shard_map/ppermute | solution.py:533
  72.2 5.7 %shard_map.112 = (bf16[4096,512]{1,0:T(8,128)(2,1)}, f32[1,512]{1,0:T(1,128)}, bf16[512,4096]{1,0:T(8,128)(2,1)}) custom-call(bf16[16,4224]{1,0:T(8,128)(2,1)S(1)} %shard_map.108.refs_0_, bf16[16,4224]{1,0:T(8,128)(2,1)S(1)} %collective-permute-done.28.refs_1_, bf16[16,4224]{1,0:T(8,128)(2,1)S(1)} %collective-permute-done.29.refs_2_, ...), custom_call_target="tpu_custom_call" | custom-call | tf_op jit(solution)/shard_map/pallas_call | solution.py:291
  (95 shorter events, 29.1 us)
Async XLA Ops:
  1.1 5.8 %collective-permute-start = (bf16[16,4096]{1,0:T(8,128)(2,1)}, bf16[16,4096]{1,0:T(8,128)(2,1)S(1)}, u32[]{:S(2)}, u32[]{:S(2)}) collective-permute-start(bf16[16,4096]{1,0:T(8,128)(2,1)} %bitcast.10), channel_id=1, source_target_pairs={{0,4},{1,3},{2,0},{3,7},{4,8},{5,1},{6,2},{7,11},{8,12},{9,5},{10,... | collective-permute-start | bytes 393224 | tf_op jit(solution)/shard_map/ppermute | solution.py:43
  3.8 5.2 %collective-permute-start.4 = (bf16[16,4096]{1,0:T(8,128)(2,1)S(1)}, bf16[16,4096]{1,0:T(8,128)(2,1)S(1)}, u32[]{:S(2)}, u32[]{:S(2)}) collective-permute-start(bf16[16,4096]{1,0:T(8,128)(2,1)S(1)} %collective-permute-done.1.signal_ref.refs_0_), channel_id=1, source_target_pairs={{0,4},{1,3},{2,0},{3,7},{4,8},{5,1},{6,2},{7,11},{8,12},{9,5},{10,... | collective-permute-start | bytes 393224 | tf_op jit(solution)/shard_map/ppermute | solution.py:43
  6.9 5.7 %collective-permute-start.2 = (bf16[16,4096]{1,0:T(8,128)(2,1)S(1)}, bf16[16,4096]{1,0:T(8,128)(2,1)S(1)}, u32[]{:S(2)}, u32[]{:S(2)}) collective-permute-start(bf16[16,4096]{1,0:T(8,128)(2,1)S(1)} %collective-permute-done.signal_ref.refs_1_), channel_id=1, source_target_pairs={{0,4},{1,3},{2,0},{3,7},{4,8},{5,1},{6,2},{7,11},{8,12},{9,5},{10,... | collective-permute-start | bytes 393224 | tf_op jit(solution)/shard_map/ppermute | solution.py:43
  9.0 5.3 %collective-permute-start.6 = (bf16[16,4096]{1,0:T(8,128)(2,1)S(1)}, bf16[16,4096]{1,0:T(8,128)(2,1)S(1)}, u32[]{:S(2)}, u32[]{:S(2)}) collective-permute-start(bf16[16,4096]{1,0:T(8,128)(2,1)S(1)} %collective-permute-done.4.refs_1_), channel_id=1, source_target_pairs={{0,1},{1,0},{2,3},{3,2},{4,5},{5,4},{6,7},{7,6},{8,9},{9,8},{10,11... | collective-permute-start | bytes 393224 | tf_op jit(solution)/shard_map/ppermute | solution.py:46
  12.6 5.2 %collective-permute-start.5 = (bf16[16,4096]{1,0:T(8,128)(2,1)S(1)}, bf16[16,4096]{1,0:T(8,128)(2,1)S(1)}, u32[]{:S(2)}, u32[]{:S(2)}) collective-permute-start(bf16[16,4096]{1,0:T(8,128)(2,1)S(1)} %collective-permute-done.2.signal_ref.refs_2_), channel_id=1, source_target_pairs={{0,4},{1,3},{2,0},{3,7},{4,8},{5,1},{6,2},{7,11},{8,12},{9,5},{10,... | collective-permute-start | bytes 393224 | tf_op jit(solution)/shard_map/ppermute | solution.py:43
  17.9 6.5 %collective-permute-start.12 = (bf16[16,4096]{1,0:T(8,128)(2,1)S(1)}, bf16[16,4096]{1,0:T(8,128)(2,1)S(1)}, u32[]{:S(2)}, u32[]{:S(2)}) collective-permute-start(bf16[16,4096]{1,0:T(8,128)(2,1)S(1)} %collective-permute-done.5.refs_3_), channel_id=1, source_target_pairs={{0,4},{1,3},{2,0},{3,7},{4,8},{5,1},{6,2},{7,11},{8,12},{9,5},{10,... | collective-permute-start | bytes 393224 | tf_op jit(solution)/shard_map/ppermute | solution.py:43
  19.3 5.1 %collective-permute-start.13 = (bf16[16,4096]{1,0:T(8,128)(2,1)S(1)}, bf16[16,4096]{1,0:T(8,128)(2,1)S(1)}, u32[]{:S(2)}, u32[]{:S(2)}) collective-permute-start(bf16[16,4096]{1,0:T(8,128)(2,1)S(1)} %collective-permute-done.5.refs_3_), channel_id=1, source_target_pairs={{0,1},{1,0},{2,3},{3,2},{4,5},{5,4},{6,7},{7,6},{8,9},{9,8},{10,11... | collective-permute-start | bytes 393224 | tf_op jit(solution)/shard_map/ppermute | solution.py:46
  28.3 15.3 %collective-permute-start.24 = (f32[1,512]{1,0:T(1,128)S(1)}, f32[1,512]{1,0:T(1,128)S(1)}, u32[]{:S(2)}, u32[]{:S(2)}) collective-permute-start(f32[1,512]{1,0:T(1,128)S(1)} %get-tuple-element.148.refs_3_), channel_id=1, source_target_pairs={{0,1},{1,0},{2,3},{3,2},{4,5},{5,4},{6,7},{7,6},{8,9},{9,8},{10,11... | collective-permute-start | bytes 6152 | tf_op jit(solution)/shard_map/ppermute | solution.py:46
  28.4 5.0 %collective-permute-start.16 = (bf16[16,4096]{1,0:T(8,128)(2,1)S(1)}, bf16[16,4096]{1,0:T(8,128)(2,1)S(1)}, u32[]{:S(2)}, u32[]{:S(2)}) collective-permute-start(bf16[16,4096]{1,0:T(8,128)(2,1)S(1)} %add_convert_fusion.8), channel_id=1, source_target_pairs={{0,4},{1,3},{2,0},{3,7},{4,8},{5,1},{6,2},{7,11},{8,12},{9,5},{10,... | collective-permute-start | bytes 393224 | tf_op jit(solution)/shard_map/ppermute | solution.py:43
  30.0 5.0 %collective-permute-start.19 = (bf16[16,4096]{1,0:T(8,128)(2,1)S(1)}, bf16[16,4096]{1,0:T(8,128)(2,1)S(1)}, u32[]{:S(2)}, u32[]{:S(2)}) collective-permute-start(bf16[16,4096]{1,0:T(8,128)(2,1)S(1)} %add_convert_fusion.5), channel_id=1, source_target_pairs={{0,4},{1,3},{2,0},{3,7},{4,8},{5,1},{6,2},{7,11},{8,12},{9,5},{10,... | collective-permute-start | bytes 393224 | tf_op jit(solution)/shard_map/ppermute | solution.py:43
  33.5 5.0 %collective-permute-start.17 = (bf16[16,4096]{1,0:T(8,128)(2,1)S(1)}, bf16[16,4096]{1,0:T(8,128)(2,1)S(1)}, u32[]{:S(2)}, u32[]{:S(2)}) collective-permute-start(bf16[16,4096]{1,0:T(8,128)(2,1)S(1)} %add_convert_fusion.7), channel_id=1, source_target_pairs={{0,4},{1,3},{2,0},{3,7},{4,8},{5,1},{6,2},{7,11},{8,12},{9,5},{10,... | collective-permute-start | bytes 393224 | tf_op jit(solution)/shard_map/ppermute | solution.py:43
  35.1 5.0 %collective-permute-start.21 = (bf16[16,4096]{1,0:T(8,128)(2,1)S(1)}, bf16[16,4096]{1,0:T(8,128)(2,1)S(1)}, u32[]{:S(2)}, u32[]{:S(2)}) collective-permute-start(bf16[16,4096]{1,0:T(8,128)(2,1)S(1)} %add_convert_fusion.3), channel_id=1, source_target_pairs={{0,4},{1,3},{2,0},{3,7},{4,8},{5,1},{6,2},{7,11},{8,12},{9,5},{10,... | collective-permute-start | bytes 393224 | tf_op jit(solution)/shard_map/ppermute | solution.py:43
  36.5 5.1 %collective-permute-start.22 = (bf16[16,4096]{1,0:T(8,128)(2,1)S(1)}, bf16[16,4096]{1,0:T(8,128)(2,1)S(1)}, u32[]{:S(2)}, u32[]{:S(2)}) collective-permute-start(bf16[16,4096]{1,0:T(8,128)(2,1)S(1)} %bitcast.20), channel_id=1, source_target_pairs={{0,16},{16,0},{1,17},{17,1},{2,18},{18,2},{3,19},{19,3},{4,20},{20... | collective-permute-start | bytes 393224 | tf_op jit(solution)/shard_map/ppermute | solution.py:510
  38.6 5.0 %collective-permute-start.20 = (bf16[16,4096]{1,0:T(8,128)(2,1)S(1)}, bf16[16,4096]{1,0:T(8,128)(2,1)S(1)}, u32[]{:S(2)}, u32[]{:S(2)}) collective-permute-start(bf16[16,4096]{1,0:T(8,128)(2,1)S(1)} %add_convert_fusion.6), channel_id=1, source_target_pairs={{0,4},{1,3},{2,0},{3,7},{4,8},{5,1},{6,2},{7,11},{8,12},{9,5},{10,... | collective-permute-start | bytes 393224 | tf_op jit(solution)/shard_map/ppermute | solution.py:43
  40.2 5.0 %collective-permute-start.26 = (bf16[16,4096]{1,0:T(8,128)(2,1)S(1)}, bf16[16,4096]{1,0:T(8,128)(2,1)S(1)}, u32[]{:S(2)}, u32[]{:S(2)}) collective-permute-start(bf16[16,4096]{1,0:T(8,128)(2,1)S(1)} %add_convert_fusion.1), channel_id=1, source_target_pairs={{0,4},{1,3},{2,0},{3,7},{4,8},{5,1},{6,2},{7,11},{8,12},{9,5},{10,... | collective-permute-start | bytes 393224 | tf_op jit(solution)/shard_map/ppermute | solution.py:43
  43.7 5.0 %collective-permute-start.25 = (bf16[16,4096]{1,0:T(8,128)(2,1)S(1)}, bf16[16,4096]{1,0:T(8,128)(2,1)S(1)}, u32[]{:S(2)}, u32[]{:S(2)}) collective-permute-start(bf16[16,4096]{1,0:T(8,128)(2,1)S(1)} %add_convert_fusion.4), channel_id=1, source_target_pairs={{0,4},{1,3},{2,0},{3,7},{4,8},{5,1},{6,2},{7,11},{8,12},{9,5},{10,... | collective-permute-start | bytes 393224 | tf_op jit(solution)/shard_map/ppermute | solution.py:43
  49.0 5.1 %collective-permute-start.28 = (bf16[16,4224]{1,0:T(8,128)(2,1)S(1)}, bf16[16,4224]{1,0:T(8,128)(2,1)S(1)}, u32[]{:S(2)}, u32[]{:S(2)}) collective-permute-start(bf16[16,4224]{1,0:T(8,128)(2,1)S(1)} %shard_map.108.refs_0_), channel_id=1, source_target_pairs={{0,4},{1,3},{2,0},{3,7},{4,8},{5,1},{6,2},{7,11},{8,12},{9,5},{10,... | collective-permute-start | bytes 405512 | tf_op jit(solution)/shard_map/ppermute | solution.py:43
  52.1 5.1 %collective-permute-start.32 = (bf16[16,4224]{1,0:T(8,128)(2,1)S(1)}, bf16[16,4224]{1,0:T(8,128)(2,1)S(1)}, u32[]{:S(2)}, u32[]{:S(2)}) collective-permute-start(bf16[16,4224]{1,0:T(8,128)(2,1)S(1)} %shard_map.109.refs_8_), channel_id=1, source_target_pairs={{0,4},{1,3},{2,0},{3,7},{4,8},{5,1},{6,2},{7,11},{8,12},{9,5},{10,... | collective-permute-start | bytes 405512 | tf_op jit(solution)/shard_map/ppermute | solution.py:43
  54.0 5.0 %collective-permute-start.29 = (bf16[16,4224]{1,0:T(8,128)(2,1)S(1)}, bf16[16,4224]{1,0:T(8,128)(2,1)S(1)}, u32[]{:S(2)}, u32[]{:S(2)}) collective-permute-start(bf16[16,4224]{1,0:T(8,128)(2,1)S(1)} %collective-permute-done.28.refs_1_), channel_id=1, source_target_pairs={{0,4},{1,3},{2,0},{3,7},{4,8},{5,1},{6,2},{7,11},{8,12},{9,5},{10,... | collective-permute-start | bytes 405512 | tf_op jit(solution)/shard_map/ppermute | solution.py:43
  57.2 5.0 %collective-permute-start.35 = (bf16[16,4224]{1,0:T(8,128)(2,1)S(1)}, bf16[16,4224]{1,0:T(8,128)(2,1)S(1)}, u32[]{:S(2)}, u32[]{:S(2)}) collective-permute-start(bf16[16,4224]{1,0:T(8,128)(2,1)S(1)} %collective-permute-done.32.refs_9_), channel_id=1, source_target_pairs={{0,4},{1,3},{2,0},{3,7},{4,8},{5,1},{6,2},{7,11},{8,12},{9,5},{10,... | collective-permute-start | bytes 405512 | tf_op jit(solution)/shard_map/ppermute | solution.py:43
  59.0 5.0 %collective-permute-start.33 = (bf16[16,4224]{1,0:T(8,128)(2,1)S(1)}, bf16[16,4224]{1,0:T(8,128)(2,1)S(1)}, u32[]{:S(2)}, u32[]{:S(2)}) collective-permute-start(bf16[16,4224]{1,0:T(8,128)(2,1)S(1)} %collective-permute-done.29.refs_2_), channel_id=1, source_target_pairs={{0,4},{1,3},{2,0},{3,7},{4,8},{5,1},{6,2},{7,11},{8,12},{9,5},{10,... | collective-permute-start | bytes 405512 | tf_op jit(solution)/shard_map/ppermute | solution.py:43
  62.2 5.0 %collective-permute-start.37 = (bf16[16,4224]{1,0:T(8,128)(2,1)S(1)}, bf16[16,4224]{1,0:T(8,128)(2,1)S(1)}, u32[]{:S(2)}, u32[]{:S(2)}) collective-permute-start(bf16[16,4224]{1,0:T(8,128)(2,1)S(1)} %collective-permute-done.35.refs_10_), channel_id=1, source_target_pairs={{0,4},{1,3},{2,0},{3,7},{4,8},{5,1},{6,2},{7,11},{8,12},{9,5},{10,... | collective-permute-start | bytes 405512 | tf_op jit(solution)/shard_map/ppermute | solution.py:43
  64.1 5.0 %collective-permute-start.40 = (bf16[16,4224]{1,0:T(8,128)(2,1)S(1)}, bf16[16,4224]{1,0:T(8,128)(2,1)S(1)}, u32[]{:S(2)}, u32[]{:S(2)}) collective-permute-start(bf16[16,4224]{1,0:T(8,128)(2,1)S(1)} %collective-permute-done.33.refs_3_), channel_id=1, source_target_pairs={{0,4},{1,3},{2,0},{3,7},{4,8},{5,1},{6,2},{7,11},{8,12},{9,5},{10,... | collective-permute-start | bytes 405512 | tf_op jit(solution)/shard_map/ppermute | solution.py:43
  70.6 7.3 %collective-permute-start.43 = (f32[8,128]{1,0:T(8,128)S(1)}, f32[8,128]{1,0:T(8,128)S(1)}, u32[]{:S(2)}, u32[]{:S(2)}) collective-permute-start(f32[8,128]{1,0:T(8,128)S(1)} %shard_map.113.own_ref), channel_id=1, source_target_pairs={{0,16},{16,0},{1,17},{17,1},{2,18},{18,2},{3,19},{19,3},{4,20},{20... | collective-permute-start | bytes 12296 | tf_op jit(solution)/shard_map/ppermute | solution.py:533
  (24 other events, 92.9 us)

commit v7 on v6

--- a/solution.py
+++ b/solution.py
@@ -78,8 +78,9 @@
             block = after(moving[chain], front[chain][k - 2]) if k >= 2 else moving[chain]
             moving[chain] = ring.along(turns.enter(chain, block))
             turns.leave(chain, moving[chain])
-            if k < ring.hops:
-                front[chain].append(ring.across(moving[chain]))
+            if k < ring.hops and chain == 1:
+                front[0].append(ring.across(after(turns.ended[0][k], moving[1])))
+                front[1].append(ring.across(moving[1]))
     last = [[], []]
     if ring.far:
         last = [[moving[0]], [moving[1] if direct else ring.across(moving[0])]]

time: 79.3 us -> 79.1 us (level)
  waiting for transfers between devices: 19 us -> 16.1 us
  starting transfers between devices: 39.9 us -> 42.6 us
    ppermute x22, starting transfers between devices: 34.2 us -> 37.1 us  [along(): return lax.ppermute(block, 'feat', self.step)]
    ppermute x22, waiting for transfers between devices: 16.3 us -> 14.8 us  [along(): return lax.ppermute(block, 'feat', self.step)]
    ppermute x20, waiting for transfers between devices: 2.72 us -> 1.38 us  [across(): return lax.ppermute(block, 'feat', self.twin)]
  transfers between devices with their start and end apart: 44 -> 44, of which waited for: 16 -> 14; matrix products, arithmetic and copies ran while one was open for 0% -> 0% of each run, Pallas kernels for 20% -> 20%
where the time goes in v7:
time: 79.1 us; the launch traced here: 78.8 us
  starting transfers between devices  42.6 us (54%)
  Pallas kernels  17.5 us (22%)
  waiting for transfers between devices  16.1 us (20%)
  between operations  2.1 us (3%)
    ppermute x22, starting transfers between devices, along(): return lax.ppermute(block, 'feat', self.step)  37.1 us
    ppermute x22, waiting for transfers between devices, along(): return lax.ppermute(block, 'feat', self.step)  14.8 us
    pallas_call x1, Pallas kernels, backward(): pl.pallas_call(functools.partial(backward_kernel, tuple((len(e) for e in...  5.68 us
    pallas_call x3, Pallas kernels, loaded(): pl.pallas_call(functools.partial(load_kernel, part * rows), out_shape=plt...  4.64 us
    pallas_call x1, Pallas kernels, prepared(): pl.pallas_call(prepare_kernel, out_shape=[pltpu.VMEM(half.shape, half.dty...  3.08 us
    pallas_call x2, Pallas kernels, forward(): pl.pallas_call(functools.partial(forward_kernel, len(pieces), min(512, wi...  2.9 us
    ppermute x20, starting transfers between devices, across(): return lax.ppermute(block, 'feat', self.twin)  2.41 us
  transfers between devices with their start and end apart: 44, of which 14 were waited for; matrix products, arithmetic and copies ran while one was open for 0% of the time, Pallas kernels for 20%

profile of v7, /device:TPU:0, one launch (start us, length us, event | category | flops | bytes accessed | tf_op | source)
XLA Modules:
  0.0 78.8 jit_solution(17724381743271796370)
XLA Ops:
  1.1 2.6 %collective-permute-start = (bf16[16,4096]{1,0:T(8,128)(2,1)}, bf16[16,4096]{1,0:T(8,128)(2,1)S(1)}, u32[]{:S(2)}, u32[]{:S(2)}) collective-permute-start(bf16[16,4096]{1,0:T(8,128)(2,1)} %bitcast.10), channel_id=1, source_target_pairs={{0,4},{1,3},{2,0},{3,7},{4,8},{5,1},{6,2},{7,11},{8,12},{9,5},{10,... | collective-permute-start | bytes 393224 | tf_op jit(solution)/shard_map/ppermute | solution.py:43
  6.9 2.0 %collective-permute-start.2 = (bf16[16,4096]{1,0:T(8,128)(2,1)S(1)}, bf16[16,4096]{1,0:T(8,128)(2,1)S(1)}, u32[]{:S(2)}, u32[]{:S(2)}) collective-permute-start(bf16[16,4096]{1,0:T(8,128)(2,1)S(1)} %collective-permute-done.signal_ref.refs_1_), channel_id=1, source_target_pairs={{0,4},{1,3},{2,0},{3,7},{4,8},{5,1},{6,2},{7,11},{8,12},{9,5},{10,... | collective-permute-start | bytes 393224 | tf_op jit(solution)/shard_map/ppermute | solution.py:43
  12.1 1.8 %collective-permute-start.5 = (bf16[16,4096]{1,0:T(8,128)(2,1)S(1)}, bf16[16,4096]{1,0:T(8,128)(2,1)S(1)}, u32[]{:S(2)}, u32[]{:S(2)}) collective-permute-start(bf16[16,4096]{1,0:T(8,128)(2,1)S(1)} %collective-permute-done.2.signal_ref.refs_2_), channel_id=1, source_target_pairs={{0,4},{1,3},{2,0},{3,7},{4,8},{5,1},{6,2},{7,11},{8,12},{9,5},{10,... | collective-permute-start | bytes 393224 | tf_op jit(solution)/shard_map/ppermute | solution.py:43
  13.9 1.6 %collective-permute-start.9 = (bf16[16,4096]{1,0:T(8,128)(2,1)S(1)}, bf16[16,4096]{1,0:T(8,128)(2,1)S(1)}, u32[]{:S(2)}, u32[]{:S(2)}) collective-permute-start(bf16[16,4096]{1,0:T(8,128)(2,1)S(1)} %collective-permute-done.7.refs_2_), channel_id=1, source_target_pairs={{0,4},{1,3},{2,0},{3,7},{4,8},{5,1},{6,2},{7,11},{8,12},{9,5},{10,... | collective-permute-start | bytes 393224 | tf_op jit(solution)/shard_map/ppermute | solution.py:43
  17.2 1.7 %collective-permute-start.12 = (bf16[16,4096]{1,0:T(8,128)(2,1)S(1)}, bf16[16,4096]{1,0:T(8,128)(2,1)S(1)}, u32[]{:S(2)}, u32[]{:S(2)}) collective-permute-start(bf16[16,4096]{1,0:T(8,128)(2,1)S(1)} %collective-permute-done.5.refs_3_), channel_id=1, source_target_pairs={{0,4},{1,3},{2,0},{3,7},{4,8},{5,1},{6,2},{7,11},{8,12},{9,5},{10,... | collective-permute-start | bytes 393224 | tf_op jit(solution)/shard_map/ppermute | solution.py:43
  21.1 3.1 %shard_map.105 = (bf16[256,4096]{1,0:T(8,128)(2,1)S(1)}, f32[1,512]{1,0:T(1,128)S(1)}, f32[128,512]{1,0:T(8,128)S(1)}, f32[128,512]{1,0:T(8,128)S(1)}) custom-call(s32[2,4]{1,0:T(2,128)S(1)} %bitcast.13, f32[16,1,256]{2,1,0:T(1,128)} %constant.4.clone.table_ref, bf16[256,4096]{1,0:T(8,128)(2,1)S(1)} %shard_map.104.half_ref.refs_10_.refs_22_, ...), custom_call_target="tpu_custom_call" | custom-call | tf_op jit(solution)/shard_map/pallas_call | solution.py:378
  28.1 1.6 %collective-permute-start.16 = (bf16[16,4096]{1,0:T(8,128)(2,1)S(1)}, bf16[16,4096]{1,0:T(8,128)(2,1)S(1)}, u32[]{:S(2)}, u32[]{:S(2)}) collective-permute-start(bf16[16,4096]{1,0:T(8,128)(2,1)S(1)} %add_convert_fusion.8), channel_id=1, source_target_pairs={{0,4},{1,3},{2,0},{3,7},{4,8},{5,1},{6,2},{7,11},{8,12},{9,5},{10,... | collective-permute-start | bytes 393224 | tf_op jit(solution)/shard_map/ppermute | solution.py:43
  29.8 1.6 %collective-permute-start.19 = (bf16[16,4096]{1,0:T(8,128)(2,1)S(1)}, bf16[16,4096]{1,0:T(8,128)(2,1)S(1)}, u32[]{:S(2)}, u32[]{:S(2)}) collective-permute-start(bf16[16,4096]{1,0:T(8,128)(2,1)S(1)} %add_convert_fusion.5), channel_id=1, source_target_pairs={{0,4},{1,3},{2,0},{3,7},{4,8},{5,1},{6,2},{7,11},{8,12},{9,5},{10,... | collective-permute-start | bytes 393224 | tf_op jit(solution)/shard_map/ppermute | solution.py:43
  31.4 1.7 %collective-permute-done.16 = bf16[16,4096]{1,0:T(8,128)(2,1)S(1)} collective-permute-done((bf16[16,4096]{1,0:T(8,128)(2,1)S(1)}, bf16[16,4096]{1,0:T(8,128)(2,1)S(1)}, u32[]{:S(2)}, u32[]{:S(2)}) %collective-permute-start.16) | collective-permute-done | bytes 131104 | tf_op jit(solution)/shard_map/ppermute | solution.py:43
  33.2 1.6 %collective-permute-start.17 = (bf16[16,4096]{1,0:T(8,128)(2,1)S(1)}, bf16[16,4096]{1,0:T(8,128)(2,1)S(1)}, u32[]{:S(2)}, u32[]{:S(2)}) collective-permute-start(bf16[16,4096]{1,0:T(8,128)(2,1)S(1)} %add_convert_fusion.7), channel_id=1, source_target_pairs={{0,4},{1,3},{2,0},{3,7},{4,8},{5,1},{6,2},{7,11},{8,12},{9,5},{10,... | collective-permute-start | bytes 393224 | tf_op jit(solution)/shard_map/ppermute | solution.py:43
  34.9 1.6 %collective-permute-start.21 = (bf16[16,4096]{1,0:T(8,128)(2,1)S(1)}, bf16[16,4096]{1,0:T(8,128)(2,1)S(1)}, u32[]{:S(2)}, u32[]{:S(2)}) collective-permute-start(bf16[16,4096]{1,0:T(8,128)(2,1)S(1)} %add_convert_fusion.3), channel_id=1, source_target_pairs={{0,4},{1,3},{2,0},{3,7},{4,8},{5,1},{6,2},{7,11},{8,12},{9,5},{10,... | collective-permute-start | bytes 393224 | tf_op jit(solution)/shard_map/ppermute | solution.py:43
  38.3 1.6 %collective-permute-start.20 = (bf16[16,4096]{1,0:T(8,128)(2,1)S(1)}, bf16[16,4096]{1,0:T(8,128)(2,1)S(1)}, u32[]{:S(2)}, u32[]{:S(2)}) collective-permute-start(bf16[16,4096]{1,0:T(8,128)(2,1)S(1)} %add_convert_fusion.6), channel_id=1, source_target_pairs={{0,4},{1,3},{2,0},{3,7},{4,8},{5,1},{6,2},{7,11},{8,12},{9,5},{10,... | collective-permute-start | bytes 393224 | tf_op jit(solution)/shard_map/ppermute | solution.py:43
  40.0 1.6 %collective-permute-start.26 = (bf16[16,4096]{1,0:T(8,128)(2,1)S(1)}, bf16[16,4096]{1,0:T(8,128)(2,1)S(1)}, u32[]{:S(2)}, u32[]{:S(2)}) collective-permute-start(bf16[16,4096]{1,0:T(8,128)(2,1)S(1)} %add_convert_fusion.1), channel_id=1, source_target_pairs={{0,4},{1,3},{2,0},{3,7},{4,8},{5,1},{6,2},{7,11},{8,12},{9,5},{10,... | collective-permute-start | bytes 393224 | tf_op jit(solution)/shard_map/ppermute | solution.py:43
  41.6 1.7 %collective-permute-done.20 = bf16[16,4096]{1,0:T(8,128)(2,1)S(1)} collective-permute-done((bf16[16,4096]{1,0:T(8,128)(2,1)S(1)}, bf16[16,4096]{1,0:T(8,128)(2,1)S(1)}, u32[]{:S(2)}, u32[]{:S(2)}) %collective-permute-start.20) | collective-permute-done | bytes 131104 | tf_op jit(solution)/shard_map/ppermute | solution.py:43
  43.4 1.6 %collective-permute-start.25 = (bf16[16,4096]{1,0:T(8,128)(2,1)S(1)}, bf16[16,4096]{1,0:T(8,128)(2,1)S(1)}, u32[]{:S(2)}, u32[]{:S(2)}) collective-permute-start(bf16[16,4096]{1,0:T(8,128)(2,1)S(1)} %add_convert_fusion.4), channel_id=1, source_target_pairs={{0,4},{1,3},{2,0},{3,7},{4,8},{5,1},{6,2},{7,11},{8,12},{9,5},{10,... | collective-permute-start | bytes 393224 | tf_op jit(solution)/shard_map/ppermute | solution.py:43
  45.1 3.3 %collective-permute-done.25 = bf16[16,4096]{1,0:T(8,128)(2,1)S(1)} collective-permute-done((bf16[16,4096]{1,0:T(8,128)(2,1)S(1)}, bf16[16,4096]{1,0:T(8,128)(2,1)S(1)}, u32[]{:S(2)}, u32[]{:S(2)}) %collective-permute-start.25) | collective-permute-done | bytes 131104 | tf_op jit(solution)/shard_map/ppermute | solution.py:43
  48.8 1.6 %collective-permute-start.28 = (bf16[16,4224]{1,0:T(8,128)(2,1)S(1)}, bf16[16,4224]{1,0:T(8,128)(2,1)S(1)}, u32[]{:S(2)}, u32[]{:S(2)}) collective-permute-start(bf16[16,4224]{1,0:T(8,128)(2,1)S(1)} %shard_map.108.refs_0_), channel_id=1, source_target_pairs={{0,4},{1,3},{2,0},{3,7},{4,8},{5,1},{6,2},{7,11},{8,12},{9,5},{10,... | collective-permute-start | bytes 405512 | tf_op jit(solution)/shard_map/ppermute | solution.py:43
  50.6 1.6 %collective-permute-start.31 = (bf16[16,4224]{1,0:T(8,128)(2,1)S(1)}, bf16[16,4224]{1,0:T(8,128)(2,1)S(1)}, u32[]{:S(2)}, u32[]{:S(2)}) collective-permute-start(bf16[16,4224]{1,0:T(8,128)(2,1)S(1)} %shard_map.109.refs_8_), channel_id=1, source_target_pairs={{0,4},{1,3},{2,0},{3,7},{4,8},{5,1},{6,2},{7,11},{8,12},{9,5},{10,... | collective-permute-start | bytes 405512 | tf_op jit(solution)/shard_map/ppermute | solution.py:43
  55.7 1.6 %collective-permute-start.35 = (bf16[16,4224]{1,0:T(8,128)(2,1)S(1)}, bf16[16,4224]{1,0:T(8,128)(2,1)S(1)}, u32[]{:S(2)}, u32[]{:S(2)}) collective-permute-start(bf16[16,4224]{1,0:T(8,128)(2,1)S(1)} %collective-permute-done.31.refs_9_), channel_id=1, source_target_pairs={{0,4},{1,3},{2,0},{3,7},{4,8},{5,1},{6,2},{7,11},{8,12},{9,5},{10,... | collective-permute-start | bytes 405512 | tf_op jit(solution)/shard_map/ppermute | solution.py:43
  60.7 1.6 %collective-permute-start.37 = (bf16[16,4224]{1,0:T(8,128)(2,1)S(1)}, bf16[16,4224]{1,0:T(8,128)(2,1)S(1)}, u32[]{:S(2)}, u32[]{:S(2)}) collective-permute-start(bf16[16,4224]{1,0:T(8,128)(2,1)S(1)} %collective-permute-done.35.refs_10_), channel_id=1, source_target_pairs={{0,4},{1,3},{2,0},{3,7},{4,8},{5,1},{6,2},{7,11},{8,12},{9,5},{10,... | collective-permute-start | bytes 405512 | tf_op jit(solution)/shard_map/ppermute | solution.py:43
  63.8 1.6 %collective-permute-start.40 = (bf16[16,4224]{1,0:T(8,128)(2,1)S(1)}, bf16[16,4224]{1,0:T(8,128)(2,1)S(1)}, u32[]{:S(2)}, u32[]{:S(2)}) collective-permute-start(bf16[16,4224]{1,0:T(8,128)(2,1)S(1)} %collective-permute-done.33.refs_3_), channel_id=1, source_target_pairs={{0,4},{1,3},{2,0},{3,7},{4,8},{5,1},{6,2},{7,11},{8,12},{9,5},{10,... | collective-permute-start | bytes 405512 | tf_op jit(solution)/shard_map/ppermute | solution.py:43
  66.2 2.6 %collective-permute-done.40.refs_7_ = bf16[16,4224]{1,0:T(8,128)(2,1)S(1)} collective-permute-done((bf16[16,4224]{1,0:T(8,128)(2,1)S(1)}, bf16[16,4224]{1,0:T(8,128)(2,1)S(1)}, u32[]{:S(2)}, u32[]{:S(2)}) %collective-permute-start.40) | collective-permute-done | bytes 135200 | tf_op jit(solution)/shard_map/ppermute | solution.py:43
  70.4 1.6 %collective-permute-start.43 = (f32[8,128]{1,0:T(8,128)S(1)}, f32[8,128]{1,0:T(8,128)S(1)}, u32[]{:S(2)}, u32[]{:S(2)}) collective-permute-start(f32[8,128]{1,0:T(8,128)S(1)} %shard_map.113.own_ref), channel_id=1, source_target_pairs={{0,16},{16,0},{1,17},{17,1},{2,18},{18,2},{3,19},{19,3},{4,20},{20... | collective-permute-start | bytes 12296 | tf_op jit(solution)/shard_map/ppermute | solution.py:534
  71.9 5.7 %shard_map.112 = (bf16[4096,512]{1,0:T(8,128)(2,1)}, f32[1,512]{1,0:T(1,128)}, bf16[512,4096]{1,0:T(8,128)(2,1)}) custom-call(bf16[16,4224]{1,0:T(8,128)(2,1)S(1)} %shard_map.108.refs_0_, bf16[16,4224]{1,0:T(8,128)(2,1)S(1)} %collective-permute-done.28.refs_1_, bf16[16,4224]{1,0:T(8,128)(2,1)S(1)} %collective-permute-done.29.refs_2_, ...), custom_call_target="tpu_custom_call" | custom-call | tf_op jit(solution)/shard_map/pallas_call | solution.py:292
  (95 shorter events, 27.8 us)
Async XLA Ops:
  1.1 5.8 %collective-permute-start = (bf16[16,4096]{1,0:T(8,128)(2,1)}, bf16[16,4096]{1,0:T(8,128)(2,1)S(1)}, u32[]{:S(2)}, u32[]{:S(2)}) collective-permute-start(bf16[16,4096]{1,0:T(8,128)(2,1)} %bitcast.10), channel_id=1, source_target_pairs={{0,4},{1,3},{2,0},{3,7},{4,8},{5,1},{6,2},{7,11},{8,12},{9,5},{10,... | collective-permute-start | bytes 393224 | tf_op jit(solution)/shard_map/ppermute | solution.py:43
  3.8 5.2 %collective-permute-start.3 = (bf16[16,4096]{1,0:T(8,128)(2,1)S(1)}, bf16[16,4096]{1,0:T(8,128)(2,1)S(1)}, u32[]{:S(2)}, u32[]{:S(2)}) collective-permute-start(bf16[16,4096]{1,0:T(8,128)(2,1)S(1)} %collective-permute-done.1.signal_ref.refs_0_), channel_id=1, source_target_pairs={{0,4},{1,3},{2,0},{3,7},{4,8},{5,1},{6,2},{7,11},{8,12},{9,5},{10,... | collective-permute-start | bytes 393224 | tf_op jit(solution)/shard_map/ppermute | solution.py:43
  6.9 5.2 %collective-permute-start.2 = (bf16[16,4096]{1,0:T(8,128)(2,1)S(1)}, bf16[16,4096]{1,0:T(8,128)(2,1)S(1)}, u32[]{:S(2)}, u32[]{:S(2)}) collective-permute-start(bf16[16,4096]{1,0:T(8,128)(2,1)S(1)} %collective-permute-done.signal_ref.refs_1_), channel_id=1, source_target_pairs={{0,4},{1,3},{2,0},{3,7},{4,8},{5,1},{6,2},{7,11},{8,12},{9,5},{10,... | collective-permute-start | bytes 393224 | tf_op jit(solution)/shard_map/ppermute | solution.py:43
  12.1 5.0 %collective-permute-start.5 = (bf16[16,4096]{1,0:T(8,128)(2,1)S(1)}, bf16[16,4096]{1,0:T(8,128)(2,1)S(1)}, u32[]{:S(2)}, u32[]{:S(2)}) collective-permute-start(bf16[16,4096]{1,0:T(8,128)(2,1)S(1)} %collective-permute-done.2.signal_ref.refs_2_), channel_id=1, source_target_pairs={{0,4},{1,3},{2,0},{3,7},{4,8},{5,1},{6,2},{7,11},{8,12},{9,5},{10,... | collective-permute-start | bytes 393224 | tf_op jit(solution)/shard_map/ppermute | solution.py:43
  13.9 5.0 %collective-permute-start.9 = (bf16[16,4096]{1,0:T(8,128)(2,1)S(1)}, bf16[16,4096]{1,0:T(8,128)(2,1)S(1)}, u32[]{:S(2)}, u32[]{:S(2)}) collective-permute-start(bf16[16,4096]{1,0:T(8,128)(2,1)S(1)} %collective-permute-done.7.refs_2_), channel_id=1, source_target_pairs={{0,4},{1,3},{2,0},{3,7},{4,8},{5,1},{6,2},{7,11},{8,12},{9,5},{10,... | collective-permute-start | bytes 393224 | tf_op jit(solution)/shard_map/ppermute | solution.py:43
  17.2 7.0 %collective-permute-start.12 = (bf16[16,4096]{1,0:T(8,128)(2,1)S(1)}, bf16[16,4096]{1,0:T(8,128)(2,1)S(1)}, u32[]{:S(2)}, u32[]{:S(2)}) collective-permute-start(bf16[16,4096]{1,0:T(8,128)(2,1)S(1)} %collective-permute-done.5.refs_3_), channel_id=1, source_target_pairs={{0,4},{1,3},{2,0},{3,7},{4,8},{5,1},{6,2},{7,11},{8,12},{9,5},{10,... | collective-permute-start | bytes 393224 | tf_op jit(solution)/shard_map/ppermute | solution.py:43
  19.0 5.2 %collective-permute-start.13 = (bf16[16,4096]{1,0:T(8,128)(2,1)S(1)}, bf16[16,4096]{1,0:T(8,128)(2,1)S(1)}, u32[]{:S(2)}, u32[]{:S(2)}) collective-permute-start(bf16[16,4096]{1,0:T(8,128)(2,1)S(1)} %collective-permute-done.5.refs_3_), channel_id=1, source_target_pairs={{0,1},{1,0},{2,3},{3,2},{4,5},{5,4},{6,7},{7,6},{8,9},{9,8},{10,11... | collective-permute-start | bytes 393224 | tf_op jit(solution)/shard_map/ppermute | solution.py:46
  19.0 5.2 %collective-permute-start.10 = (bf16[16,4096]{1,0:T(8,128)(2,1)S(1)}, bf16[16,4096]{1,0:T(8,128)(2,1)S(1)}, u32[]{:S(2)}, u32[]{:S(2)}) collective-permute-start(bf16[16,4096]{1,0:T(8,128)(2,1)S(1)} %collective-permute-done.9.signal_ref.refs_3_), channel_id=1, source_target_pairs={{0,1},{1,0},{2,3},{3,2},{4,5},{5,4},{6,7},{7,6},{8,9},{9,8},{10,11... | collective-permute-start | bytes 393224 | tf_op jit(solution)/shard_map/ppermute | solution.py:46
  28.0 15.3 %collective-permute-start.24 = (f32[1,512]{1,0:T(1,128)S(1)}, f32[1,512]{1,0:T(1,128)S(1)}, u32[]{:S(2)}, u32[]{:S(2)}) collective-permute-start(f32[1,512]{1,0:T(1,128)S(1)} %get-tuple-element.160.refs_3_), channel_id=1, source_target_pairs={{0,1},{1,0},{2,3},{3,2},{4,5},{5,4},{6,7},{7,6},{8,9},{9,8},{10,11... | collective-permute-start | bytes 6152 | tf_op jit(solution)/shard_map/ppermute | solution.py:46
  28.1 5.0 %collective-permute-start.16 = (bf16[16,4096]{1,0:T(8,128)(2,1)S(1)}, bf16[16,4096]{1,0:T(8,128)(2,1)S(1)}, u32[]{:S(2)}, u32[]{:S(2)}) collective-permute-start(bf16[16,4096]{1,0:T(8,128)(2,1)S(1)} %add_convert_fusion.8), channel_id=1, source_target_pairs={{0,4},{1,3},{2,0},{3,7},{4,8},{5,1},{6,2},{7,11},{8,12},{9,5},{10,... | collective-permute-start | bytes 393224 | tf_op jit(solution)/shard_map/ppermute | solution.py:43
  29.8 5.0 %collective-permute-start.19 = (bf16[16,4096]{1,0:T(8,128)(2,1)S(1)}, bf16[16,4096]{1,0:T(8,128)(2,1)S(1)}, u32[]{:S(2)}, u32[]{:S(2)}) collective-permute-start(bf16[16,4096]{1,0:T(8,128)(2,1)S(1)} %add_convert_fusion.5), channel_id=1, source_target_pairs={{0,4},{1,3},{2,0},{3,7},{4,8},{5,1},{6,2},{7,11},{8,12},{9,5},{10,... | collective-permute-start | bytes 393224 | tf_op jit(solution)/shard_map/ppermute | solution.py:43
  33.2 5.0 %collective-permute-start.17 = (bf16[16,4096]{1,0:T(8,128)(2,1)S(1)}, bf16[16,4096]{1,0:T(8,128)(2,1)S(1)}, u32[]{:S(2)}, u32[]{:S(2)}) collective-permute-start(bf16[16,4096]{1,0:T(8,128)(2,1)S(1)} %add_convert_fusion.7), channel_id=1, source_target_pairs={{0,4},{1,3},{2,0},{3,7},{4,8},{5,1},{6,2},{7,11},{8,12},{9,5},{10,... | collective-permute-start | bytes 393224 | tf_op jit(solution)/shard_map/ppermute | solution.py:43
  34.9 5.0 %collective-permute-start.21 = (bf16[16,4096]{1,0:T(8,128)(2,1)S(1)}, bf16[16,4096]{1,0:T(8,128)(2,1)S(1)}, u32[]{:S(2)}, u32[]{:S(2)}) collective-permute-start(bf16[16,4096]{1,0:T(8,128)(2,1)S(1)} %add_convert_fusion.3), channel_id=1, source_target_pairs={{0,4},{1,3},{2,0},{3,7},{4,8},{5,1},{6,2},{7,11},{8,12},{9,5},{10,... | collective-permute-start | bytes 393224 | tf_op jit(solution)/shard_map/ppermute | solution.py:43
  36.5 5.1 %collective-permute-start.22 = (bf16[16,4096]{1,0:T(8,128)(2,1)S(1)}, bf16[16,4096]{1,0:T(8,128)(2,1)S(1)}, u32[]{:S(2)}, u32[]{:S(2)}) collective-permute-start(bf16[16,4096]{1,0:T(8,128)(2,1)S(1)} %bitcast.20), channel_id=1, source_target_pairs={{0,16},{16,0},{1,17},{17,1},{2,18},{18,2},{3,19},{19,3},{4,20},{20... | collective-permute-start | bytes 393224 | tf_op jit(solution)/shard_map/ppermute | solution.py:511
  38.3 5.0 %collective-permute-start.20 = (bf16[16,4096]{1,0:T(8,128)(2,1)S(1)}, bf16[16,4096]{1,0:T(8,128)(2,1)S(1)}, u32[]{:S(2)}, u32[]{:S(2)}) collective-permute-start(bf16[16,4096]{1,0:T(8,128)(2,1)S(1)} %add_convert_fusion.6), channel_id=1, source_target_pairs={{0,4},{1,3},{2,0},{3,7},{4,8},{5,1},{6,2},{7,11},{8,12},{9,5},{10,... | collective-permute-start | bytes 393224 | tf_op jit(solution)/shard_map/ppermute | solution.py:43
  40.0 5.0 %collective-permute-start.26 = (bf16[16,4096]{1,0:T(8,128)(2,1)S(1)}, bf16[16,4096]{1,0:T(8,128)(2,1)S(1)}, u32[]{:S(2)}, u32[]{:S(2)}) collective-permute-start(bf16[16,4096]{1,0:T(8,128)(2,1)S(1)} %add_convert_fusion.1), channel_id=1, source_target_pairs={{0,4},{1,3},{2,0},{3,7},{4,8},{5,1},{6,2},{7,11},{8,12},{9,5},{10,... | collective-permute-start | bytes 393224 | tf_op jit(solution)/shard_map/ppermute | solution.py:43
  43.4 5.0 %collective-permute-start.25 = (bf16[16,4096]{1,0:T(8,128)(2,1)S(1)}, bf16[16,4096]{1,0:T(8,128)(2,1)S(1)}, u32[]{:S(2)}, u32[]{:S(2)}) collective-permute-start(bf16[16,4096]{1,0:T(8,128)(2,1)S(1)} %add_convert_fusion.4), channel_id=1, source_target_pairs={{0,4},{1,3},{2,0},{3,7},{4,8},{5,1},{6,2},{7,11},{8,12},{9,5},{10,... | collective-permute-start | bytes 393224 | tf_op jit(solution)/shard_map/ppermute | solution.py:43
  48.8 5.1 %collective-permute-start.28 = (bf16[16,4224]{1,0:T(8,128)(2,1)S(1)}, bf16[16,4224]{1,0:T(8,128)(2,1)S(1)}, u32[]{:S(2)}, u32[]{:S(2)}) collective-permute-start(bf16[16,4224]{1,0:T(8,128)(2,1)S(1)} %shard_map.108.refs_0_), channel_id=1, source_target_pairs={{0,4},{1,3},{2,0},{3,7},{4,8},{5,1},{6,2},{7,11},{8,12},{9,5},{10,... | collective-permute-start | bytes 405512 | tf_op jit(solution)/shard_map/ppermute | solution.py:43
  50.6 5.1 %collective-permute-start.31 = (bf16[16,4224]{1,0:T(8,128)(2,1)S(1)}, bf16[16,4224]{1,0:T(8,128)(2,1)S(1)}, u32[]{:S(2)}, u32[]{:S(2)}) collective-permute-start(bf16[16,4224]{1,0:T(8,128)(2,1)S(1)} %shard_map.109.refs_8_), channel_id=1, source_target_pairs={{0,4},{1,3},{2,0},{3,7},{4,8},{5,1},{6,2},{7,11},{8,12},{9,5},{10,... | collective-permute-start | bytes 405512 | tf_op jit(solution)/shard_map/ppermute | solution.py:43
  55.7 5.0 %collective-permute-start.35 = (bf16[16,4224]{1,0:T(8,128)(2,1)S(1)}, bf16[16,4224]{1,0:T(8,128)(2,1)S(1)}, u32[]{:S(2)}, u32[]{:S(2)}) collective-permute-start(bf16[16,4224]{1,0:T(8,128)(2,1)S(1)} %collective-permute-done.31.refs_9_), channel_id=1, source_target_pairs={{0,4},{1,3},{2,0},{3,7},{4,8},{5,1},{6,2},{7,11},{8,12},{9,5},{10,... | collective-permute-start | bytes 405512 | tf_op jit(solution)/shard_map/ppermute | solution.py:43
  58.8 5.0 %collective-permute-start.33 = (bf16[16,4224]{1,0:T(8,128)(2,1)S(1)}, bf16[16,4224]{1,0:T(8,128)(2,1)S(1)}, u32[]{:S(2)}, u32[]{:S(2)}) collective-permute-start(bf16[16,4224]{1,0:T(8,128)(2,1)S(1)} %collective-permute-done.29.refs_2_), channel_id=1, source_target_pairs={{0,4},{1,3},{2,0},{3,7},{4,8},{5,1},{6,2},{7,11},{8,12},{9,5},{10,... | collective-permute-start | bytes 405512 | tf_op jit(solution)/shard_map/ppermute | solution.py:43
  60.7 5.0 %collective-permute-start.37 = (bf16[16,4224]{1,0:T(8,128)(2,1)S(1)}, bf16[16,4224]{1,0:T(8,128)(2,1)S(1)}, u32[]{:S(2)}, u32[]{:S(2)}) collective-permute-start(bf16[16,4224]{1,0:T(8,128)(2,1)S(1)} %collective-permute-done.35.refs_10_), channel_id=1, source_target_pairs={{0,4},{1,3},{2,0},{3,7},{4,8},{5,1},{6,2},{7,11},{8,12},{9,5},{10,... | collective-permute-start | bytes 405512 | tf_op jit(solution)/shard_map/ppermute | solution.py:43
  63.8 5.0 %collective-permute-start.40 = (bf16[16,4224]{1,0:T(8,128)(2,1)S(1)}, bf16[16,4224]{1,0:T(8,128)(2,1)S(1)}, u32[]{:S(2)}, u32[]{:S(2)}) collective-permute-start(bf16[16,4224]{1,0:T(8,128)(2,1)S(1)} %collective-permute-done.33.refs_3_), channel_id=1, source_target_pairs={{0,4},{1,3},{2,0},{3,7},{4,8},{5,1},{6,2},{7,11},{8,12},{9,5},{10,... | collective-permute-start | bytes 405512 | tf_op jit(solution)/shard_map/ppermute | solution.py:43
  70.4 7.3 %collective-permute-start.43 = (f32[8,128]{1,0:T(8,128)S(1)}, f32[8,128]{1,0:T(8,128)S(1)}, u32[]{:S(2)}, u32[]{:S(2)}) collective-permute-start(f32[8,128]{1,0:T(8,128)S(1)} %shard_map.113.own_ref), channel_id=1, source_target_pairs={{0,16},{16,0},{1,17},{17,1},{2,18},{18,2},{3,19},{19,3},{4,20},{20... | collective-permute-start | bytes 12296 | tf_op jit(solution)/shard_map/ppermute | solution.py:534
  (24 other events, 92.0 us)

commit v8 on v7

--- a/solution.py
+++ b/solution.py
@@ -150,11 +150,11 @@
 
 def forward_kernel(count, step, *refs):
     pieces = refs[:count]
-    enc_refs, dec_refs = refs[count : count + 2], refs[count + 2 : count + 4]
-    bias_ref, keep_ref, act_ref, gate_ref, sum_ref = refs[count + 4 : count + 9]
-    outs = refs[count + 9 :]
+    enc_refs, dec_refs = refs[count : count + 1], refs[count + 1 : count + 3]
+    bias_ref, keep_ref, act_ref, gate_ref, sum_ref = refs[count + 3 : count + 8]
+    outs = refs[count + 8 :]
     width = dec_refs[0].shape[1]
-    cut = width // 2
+    cut = width
     preact = bias_ref[...]
     for i, enc_ref in enumerate(enc_refs):
         for at in range(0, cut, 512):
@@ -204,7 +204,7 @@
     outs = pl.pallas_call(
         functools.partial(forward_kernel, len(pieces), min(512, width)),
         out_shape=[pltpu.VMEM(shape, dtype) for shape, dtype in shapes],
-        in_specs=[VMEM_SPEC] * (len(pieces) + 6),
+        in_specs=[VMEM_SPEC] * (len(pieces) + 5),
         out_specs=[VMEM_SPEC] * len(shapes),
         compiler_params=pltpu.CompilerParams(vmem_limit_bytes=12 << 20),
         cost_estimate=SHORT,
@@ -491,14 +491,9 @@
         )
         return [held["decoder", 1], held["norm"], *held["keep"]]
 
-    pins = {
-        2: load_in("encoder", w_enc[0], 0, 0),
-        3: load_in("encoder", w_enc[0], 1, 1),
-        4: load_in("decoder", w_dec[0], 0, 2),
-        0: rest_in,
-    }
+    pins = {4: load_in("decoder", w_dec[0], 0, 2), 0: rest_in}
     gathered = gather(ring, own, twins, pins, True)
-    encoder = [held["encoder", i] for i in (0, 1)]
+    encoder = [w_enc[0]]
     decoder = [held["decoder", i] for i in (0, 1)]
 
     acts, gates, sums, shares = zip(

time: 79.1 us -> 79 us (level)
  Pallas kernels: 17.5 us -> 14.4 us
  waiting for transfers between devices: 16.1 us -> 19 us
    pallas_call x3 -> x1, Pallas kernels: 4.64 us -> 1.55 us  [loaded(): pl.pallas_call(functools.partial(load_kernel, part * rows), out_shape=plt...]
    ppermute x22, waiting for transfers between devices: 14.8 us -> 17.6 us  [along(): return lax.ppermute(block, 'feat', self.step)]
  transfers between devices with their start and end apart: 44 -> 44, of which waited for: 14 -> 16; matrix products, arithmetic and copies ran while one was open for 0% -> 1% of each run, Pallas kernels for 20% -> 16%
where the time goes in v8:
time: 79 us; the launch traced here: 78.8 us
  starting transfers between devices  42.9 us (54%)
  waiting for transfers between devices  19 us (24%)
  Pallas kernels  14.4 us (18%)
  between operations  2.08 us (3%)
    ppermute x22, starting transfers between devices, along(): return lax.ppermute(block, 'feat', self.step)  37.4 us
    ppermute x22, waiting for transfers between devices, along(): return lax.ppermute(block, 'feat', self.step)  17.6 us
    pallas_call x1, Pallas kernels, backward(): pl.pallas_call(functools.partial(backward_kernel, tuple((len(e) for e in...  5.64 us
    pallas_call x1, Pallas kernels, prepared(): pl.pallas_call(prepare_kernel, out_shape=[pltpu.VMEM(half.shape, half.dty...  3.08 us
    pallas_call x2, Pallas kernels, forward(): pl.pallas_call(functools.partial(forward_kernel, len(pieces), min(512, wi...  2.87 us
    ppermute x20, starting transfers between devices, across(): return lax.ppermute(block, 'feat', self.twin)  2.41 us
    ppermute x1, starting transfers between devices, body(): group_losses.append(lax.ppermute(group_losses[-1], 'layer', route))  1.58 us
  transfers between devices with their start and end apart: 44, of which 16 were waited for; matrix products, arithmetic and copies ran while one was open for 1% of the time, Pallas kernels for 16%

profile of v8, /device:TPU:0, one launch (start us, length us, event | category | flops | bytes accessed | tf_op | source)
XLA Modules:
  0.0 78.8 jit_solution(9177676537096103968)
XLA Ops:
  1.2 2.6 %collective-permute-start = (bf16[16,4096]{1,0:T(8,128)(2,1)}, bf16[16,4096]{1,0:T(8,128)(2,1)S(1)}, u32[]{:S(2)}, u32[]{:S(2)}) collective-permute-start(bf16[16,4096]{1,0:T(8,128)(2,1)} %bitcast.12), channel_id=1, source_target_pairs={{0,4},{1,3},{2,0},{3,7},{4,8},{5,1},{6,2},{7,11},{8,12},{9,5},{10,... | collective-permute-start | bytes 393224 | tf_op jit(solution)/shard_map/ppermute | solution.py:43
  3.8 1.6 %collective-permute-start.3 = (bf16[16,4096]{1,0:T(8,128)(2,1)S(1)}, bf16[16,4096]{1,0:T(8,128)(2,1)S(1)}, u32[]{:S(2)}, u32[]{:S(2)}) collective-permute-start(bf16[16,4096]{1,0:T(8,128)(2,1)S(1)} %collective-permute-done.2.refs_0_), channel_id=1, source_target_pairs={{0,4},{1,3},{2,0},{3,7},{4,8},{5,1},{6,2},{7,11},{8,12},{9,5},{10,... | collective-permute-start | bytes 393224 | tf_op jit(solution)/shard_map/ppermute | solution.py:43
  6.9 2.1 %collective-permute-start.1 = (bf16[16,4096]{1,0:T(8,128)(2,1)S(1)}, bf16[16,4096]{1,0:T(8,128)(2,1)S(1)}, u32[]{:S(2)}, u32[]{:S(2)}) collective-permute-start(bf16[16,4096]{1,0:T(8,128)(2,1)S(1)} %collective-permute-done.refs_1_), channel_id=1, source_target_pairs={{0,4},{1,3},{2,0},{3,7},{4,8},{5,1},{6,2},{7,11},{8,12},{9,5},{10,... | collective-permute-start | bytes 393224 | tf_op jit(solution)/shard_map/ppermute | solution.py:43
  9.0 1.6 %collective-permute-start.7 = (bf16[16,4096]{1,0:T(8,128)(2,1)S(1)}, bf16[16,4096]{1,0:T(8,128)(2,1)S(1)}, u32[]{:S(2)}, u32[]{:S(2)}) collective-permute-start(bf16[16,4096]{1,0:T(8,128)(2,1)S(1)} %collective-permute-done.3.refs_1_), channel_id=1, source_target_pairs={{0,4},{1,3},{2,0},{3,7},{4,8},{5,1},{6,2},{7,11},{8,12},{9,5},{10,... | collective-permute-start | bytes 393224 | tf_op jit(solution)/shard_map/ppermute | solution.py:43
  11.8 2.1 %collective-permute-start.5 = (bf16[16,4096]{1,0:T(8,128)(2,1)S(1)}, bf16[16,4096]{1,0:T(8,128)(2,1)S(1)}, u32[]{:S(2)}, u32[]{:S(2)}) collective-permute-start(bf16[16,4096]{1,0:T(8,128)(2,1)S(1)} %collective-permute-done.1.signal_ref.refs_2_), channel_id=1, source_target_pairs={{0,4},{1,3},{2,0},{3,7},{4,8},{5,1},{6,2},{7,11},{8,12},{9,5},{10,... | collective-permute-start | bytes 393224 | tf_op jit(solution)/shard_map/ppermute | solution.py:43
  14.0 1.6 %collective-permute-start.9 = (bf16[16,4096]{1,0:T(8,128)(2,1)S(1)}, bf16[16,4096]{1,0:T(8,128)(2,1)S(1)}, u32[]{:S(2)}, u32[]{:S(2)}) collective-permute-start(bf16[16,4096]{1,0:T(8,128)(2,1)S(1)} %collective-permute-done.7.refs_2_), channel_id=1, source_target_pairs={{0,4},{1,3},{2,0},{3,7},{4,8},{5,1},{6,2},{7,11},{8,12},{9,5},{10,... | collective-permute-start | bytes 393224 | tf_op jit(solution)/shard_map/ppermute | solution.py:43
  17.2 1.7 %collective-permute-start.12 = (bf16[16,4096]{1,0:T(8,128)(2,1)S(1)}, bf16[16,4096]{1,0:T(8,128)(2,1)S(1)}, u32[]{:S(2)}, u32[]{:S(2)}) collective-permute-start(bf16[16,4096]{1,0:T(8,128)(2,1)S(1)} %collective-permute-done.5.refs_3_), channel_id=1, source_target_pairs={{0,4},{1,3},{2,0},{3,7},{4,8},{5,1},{6,2},{7,11},{8,12},{9,5},{10,... | collective-permute-start | bytes 393224 | tf_op jit(solution)/shard_map/ppermute | solution.py:43
  21.1 3.1 %shard_map.103 = (bf16[256,4096]{1,0:T(8,128)(2,1)S(1)}, f32[1,512]{1,0:T(1,128)S(1)}, f32[128,512]{1,0:T(8,128)S(1)}, f32[128,512]{1,0:T(8,128)S(1)}) custom-call(s32[2,4]{1,0:T(2,128)S(1)} %bitcast.15, f32[16,1,256]{2,1,0:T(1,128)} %constant.4.clone.table_ref, bf16[256,4096]{1,0:T(8,128)(2,1)S(1)} %shard_map.102.half_ref.refs_9_.refs_22_, ...), custom_call_target="tpu_custom_call" | custom-call | tf_op jit(solution)/shard_map/pallas_call | solution.py:378
  28.1 1.6 %collective-permute-start.16 = (bf16[16,4096]{1,0:T(8,128)(2,1)S(1)}, bf16[16,4096]{1,0:T(8,128)(2,1)S(1)}, u32[]{:S(2)}, u32[]{:S(2)}) collective-permute-start(bf16[16,4096]{1,0:T(8,128)(2,1)S(1)} %add_convert_fusion.8), channel_id=1, source_target_pairs={{0,4},{1,3},{2,0},{3,7},{4,8},{5,1},{6,2},{7,11},{8,12},{9,5},{10,... | collective-permute-start | bytes 393224 | tf_op jit(solution)/shard_map/ppermute | solution.py:43
  29.8 1.6 %collective-permute-start.19 = (bf16[16,4096]{1,0:T(8,128)(2,1)S(1)}, bf16[16,4096]{1,0:T(8,128)(2,1)S(1)}, u32[]{:S(2)}, u32[]{:S(2)}) collective-permute-start(bf16[16,4096]{1,0:T(8,128)(2,1)S(1)} %add_convert_fusion.5), channel_id=1, source_target_pairs={{0,4},{1,3},{2,0},{3,7},{4,8},{5,1},{6,2},{7,11},{8,12},{9,5},{10,... | collective-permute-start | bytes 393224 | tf_op jit(solution)/shard_map/ppermute | solution.py:43
  31.4 1.7 %collective-permute-done.16 = bf16[16,4096]{1,0:T(8,128)(2,1)S(1)} collective-permute-done((bf16[16,4096]{1,0:T(8,128)(2,1)S(1)}, bf16[16,4096]{1,0:T(8,128)(2,1)S(1)}, u32[]{:S(2)}, u32[]{:S(2)}) %collective-permute-start.16) | collective-permute-done | bytes 131104 | tf_op jit(solution)/shard_map/ppermute | solution.py:43
  33.2 1.6 %collective-permute-start.17 = (bf16[16,4096]{1,0:T(8,128)(2,1)S(1)}, bf16[16,4096]{1,0:T(8,128)(2,1)S(1)}, u32[]{:S(2)}, u32[]{:S(2)}) collective-permute-start(bf16[16,4096]{1,0:T(8,128)(2,1)S(1)} %add_convert_fusion.7), channel_id=1, source_target_pairs={{0,4},{1,3},{2,0},{3,7},{4,8},{5,1},{6,2},{7,11},{8,12},{9,5},{10,... | collective-permute-start | bytes 393224 | tf_op jit(solution)/shard_map/ppermute | solution.py:43
  34.9 1.6 %collective-permute-start.21 = (bf16[16,4096]{1,0:T(8,128)(2,1)S(1)}, bf16[16,4096]{1,0:T(8,128)(2,1)S(1)}, u32[]{:S(2)}, u32[]{:S(2)}) collective-permute-start(bf16[16,4096]{1,0:T(8,128)(2,1)S(1)} %add_convert_fusion.3), channel_id=1, source_target_pairs={{0,4},{1,3},{2,0},{3,7},{4,8},{5,1},{6,2},{7,11},{8,12},{9,5},{10,... | collective-permute-start | bytes 393224 | tf_op jit(solution)/shard_map/ppermute | solution.py:43
  38.3 1.6 %collective-permute-start.20 = (bf16[16,4096]{1,0:T(8,128)(2,1)S(1)}, bf16[16,4096]{1,0:T(8,128)(2,1)S(1)}, u32[]{:S(2)}, u32[]{:S(2)}) collective-permute-start(bf16[16,4096]{1,0:T(8,128)(2,1)S(1)} %add_convert_fusion.6), channel_id=1, source_target_pairs={{0,4},{1,3},{2,0},{3,7},{4,8},{5,1},{6,2},{7,11},{8,12},{9,5},{10,... | collective-permute-start | bytes 393224 | tf_op jit(solution)/shard_map/ppermute | solution.py:43
  40.0 1.6 %collective-permute-start.26 = (bf16[16,4096]{1,0:T(8,128)(2,1)S(1)}, bf16[16,4096]{1,0:T(8,128)(2,1)S(1)}, u32[]{:S(2)}, u32[]{:S(2)}) collective-permute-start(bf16[16,4096]{1,0:T(8,128)(2,1)S(1)} %add_convert_fusion.1), channel_id=1, source_target_pairs={{0,4},{1,3},{2,0},{3,7},{4,8},{5,1},{6,2},{7,11},{8,12},{9,5},{10,... | collective-permute-start | bytes 393224 | tf_op jit(solution)/shard_map/ppermute | solution.py:43
  41.6 1.7 %collective-permute-done.20 = bf16[16,4096]{1,0:T(8,128)(2,1)S(1)} collective-permute-done((bf16[16,4096]{1,0:T(8,128)(2,1)S(1)}, bf16[16,4096]{1,0:T(8,128)(2,1)S(1)}, u32[]{:S(2)}, u32[]{:S(2)}) %collective-permute-start.20) | collective-permute-done | bytes 131104 | tf_op jit(solution)/shard_map/ppermute | solution.py:43
  43.4 1.6 %collective-permute-start.25 = (bf16[16,4096]{1,0:T(8,128)(2,1)S(1)}, bf16[16,4096]{1,0:T(8,128)(2,1)S(1)}, u32[]{:S(2)}, u32[]{:S(2)}) collective-permute-start(bf16[16,4096]{1,0:T(8,128)(2,1)S(1)} %add_convert_fusion.4), channel_id=1, source_target_pairs={{0,4},{1,3},{2,0},{3,7},{4,8},{5,1},{6,2},{7,11},{8,12},{9,5},{10,... | collective-permute-start | bytes 393224 | tf_op jit(solution)/shard_map/ppermute | solution.py:43
  45.1 3.3 %collective-permute-done.25 = bf16[16,4096]{1,0:T(8,128)(2,1)S(1)} collective-permute-done((bf16[16,4096]{1,0:T(8,128)(2,1)S(1)}, bf16[16,4096]{1,0:T(8,128)(2,1)S(1)}, u32[]{:S(2)}, u32[]{:S(2)}) %collective-permute-start.25) | collective-permute-done | bytes 131104 | tf_op jit(solution)/shard_map/ppermute | solution.py:43
  48.8 1.6 %collective-permute-start.28 = (bf16[16,4224]{1,0:T(8,128)(2,1)S(1)}, bf16[16,4224]{1,0:T(8,128)(2,1)S(1)}, u32[]{:S(2)}, u32[]{:S(2)}) collective-permute-start(bf16[16,4224]{1,0:T(8,128)(2,1)S(1)} %shard_map.106.refs_0_), channel_id=1, source_target_pairs={{0,4},{1,3},{2,0},{3,7},{4,8},{5,1},{6,2},{7,11},{8,12},{9,5},{10,... | collective-permute-start | bytes 405512 | tf_op jit(solution)/shard_map/ppermute | solution.py:43
  50.6 1.6 %collective-permute-start.31 = (bf16[16,4224]{1,0:T(8,128)(2,1)S(1)}, bf16[16,4224]{1,0:T(8,128)(2,1)S(1)}, u32[]{:S(2)}, u32[]{:S(2)}) collective-permute-start(bf16[16,4224]{1,0:T(8,128)(2,1)S(1)} %shard_map.107.refs_8_), channel_id=1, source_target_pairs={{0,4},{1,3},{2,0},{3,7},{4,8},{5,1},{6,2},{7,11},{8,12},{9,5},{10,... | collective-permute-start | bytes 405512 | tf_op jit(solution)/shard_map/ppermute | solution.py:43
  52.2 1.6 %collective-permute-done.28.refs_1_ = bf16[16,4224]{1,0:T(8,128)(2,1)S(1)} collective-permute-done((bf16[16,4224]{1,0:T(8,128)(2,1)S(1)}, bf16[16,4224]{1,0:T(8,128)(2,1)S(1)}, u32[]{:S(2)}, u32[]{:S(2)}) %collective-permute-start.28) | collective-permute-done | bytes 135200 | tf_op jit(solution)/shard_map/ppermute | solution.py:43
  66.2 2.6 %collective-permute-done.40.refs_7_ = bf16[16,4224]{1,0:T(8,128)(2,1)S(1)} collective-permute-done((bf16[16,4224]{1,0:T(8,128)(2,1)S(1)}, bf16[16,4224]{1,0:T(8,128)(2,1)S(1)}, u32[]{:S(2)}, u32[]{:S(2)}) %collective-permute-start.40) | collective-permute-done | bytes 135200 | tf_op jit(solution)/shard_map/ppermute | solution.py:43
  70.4 1.6 %collective-permute-start.43 = (f32[8,128]{1,0:T(8,128)S(1)}, f32[8,128]{1,0:T(8,128)S(1)}, u32[]{:S(2)}, u32[]{:S(2)}) collective-permute-start(f32[8,128]{1,0:T(8,128)S(1)} %shard_map.111.own_ref), channel_id=1, source_target_pairs={{0,16},{16,0},{1,17},{17,1},{2,18},{18,2},{3,19},{19,3},{4,20},{20... | collective-permute-start | bytes 12296 | tf_op jit(solution)/shard_map/ppermute | solution.py:529
  72.0 5.6 %shard_map.110 = (bf16[4096,512]{1,0:T(8,128)(2,1)}, f32[1,512]{1,0:T(1,128)}, bf16[512,4096]{1,0:T(8,128)(2,1)}) custom-call(bf16[16,4224]{1,0:T(8,128)(2,1)S(1)} %shard_map.106.refs_0_, bf16[16,4224]{1,0:T(8,128)(2,1)S(1)} %collective-permute-done.28.refs_1_, bf16[16,4224]{1,0:T(8,128)(2,1)S(1)} %collective-permute-done.29.refs_2_, ...), custom_call_target="tpu_custom_call" | custom-call | tf_op jit(solution)/shard_map/pallas_call | solution.py:292
  (95 shorter events, 27.5 us)
Async XLA Ops:
  1.2 5.7 %collective-permute-start = (bf16[16,4096]{1,0:T(8,128)(2,1)}, bf16[16,4096]{1,0:T(8,128)(2,1)S(1)}, u32[]{:S(2)}, u32[]{:S(2)}) collective-permute-start(bf16[16,4096]{1,0:T(8,128)(2,1)} %bitcast.12), channel_id=1, source_target_pairs={{0,4},{1,3},{2,0},{3,7},{4,8},{5,1},{6,2},{7,11},{8,12},{9,5},{10,... | collective-permute-start | bytes 393224 | tf_op jit(solution)/shard_map/ppermute | solution.py:43
  3.8 5.2 %collective-permute-start.3 = (bf16[16,4096]{1,0:T(8,128)(2,1)S(1)}, bf16[16,4096]{1,0:T(8,128)(2,1)S(1)}, u32[]{:S(2)}, u32[]{:S(2)}) collective-permute-start(bf16[16,4096]{1,0:T(8,128)(2,1)S(1)} %collective-permute-done.2.refs_0_), channel_id=1, source_target_pairs={{0,4},{1,3},{2,0},{3,7},{4,8},{5,1},{6,2},{7,11},{8,12},{9,5},{10,... | collective-permute-start | bytes 393224 | tf_op jit(solution)/shard_map/ppermute | solution.py:43
  11.8 5.3 %collective-permute-start.5 = (bf16[16,4096]{1,0:T(8,128)(2,1)S(1)}, bf16[16,4096]{1,0:T(8,128)(2,1)S(1)}, u32[]{:S(2)}, u32[]{:S(2)}) collective-permute-start(bf16[16,4096]{1,0:T(8,128)(2,1)S(1)} %collective-permute-done.1.signal_ref.refs_2_), channel_id=1, source_target_pairs={{0,4},{1,3},{2,0},{3,7},{4,8},{5,1},{6,2},{7,11},{8,12},{9,5},{10,... | collective-permute-start | bytes 393224 | tf_op jit(solution)/shard_map/ppermute | solution.py:43
  14.0 5.0 %collective-permute-start.9 = (bf16[16,4096]{1,0:T(8,128)(2,1)S(1)}, bf16[16,4096]{1,0:T(8,128)(2,1)S(1)}, u32[]{:S(2)}, u32[]{:S(2)}) collective-permute-start(bf16[16,4096]{1,0:T(8,128)(2,1)S(1)} %collective-permute-done.7.refs_2_), channel_id=1, source_target_pairs={{0,4},{1,3},{2,0},{3,7},{4,8},{5,1},{6,2},{7,11},{8,12},{9,5},{10,... | collective-permute-start | bytes 393224 | tf_op jit(solution)/shard_map/ppermute | solution.py:43
  17.2 7.0 %collective-permute-start.12 = (bf16[16,4096]{1,0:T(8,128)(2,1)S(1)}, bf16[16,4096]{1,0:T(8,128)(2,1)S(1)}, u32[]{:S(2)}, u32[]{:S(2)}) collective-permute-start(bf16[16,4096]{1,0:T(8,128)(2,1)S(1)} %collective-permute-done.5.refs_3_), channel_id=1, source_target_pairs={{0,4},{1,3},{2,0},{3,7},{4,8},{5,1},{6,2},{7,11},{8,12},{9,5},{10,... | collective-permute-start | bytes 393224 | tf_op jit(solution)/shard_map/ppermute | solution.py:43
  19.0 5.2 %collective-permute-start.13 = (bf16[16,4096]{1,0:T(8,128)(2,1)S(1)}, bf16[16,4096]{1,0:T(8,128)(2,1)S(1)}, u32[]{:S(2)}, u32[]{:S(2)}) collective-permute-start(bf16[16,4096]{1,0:T(8,128)(2,1)S(1)} %collective-permute-done.5.refs_3_), channel_id=1, source_target_pairs={{0,1},{1,0},{2,3},{3,2},{4,5},{5,4},{6,7},{7,6},{8,9},{9,8},{10,11... | collective-permute-start | bytes 393224 | tf_op jit(solution)/shard_map/ppermute | solution.py:46
  19.0 5.2 %collective-permute-start.10 = (bf16[16,4096]{1,0:T(8,128)(2,1)S(1)}, bf16[16,4096]{1,0:T(8,128)(2,1)S(1)}, u32[]{:S(2)}, u32[]{:S(2)}) collective-permute-start(bf16[16,4096]{1,0:T(8,128)(2,1)S(1)} %collective-permute-done.9.signal_ref.refs_3_), channel_id=1, source_target_pairs={{0,1},{1,0},{2,3},{3,2},{4,5},{5,4},{6,7},{7,6},{8,9},{9,8},{10,11... | collective-permute-start | bytes 393224 | tf_op jit(solution)/shard_map/ppermute | solution.py:46
  28.0 15.4 %collective-permute-start.24 = (f32[1,512]{1,0:T(1,128)S(1)}, f32[1,512]{1,0:T(1,128)S(1)}, u32[]{:S(2)}, u32[]{:S(2)}) collective-permute-start(f32[1,512]{1,0:T(1,128)S(1)} %get-tuple-element.158.refs_3_), channel_id=1, source_target_pairs={{0,1},{1,0},{2,3},{3,2},{4,5},{5,4},{6,7},{7,6},{8,9},{9,8},{10,11... | collective-permute-start | bytes 6152 | tf_op jit(solution)/shard_map/ppermute | solution.py:46
  28.1 5.0 %collective-permute-start.16 = (bf16[16,4096]{1,0:T(8,128)(2,1)S(1)}, bf16[16,4096]{1,0:T(8,128)(2,1)S(1)}, u32[]{:S(2)}, u32[]{:S(2)}) collective-permute-start(bf16[16,4096]{1,0:T(8,128)(2,1)S(1)} %add_convert_fusion.8), channel_id=1, source_target_pairs={{0,4},{1,3},{2,0},{3,7},{4,8},{5,1},{6,2},{7,11},{8,12},{9,5},{10,... | collective-permute-start | bytes 393224 | tf_op jit(solution)/shard_map/ppermute | solution.py:43
  29.8 5.1 %collective-permute-start.19 = (bf16[16,4096]{1,0:T(8,128)(2,1)S(1)}, bf16[16,4096]{1,0:T(8,128)(2,1)S(1)}, u32[]{:S(2)}, u32[]{:S(2)}) collective-permute-start(bf16[16,4096]{1,0:T(8,128)(2,1)S(1)} %add_convert_fusion.5), channel_id=1, source_target_pairs={{0,4},{1,3},{2,0},{3,7},{4,8},{5,1},{6,2},{7,11},{8,12},{9,5},{10,... | collective-permute-start | bytes 393224 | tf_op jit(solution)/shard_map/ppermute | solution.py:43
  33.2 5.0 %collective-permute-start.17 = (bf16[16,4096]{1,0:T(8,128)(2,1)S(1)}, bf16[16,4096]{1,0:T(8,128)(2,1)S(1)}, u32[]{:S(2)}, u32[]{:S(2)}) collective-permute-start(bf16[16,4096]{1,0:T(8,128)(2,1)S(1)} %add_convert_fusion.7), channel_id=1, source_target_pairs={{0,4},{1,3},{2,0},{3,7},{4,8},{5,1},{6,2},{7,11},{8,12},{9,5},{10,... | collective-permute-start | bytes 393224 | tf_op jit(solution)/shard_map/ppermute | solution.py:43
  34.9 5.0 %collective-permute-start.21 = (bf16[16,4096]{1,0:T(8,128)(2,1)S(1)}, bf16[16,4096]{1,0:T(8,128)(2,1)S(1)}, u32[]{:S(2)}, u32[]{:S(2)}) collective-permute-start(bf16[16,4096]{1,0:T(8,128)(2,1)S(1)} %add_convert_fusion.3), channel_id=1, source_target_pairs={{0,4},{1,3},{2,0},{3,7},{4,8},{5,1},{6,2},{7,11},{8,12},{9,5},{10,... | collective-permute-start | bytes 393224 | tf_op jit(solution)/shard_map/ppermute | solution.py:43
  36.5 5.1 %collective-permute-start.22 = (bf16[16,4096]{1,0:T(8,128)(2,1)S(1)}, bf16[16,4096]{1,0:T(8,128)(2,1)S(1)}, u32[]{:S(2)}, u32[]{:S(2)}) collective-permute-start(bf16[16,4096]{1,0:T(8,128)(2,1)S(1)} %bitcast.20), channel_id=1, source_target_pairs={{0,16},{16,0},{1,17},{17,1},{2,18},{18,2},{3,19},{19,3},{4,20},{20... | collective-permute-start | bytes 393224 | tf_op jit(solution)/shard_map/ppermute | solution.py:506
  38.3 5.0 %collective-permute-start.20 = (bf16[16,4096]{1,0:T(8,128)(2,1)S(1)}, bf16[16,4096]{1,0:T(8,128)(2,1)S(1)}, u32[]{:S(2)}, u32[]{:S(2)}) collective-permute-start(bf16[16,4096]{1,0:T(8,128)(2,1)S(1)} %add_convert_fusion.6), channel_id=1, source_target_pairs={{0,4},{1,3},{2,0},{3,7},{4,8},{5,1},{6,2},{7,11},{8,12},{9,5},{10,... | collective-permute-start | bytes 393224 | tf_op jit(solution)/shard_map/ppermute | solution.py:43
  40.0 5.0 %collective-permute-start.26 = (bf16[16,4096]{1,0:T(8,128)(2,1)S(1)}, bf16[16,4096]{1,0:T(8,128)(2,1)S(1)}, u32[]{:S(2)}, u32[]{:S(2)}) collective-permute-start(bf16[16,4096]{1,0:T(8,128)(2,1)S(1)} %add_convert_fusion.1), channel_id=1, source_target_pairs={{0,4},{1,3},{2,0},{3,7},{4,8},{5,1},{6,2},{7,11},{8,12},{9,5},{10,... | collective-permute-start | bytes 393224 | tf_op jit(solution)/shard_map/ppermute | solution.py:43
  43.4 5.0 %collective-permute-start.25 = (bf16[16,4096]{1,0:T(8,128)(2,1)S(1)}, bf16[16,4096]{1,0:T(8,128)(2,1)S(1)}, u32[]{:S(2)}, u32[]{:S(2)}) collective-permute-start(bf16[16,4096]{1,0:T(8,128)(2,1)S(1)} %add_convert_fusion.4), channel_id=1, source_target_pairs={{0,4},{1,3},{2,0},{3,7},{4,8},{5,1},{6,2},{7,11},{8,12},{9,5},{10,... | collective-permute-start | bytes 393224 | tf_op jit(solution)/shard_map/ppermute | solution.py:43
  48.8 5.1 %collective-permute-start.28 = (bf16[16,4224]{1,0:T(8,128)(2,1)S(1)}, bf16[16,4224]{1,0:T(8,128)(2,1)S(1)}, u32[]{:S(2)}, u32[]{:S(2)}) collective-permute-start(bf16[16,4224]{1,0:T(8,128)(2,1)S(1)} %shard_map.106.refs_0_), channel_id=1, source_target_pairs={{0,4},{1,3},{2,0},{3,7},{4,8},{5,1},{6,2},{7,11},{8,12},{9,5},{10,... | collective-permute-start | bytes 405512 | tf_op jit(solution)/shard_map/ppermute | solution.py:43
  50.6 5.1 %collective-permute-start.31 = (bf16[16,4224]{1,0:T(8,128)(2,1)S(1)}, bf16[16,4224]{1,0:T(8,128)(2,1)S(1)}, u32[]{:S(2)}, u32[]{:S(2)}) collective-permute-start(bf16[16,4224]{1,0:T(8,128)(2,1)S(1)} %shard_map.107.refs_8_), channel_id=1, source_target_pairs={{0,4},{1,3},{2,0},{3,7},{4,8},{5,1},{6,2},{7,11},{8,12},{9,5},{10,... | collective-permute-start | bytes 405512 | tf_op jit(solution)/shard_map/ppermute | solution.py:43
  53.8 5.0 %collective-permute-start.29 = (bf16[16,4224]{1,0:T(8,128)(2,1)S(1)}, bf16[16,4224]{1,0:T(8,128)(2,1)S(1)}, u32[]{:S(2)}, u32[]{:S(2)}) collective-permute-start(bf16[16,4224]{1,0:T(8,128)(2,1)S(1)} %collective-permute-done.28.refs_1_), channel_id=1, source_target_pairs={{0,4},{1,3},{2,0},{3,7},{4,8},{5,1},{6,2},{7,11},{8,12},{9,5},{10,... | collective-permute-start | bytes 405512 | tf_op jit(solution)/shard_map/ppermute | solution.py:43
  55.7 5.0 %collective-permute-start.35 = (bf16[16,4224]{1,0:T(8,128)(2,1)S(1)}, bf16[16,4224]{1,0:T(8,128)(2,1)S(1)}, u32[]{:S(2)}, u32[]{:S(2)}) collective-permute-start(bf16[16,4224]{1,0:T(8,128)(2,1)S(1)} %collective-permute-done.31.refs_9_), channel_id=1, source_target_pairs={{0,4},{1,3},{2,0},{3,7},{4,8},{5,1},{6,2},{7,11},{8,12},{9,5},{10,... | collective-permute-start | bytes 405512 | tf_op jit(solution)/shard_map/ppermute | solution.py:43
  58.8 5.0 %collective-permute-start.33 = (bf16[16,4224]{1,0:T(8,128)(2,1)S(1)}, bf16[16,4224]{1,0:T(8,128)(2,1)S(1)}, u32[]{:S(2)}, u32[]{:S(2)}) collective-permute-start(bf16[16,4224]{1,0:T(8,128)(2,1)S(1)} %collective-permute-done.29.refs_2_), channel_id=1, source_target_pairs={{0,4},{1,3},{2,0},{3,7},{4,8},{5,1},{6,2},{7,11},{8,12},{9,5},{10,... | collective-permute-start | bytes 405512 | tf_op jit(solution)/shard_map/ppermute | solution.py:43
  60.7 5.0 %collective-permute-start.37 = (bf16[16,4224]{1,0:T(8,128)(2,1)S(1)}, bf16[16,4224]{1,0:T(8,128)(2,1)S(1)}, u32[]{:S(2)}, u32[]{:S(2)}) collective-permute-start(bf16[16,4224]{1,0:T(8,128)(2,1)S(1)} %collective-permute-done.35.refs_10_), channel_id=1, source_target_pairs={{0,4},{1,3},{2,0},{3,7},{4,8},{5,1},{6,2},{7,11},{8,12},{9,5},{10,... | collective-permute-start | bytes 405512 | tf_op jit(solution)/shard_map/ppermute | solution.py:43
  63.9 5.0 %collective-permute-start.40 = (bf16[16,4224]{1,0:T(8,128)(2,1)S(1)}, bf16[16,4224]{1,0:T(8,128)(2,1)S(1)}, u32[]{:S(2)}, u32[]{:S(2)}) collective-permute-start(bf16[16,4224]{1,0:T(8,128)(2,1)S(1)} %collective-permute-done.33.refs_3_), channel_id=1, source_target_pairs={{0,4},{1,3},{2,0},{3,7},{4,8},{5,1},{6,2},{7,11},{8,12},{9,5},{10,... | collective-permute-start | bytes 405512 | tf_op jit(solution)/shard_map/ppermute | solution.py:43
  70.4 7.2 %collective-permute-start.43 = (f32[8,128]{1,0:T(8,128)S(1)}, f32[8,128]{1,0:T(8,128)S(1)}, u32[]{:S(2)}, u32[]{:S(2)}) collective-permute-start(f32[8,128]{1,0:T(8,128)S(1)} %shard_map.111.own_ref), channel_id=1, source_target_pairs={{0,16},{16,0},{1,17},{17,1},{2,18},{18,2},{3,19},{19,3},{4,20},{20... | collective-permute-start | bytes 12296 | tf_op jit(solution)/shard_map/ppermute | solution.py:529
  (25 other events, 110.5 us)
